TPU v7x, 128 devices: a whole 4x4x4 slice. The times are simulated.
128 devices in a mesh: gx: 4 (over z_lo, core), gy: 4 (over y), gz: 8 (over z_hi, x).
Axes of the slice: x: 4, y: 4, z: 4 (z_hi: 2, z_lo: 2; z = z_hi * 2 + z_lo), core: 2. Of those that a mesh axis runs over, the one named last changes fastest.
Arguments:
- displacement: float32 [3, 98304], P(None, ('gx', 'gy', 'gz')), may hold values from -2.5 to 2.5
- neighbour_mask: int32 [98304], P(('gx', 'gy', 'gz')), may hold values from 0 to 1, as said below
- reverse_slot: int32 [98304], P(('gx', 'gy', 'gz')), may hold values from 0 to 1199, as said below
- send_edges: int32 [53248], P(('gx', 'gy', 'gz')), may hold values from 0 to 767
- species: int32 [4096], P(('gx', 'gy', 'gz')), may hold values from 0 to 84
- prev_tokens: bfloat16 [98304, 256], P(('gx', 'gy', 'gz')), may hold values from -6 to 6
- atom_state: bfloat16 [4096, 256], P(('gx', 'gy', 'gz')), may hold values from -6 to 6
- species_table: bfloat16 [85, 256], replicated, may hold values from -6 to 6
- w_neigh: bfloat16 [256, 256], replicated, may hold values from -0.375 to 0.375
- w_vec: float32 [3, 256], replicated, may hold values from -3.5 to 3.5
- w_rbf: float32 [64, 256], replicated, may hold values from -3 to 3
- gains: float32 [5, 256], replicated, may hold values from 0.25 to 1.75
- w_qkv: bfloat16 [2, 256, 768], replicated, may hold values from -0.375 to 0.375
- w_out: bfloat16 [2, 256, 256], replicated, may hold values from -0.375 to 0.375
- w_up: bfloat16 [2, 256, 512], replicated, may hold values from -0.375 to 0.375
- w_down: bfloat16 [2, 512, 256], replicated, may hold values from -0.25 to 0.25
- w_energy: float32 [256], replicated, may hold values from -0.375 to 0.375
Outputs:
- edge_tokens: bfloat16 [98304, 256], P(('gx', 'gy', 'gz'))
- atom_energy: float32 [4096], P(('gx', 'gy', 'gz'))
- forces: float32 [3, 4096], P(None, ('gx', 'gy', 'gz'))
Inputs may be any that keep to these rules, and one draw needn't show every extreme that they name: `neighbour_mask`: on each atom the first n of its 24 slots are 1 and the rest 0, with 20 <= n <= 24. `reverse_slot`: on each device, every value v >= 768 with (v - 768) // 16 != 13 is taken by exactly one edge whose neighbour_mask is 1, and no value has (v - 768) // 16 == 13; every edge of a device's first 4 atoms has a value below 768. `send_edges`: local edge numbers of the sending device.
All inputs are finite; a program needn't handle non-finite values.
Results may differ from a plain program's by a relative error of at most 0.014.
Values may be sent and summed in bfloat16 or wider, within the bound.
No kernel may reach another device: no remote copies, remote signals or barrier semaphores. Data moves between devices by JAX's collectives and lax.ppermute only.
A program may use at most 128 MiB of HBM per device.

v0:
```python
import math

import jax
import jax.numpy as jnp
from jax import lax
from jax.experimental import pallas as pl
from jax.experimental.pallas import tpu as pltpu
from jax.sharding import PartitionSpec as P

HEADS = 8
NBR = 24
ATOMS_DEV = 32
EDGE_DEV = 768
D = 256
FF = 512
NB = 64
NSPEC = 85
SLOTS = 16
SIDE = 9 * SLOTS
NFEAT = 72
score_cap = 8.0
cutoff_radius = 5.0
norm_eps = 1e-06

BF = jnp.bfloat16
F32 = jnp.float32
VMEM = pltpu.VMEM


def dot_nn(a, b):
    return lax.dot_general(a, b, (((1,), (0,)), ((), ())), preferred_element_type=F32)


def dot_nt(a, b):
    return lax.dot_general(a, b, (((1,), (1,)), ((), ())), preferred_element_type=F32)


def dot_tn(a, b):
    return lax.dot_general(a, b, (((0,), (0,)), ((), ())), preferred_element_type=F32)


def iota(shape, axis):
    return lax.broadcasted_iota(jnp.int32, shape, axis)


def split2(x):
    hi = x.astype(BF)
    lo = (x - hi.astype(F32)).astype(BF)
    return hi, lo


def as_column(row):
    return jnp.broadcast_to(row, (8, row.shape[1])).T[:, 0:1]


def atom_rows(count, dtype=BF):
    edge = iota((count * NBR, count), 0)
    first = iota((count * NBR, count), 1) * NBR
    return jnp.where((edge >= first) & (edge < first + NBR), 1.0, 0.0).astype(dtype)


def one_hot_lanes(column, width):
    lanes = iota((column.shape[0], width), 1).astype(F32)
    return jnp.where(lanes == column, 1.0, 0.0).astype(BF)


def message_kernel(state, w_neigh, prev, send, message, low, mid, high):
    projected = dot_nn(state[...], w_neigh[...])
    expand = atom_rows(ATOMS_DEV)
    hi, lo = split2(projected)
    rest = (projected - hi.astype(F32) - lo.astype(F32)).astype(BF)
    wide = dot_nn(expand, hi) + dot_nn(expand, lo) + dot_nn(expand, rest)
    out = (prev[...].astype(F32) + wide).astype(BF)
    message[...] = out
    pick = one_hot_lanes(as_column(send[...].astype(F32)), EDGE_DEV)
    payload = dot_nn(pick, out).astype(BF)
    low[...] = payload[0:SIDE]
    mid[...] = payload[SIDE : 2 * SIDE]
    high[...] = payload[2 * SIDE : 3 * SIDE]


def remote_index(slot):
    far = slot - EDGE_DEV
    bucket = far >> 4
    pair = (bucket * 11) >> 5
    third = bucket - 3 * pair
    return jnp.where(far >= 0, third * SIDE + pair * SLOTS + (far & 15), -1).astype(F32)


def geometry_kernel(
    disp, mask, slot, species, message, table, w_vec, w_rbf, base, kwb, feat, rows, mt, wfeat
):
    d = disp[...]
    dist = jnp.sqrt(jnp.sum(d * d, axis=0, keepdims=True) + 0.5)
    angle = (math.pi / cutoff_radius) * dist
    cut = 0.5 * (jnp.cos(angle) + 1.0)
    live = mask[...].astype(F32)
    kw = live * cut
    centres = 0.5 + 4.0 * iota((NB, 1), 0).astype(F32) / (NB - 1)
    offset = dist - centres
    radial = jnp.exp(-jnp.square(offset * (NB / 8.0)))
    feat[0:NB, :] = radial
    feat[NB:NFEAT, :] = jnp.zeros((NFEAT - NB, EDGE_DEV), F32)
    feat[NB : NB + 3, :] = d
    wfeat[0:NB, :] = w_rbf[...]
    wfeat[NB:NFEAT, :] = jnp.zeros((NFEAT - NB, D), F32)
    wfeat[NB : NB + 3, :] = w_vec[...]
    rows[0:1, :] = dist
    rows[1:2, :] = cut
    rows[2:3, :] = live
    rows[3:4, :] = kw
    rows[4:5, :] = (-0.5 * math.pi / cutoff_radius) * jnp.sin(angle)
    rows[5:8, :] = jnp.zeros((3, EDGE_DEV), F32)
    scaled = feat[...] * cut
    hi = scaled.astype(BF).astype(F32)
    left = jnp.concatenate([hi, scaled - hi, hi], axis=0).T.astype(BF)
    w = wfeat[...]
    whi = w.astype(BF).astype(F32)
    right = jnp.concatenate([whi, whi, w - whi], axis=0).astype(BF)
    kind = jnp.where(iota((NSPEC, ATOMS_DEV), 0) == species[...], 1.0, 0.0).astype(BF)
    centre = dot_tn(kind, table[...]).astype(BF)
    expand = atom_rows(ATOMS_DEV)
    slot_row = slot[...]
    local = one_hot_lanes(as_column(slot_row.astype(F32)), EDGE_DEV)
    base[...] = dot_nn(left, right) + dot_nn(expand, centre) + dot_nn(local, message[...])
    kwb[...] = jnp.broadcast_to(as_column(kw), (EDGE_DEV, 128))
    far = one_hot_lanes(as_column(remote_index(slot_row)), 3 * SIDE)
    live_rows = expand.astype(F32) * as_column(live)
    mt[...] = dot_tn(live_rows.astype(BF), far)


def rms_factor(x):
    return lax.rsqrt(jnp.mean(x * x, axis=-1, keepdims=True) + norm_eps)


def rms_back(x, r, z):
    inner = jnp.mean(x * z, axis=-1, keepdims=True)
    return r * z - x * (r * r * r * inner)


ROWS = 192
GROUP = 4


def layer_kernel(
    base,
    arr_r,
    arr_m,
    arr_l,
    slot,
    kwb,
    feat,
    rows,
    wfeat,
    gains,
    w_qkv,
    w_out,
    w_up,
    w_down,
    w_energy,
    send,
    tokens,
    energy,
    grad,
    low,
    mid,
    high,
    xs,
    qkv,
    ups,
    probs,
    slope,
    att,
    dqkv,
    acc,
):
    edges = base.shape[0]
    atoms = edges // NBR
    blocks = [slice(i, i + ROWS) for i in range(0, edges, ROWS)]
    lane_head = iota((1, 128), 1) >> 5
    head_lanes = [lane_head == h for h in range(4)]
    row_head = iota((128, 128), 0)
    mask_low = (iota((128, 128), 1) >> 5) * NBR
    block_mask = jnp.where(
        (row_head >= mask_low) & (row_head < mask_low + NBR), 1.0, 0.0
    ).astype(BF)
    score_scale = 1.0 / (math.sqrt(D // HEADS) * score_cap)
    slope_scale = 1.0 / math.sqrt(D // HEADS)

    def spread(x):
        two = jnp.concatenate([x, x], axis=0).astype(BF)
        return jnp.concatenate([two, two, jnp.zeros((32, 128), BF)], axis=0) * block_mask

    def gather_heads(wide):
        out = jnp.where(head_lanes[0], wide[0:NBR], 0.0)
        for h in range(1, 4):
            out = jnp.where(head_lanes[h], wide[h * NBR : (h + 1) * NBR], out)
        return out

    far = one_hot_lanes(as_column(remote_index(slot[...])), 3 * SIDE)
    arrived = jnp.concatenate([arr_r[...], arr_m[...], arr_l[...]], axis=0)
    x = [base[b, :] + dot_nn(far[b], arrived) for b in blocks]

    for layer in range(2):
        for b, v in zip(blocks, x):
            xs[2 * layer, b, :] = v
        gain = gains[2 * layer : 2 * layer + 1, :]
        normed = [(v * rms_factor(v) * gain).astype(BF) for v in x]
        for b, v in zip(blocks, normed):
            qkv[layer, b, :] = dot_nn(v, w_qkv[layer])

        @pl.loop(0, atoms // GROUP)
        def _(step):
            for u in range(GROUP):
                span = pl.ds(pl.multiple_of(step * (GROUP * NBR) + u * NBR, 8), NBR)
                weight = kwb[span, :]
                for g in range(2):
                    c = 128 * g
                    q = spread(qkv[layer, span, c : c + 128])
                    k = qkv[layer, span, D + c : D + c + 128].astype(BF)
                    v = qkv[layer, span, 2 * D + c : 2 * D + c + 128].astype(BF)
                    t = jnp.tanh(dot_nt(k, q) * score_scale)
                    e = weight * jnp.exp(score_cap * t)
                    p = e * (1.0 / jnp.sum(e, axis=0, keepdims=True))
                    probs[layer, span, c : c + 128] = p
                    slope[layer, span, c : c + 128] = (1.0 - t * t) * slope_scale
                    att[span, c : c + 128] = gather_heads(dot_tn(p.astype(BF), v))

        x = [xs[2 * layer, b, :] + dot_nn(att[b, :].astype(BF), w_out[layer]) for b in blocks]
        for b, v in zip(blocks, x):
            xs[2 * layer + 1, b, :] = v
        gain = gains[2 * layer + 1 : 2 * layer + 2, :]
        normed = [(v * rms_factor(v) * gain).astype(BF) for v in x]
        up = [dot_nn(v, w_up[layer]) for v in normed]
        for b, v in zip(blocks, up):
            ups[layer, b, :] = v
        hidden = [(u / (1.0 + jnp.exp(-u))).astype(BF) for u in up]
        x = [v + dot_nn(h, w_down[layer]) for v, h in zip(x, hidden)]

    read = gains[4:5, :] * w_energy[...]
    ones8 = jnp.ones((8, 128), BF)
    readout = []
    dx = []
    for b, v in zip(blocks, x):
        tokens[b, :] = v.astype(BF)
        r = rms_factor(v)
        scaled = v * r
        terms = scaled * read
        part_hi, part_lo = split2(terms[:, 0:128] + terms[:, 128:256])
        readout.append(dot_nt(ones8, part_hi) + dot_nt(ones8, part_lo))
        total = jnp.sum(terms, axis=-1, keepdims=True) * (1.0 / D)
        kw_col = kwb[b, 0:1]
        dx.append((kw_col * r) * (read - scaled * total))
    readout = jnp.concatenate(readout, axis=1)[0:1]
    live = rows[2:3, :]
    kw = rows[3:4, :]
    parts = kw * readout
    part_hi = parts.astype(BF).astype(F32)
    stacked = jnp.concatenate(
        [jnp.broadcast_to(part_hi, (8, edges)), jnp.broadcast_to(parts - part_hi, (8, edges))], axis=0
    ).astype(BF)
    summed = dot_nn(stacked, atom_rows(atoms))
    energy[...] = summed[0:1] + summed[8:9]

    for layer in (1, 0):
        dhid = [dot_nt(v.astype(BF), w_down[layer]) for v in dx]
        dup = []
        for b, dh in zip(blocks, dhid):
            u = ups[layer, b, :]
            sig = 1.0 / (1.0 + jnp.exp(-u))
            dup.append((dh * (sig * (1.0 + u * (1.0 - sig)))).astype(BF))
        gain = gains[2 * layer + 1 : 2 * layer + 2, :]
        dnorm = [dot_nt(v, w_up[layer]) * gain for v in dup]
        new = []
        for b, v, dn in zip(blocks, dx, dnorm):
            xv = xs[2 * layer + 1, b, :]
            new.append(v + rms_back(xv, rms_factor(xv), dn))
        dx = new
        for b, v in zip(blocks, dx):
            att[b, :] = dot_nt(v.astype(BF), w_out[layer])

        @pl.loop(0, atoms // GROUP)
        def _(step):
            for u in range(GROUP):
                span = pl.ds(pl.multiple_of(step * (GROUP * NBR) + u * NBR, 8), NBR)
                total = None
                for g in range(2):
                    c = 128 * g
                    q = spread(qkv[layer, span, c : c + 128])
                    k = qkv[layer, span, D + c : D + c + 128].astype(BF)
                    v = qkv[layer, span, 2 * D + c : 2 * D + c + 128].astype(BF)
                    do = spread(att[span, c : c + 128])
                    p = probs[layer, span, c : c + 128]
                    dp = dot_nt(v, do)
                    inner = jnp.sum(p * dp, axis=0, keepdims=True)
                    dl = p * (dp - inner)
                    total = dl if total is None else total + dl
                    ds = (dl * slope[layer, span, c : c + 128]).astype(BF)
                    dqkv[span, c : c + 128] = gather_heads(dot_tn(ds, k))
                    dqkv[span, D + c : D + c + 128] = dot_nn(ds, q)
                    dqkv[span, 2 * D + c : 2 * D + c + 128] = dot_nn(p.astype(BF), do)
                if layer == 1:
                    acc[span, :] = total
                else:
                    acc[span, :] = acc[span, :] + total

        gain = gains[2 * layer : 2 * layer + 1, :]
        dnorm = [dot_nt(dqkv[b, :].astype(BF), w_qkv[layer]) * gain for b in blocks]
        new = []
        for b, v, dn in zip(blocks, dx, dnorm):
            xv = xs[2 * layer, b, :]
            new.append(v + rms_back(xv, rms_factor(xv), dn))
        dx = new

    w = wfeat[...]
    whi = w.astype(BF)
    wlo = (w - whi.astype(F32)).astype(BF)
    back = []
    acc_row = []
    for b, v in zip(blocks, dx):
        hi, lo = split2(v)
        back.append(dot_nt(whi, hi) + dot_nt(whi, lo) + dot_nt(wlo, hi))
        part_hi, part_lo = split2(acc[b, :])
        acc_row.append(dot_nt(ones8, part_hi) + dot_nt(ones8, part_lo))
    back = jnp.concatenate(back, axis=1)
    acc_row = jnp.concatenate(acc_row, axis=1)[0:1]
    dist = rows[0:1, :]
    cut = rows[1:2, :]
    f = feat[...]
    dcut = jnp.sum(f * back, axis=0, keepdims=True) + live * (readout + acc_row / cut)
    centres = 0.5 + 4.0 * iota((NB, 1), 0).astype(F32) / (NB - 1)
    dradial = back[0:NB] * f[0:NB] * (dist - centres)
    ddist = dcut * rows[4:5, :] - (2.0 * (NB / 8.0) ** 2) * cut * jnp.sum(
        dradial, axis=0, keepdims=True
    )
    g = cut * back[NB:NFEAT] + f[NB:NFEAT] * (ddist / dist)
    grad[...] = g
    ghi = g.astype(BF).astype(F32)
    both = jnp.concatenate([ghi, g - ghi], axis=0).astype(BF)
    pick = jnp.where(iota((edges, 3 * SIDE), 0) == send[...], 1.0, 0.0).astype(BF)
    out = dot_nn(both, pick)
    out = out[0:8] + out[8:16]
    low[...] = out[:, 0:SIDE]
    mid[...] = out[:, SIDE : 2 * SIDE]
    high[...] = out[:, 2 * SIDE : 3 * SIDE]


def local_force_kernel(grad, slot, rows, out):
    g = grad[...]
    ghi = g.astype(BF).astype(F32)
    both = jnp.concatenate([ghi, g - ghi], axis=0).astype(BF)
    local = one_hot_lanes(as_column(slot[...].astype(F32)), EDGE_DEV)
    partner = dot_nt(both, local)
    diff = (g - partner[0:8] - partner[8:16]) * rows[2:3, :]
    hi = diff.astype(BF).astype(F32)
    both = jnp.concatenate([hi, diff - hi], axis=0).astype(BF)
    summed = dot_nn(both, atom_rows(ATOMS_DEV))
    out[...] = summed[0:8] + summed[8:16]


def force_kernel(partial, mt, r, m, l, forces):
    pieces = []
    for part in (r, m, l):
        for a in range(3):
            for b in range(3):
                pieces.append(part[b, a])
    table = jnp.concatenate(pieces, axis=1)
    hi = table.astype(BF).astype(F32)
    both = jnp.concatenate([hi, table - hi], axis=0).astype(BF)
    far = dot_nt(both, mt[...].astype(BF))
    forces[...] = (partial[...] - far[0:8] - far[8:16])[0:3]


def vmem_call(kernel, outs, *args, scratch=(), limit=60 * 2**20):
    spec = pl.BlockSpec(memory_space=VMEM)
    return pl.pallas_call(
        kernel,
        out_shape=outs,
        in_specs=[spec] * len(args),
        out_specs=jax.tree.map(lambda _: spec, outs),
        scratch_shapes=list(scratch),
        compiler_params=pltpu.CompilerParams(vmem_limit_bytes=limit),
    )(*args)


def shape(dims, dtype=F32):
    return jax.ShapeDtypeStruct(dims, dtype)


def messages(atom_state, w_neigh, prev_tokens, send):
    side = shape((SIDE, D), BF)
    return vmem_call(
        message_kernel,
        [shape((EDGE_DEV, D), BF), side, side, side],
        atom_state,
        w_neigh,
        prev_tokens,
        send,
    )


def geometry(disp, mask, slot, species, message, table, w_vec, w_rbf):
    return vmem_call(
        geometry_kernel,
        [
            shape((EDGE_DEV, D)),
            shape((EDGE_DEV, 128)),
            shape((NFEAT, EDGE_DEV)),
            shape((8, EDGE_DEV)),
            shape((ATOMS_DEV, 3 * SIDE)),
            shape((NFEAT, D)),
        ],
        disp,
        mask,
        slot,
        species,
        message,
        table,
        w_vec,
        w_rbf,
    )


def layers(base, arr, slot, kwb, feat, rows, wfeat, gains, w_qkv, w_out, w_up, w_down, w_energy, send):
    side = shape((8, SIDE))
    n = EDGE_DEV
    return vmem_call(
        layer_kernel,
        [shape((n, D), BF), shape((1, ATOMS_DEV)), shape((8, n)), side, side, side],
        base,
        *arr,
        slot,
        kwb,
        feat,
        rows,
        wfeat,
        gains,
        w_qkv,
        w_out,
        w_up,
        w_down,
        w_energy,
        send,
        scratch=[
            VMEM((4, n, D), F32),
            VMEM((2, n, 3 * D), F32),
            VMEM((2, n, FF), F32),
            VMEM((2, n, D), F32),
            VMEM((2, n, D), F32),
            VMEM((n, D), F32),
            VMEM((n, 3 * D), F32),
            VMEM((n, 128), F32),
        ],
    )


def to_right(x, axis):
    count = lax.axis_size(axis)
    return lax.ppermute(x, axis, [(i, (i + 1) % count) for i in range(count)])


def to_left(x, axis):
    count = lax.axis_size(axis)
    return lax.ppermute(x, axis, [((i + 1) % count, i) for i in range(count)])


def on_device(
    displacement,
    neighbour_mask,
    reverse_slot,
    send_edges,
    species,
    prev_tokens,
    atom_state,
    species_table,
    w_neigh,
    w_vec,
    w_rbf,
    gains,
    w_qkv,
    w_out,
    w_up,
    w_down,
    w_energy,
):
    centre = jnp.full((SLOTS,), -1, jnp.int32)
    send = jnp.concatenate([send_edges[: 13 * SLOTS], centre, send_edges[13 * SLOTS :]])
    send = send.reshape(1, 3 * SIDE)
    slot = reverse_slot.reshape(1, EDGE_DEV)
    message, low, mid, high = messages(atom_state, w_neigh, prev_tokens, send)
    right, left = to_right(high, "gx"), to_left(low, "gx")
    base, kwb, feat, rows, mt, wfeat = geometry(
        displacement,
        neighbour_mask.reshape(1, EDGE_DEV),
        slot,
        species.reshape(1, ATOMS_DEV),
        message,
        species_table,
        w_vec,
        w_rbf,
    )
    cells = [v.reshape(3, 3, SLOTS, D) for v in (right, mid, left)]
    high, mid, low = (jnp.stack([v[i] for v in cells]) for i in (2, 1, 0))
    right, left = to_right(high, "gy"), to_left(low, "gy")
    cells = (right, mid, left)
    high, mid, low = (jnp.stack([v[:, i] for v in cells], axis=1) for i in (2, 1, 0))
    right, left = to_right(high, "gz"), to_left(low, "gz")
    arr = [v.reshape(SIDE, D) for v in (right, mid, left)]
    tokens, energy, grad, low, mid, high = layers(
        base,
        arr,
        slot,
        kwb,
        feat,
        rows,
        wfeat,
        gains,
        w_qkv,
        w_out,
        w_up,
        w_down,
        w_energy.reshape(1, D),
        send,
    )
    right, left = to_right(high, "gx"), to_left(low, "gx")
    partial = vmem_call(local_force_kernel, shape((8, ATOMS_DEV)), grad, slot, rows)
    cells = jnp.stack([right, mid, left])
    cut = 3 * SLOTS
    right, left = to_right(cells[:, :, 2 * cut :], "gy"), to_left(cells[:, :, :cut], "gy")
    cells = jnp.stack([right, cells[:, :, cut : 2 * cut], left])
    cut = SLOTS
    right, left = to_right(cells[..., 2 * cut :], "gz"), to_left(cells[..., :cut], "gz")
    mid = cells[..., cut : 2 * cut]
    forces = vmem_call(force_kernel, shape((3, ATOMS_DEV)), partial, mt, right, mid, left)
    return (tokens, energy.reshape(ATOMS_DEV), forces)


def solution(mesh):
    return jax.shard_map(
        on_device,
        mesh=mesh,
        in_specs=(
            P(None, ("gx", "gy", "gz")),
            P(("gx", "gy", "gz")),
            P(("gx", "gy", "gz")),
            P(("gx", "gy", "gz")),
            P(("gx", "gy", "gz")),
            P(("gx", "gy", "gz"), None),
            P(("gx", "gy", "gz"), None),
            P(),
            P(),
            P(),
            P(),
            P(),
            P(),
            P(),
            P(),
            P(),
            P(),
        ),
        out_specs=(P(("gx", "gy", "gz"), None), P(("gx", "gy", "gz")), P(None, ("gx", "gy", "gz"))),
        check_vma=False,
    )
```

profile of v0, /device:TPU:0, one launch (start us, length us, event | category | flops | bytes accessed | tf_op | source)
XLA Modules:
  0.0 119.2 jit_solution(5769360385089845906)
XLA Ops:
  0.6 0.8 fusion.8
  1.5 0.7 pad_add_fusion
  2.1 2.9 %shard_map.184 = (bf16[768,256]{1,0:T(8,128)(2,1)}, bf16[144,256]{1,0:T(8,128)(2,1)}, bf16[144,256]{1,0:T(8,128)(2,1)}, bf16[144,256]{1,0:T(8,128)(2,1)}) custom-call(bf16[32,256]{1,0:T(8,128)(2,1)} %state.1, bf16[256,256]{1,0:T(8,128)(2,1)} %w_neigh.1, bf16[768,256]{1,0:T(8,128)(2,1)} %prev.1, s32[1,432]{1,0:T(1,128)} %bitcast.35), custom_call_target="tpu_custom_call" | custom-call | tf_op jit(solution)/shard_map/pallas_call | solution.py:376
  5.0 0.0 collective-permute-start
  5.0 1.7 %collective-permute-start.1 = (bf16[144,256]{1,0:T(8,128)(2,1)}, bf16[144,256]{1,0:T(8,128)(2,1)S(1)}, u32[]{:S(2)}, u32[]{:S(2)}) collective-permute-start(bf16[144,256]{1,0:T(8,128)(2,1)} %get-tuple-element.23), channel_id=1, source_target_pairs={{32,0},{64,32},{96,64},{0,96},{33,1},{65,33},{97,65},{1,97},{34,2}... | collective-permute-start | bytes 221192 | tf_op jit(solution)/shard_map/ppermute | solution.py:464
  6.7 0.0 copy-start.5
  6.7 0.8 fusion.4
  7.5 0.0 copy-done.5
  7.5 0.0 copy-start.6
  7.5 0.6 reshape.46.slot
  8.1 0.1 copy-done.6
  8.2 0.6 reshape.45.mask
  8.8 3.4 %shard_map.185 = (f32[768,256]{1,0:T(8,128)}, f32[768,128]{1,0:T(8,128)}, f32[72,768]{1,0:T(8,128)}, f32[8,768]{1,0:T(8,128)}, f32[32,432]{1,0:T(8,128)}, /*index=5*/f32[72,256]{1,0:T(8,128)}) custom-call(f32[3,768]{1,0:T(4,128)} %disp.1, s32[1,768]{1,0:T(1,128)} %reshape.45.mask, s32[1,768]{1,0:T(1,128)} %reshape.46.slot, s32[1,32]{1,0:T(1,128)} %bitcast.43, ...), custom_call_target="tpu_custom_call" | custom-call | tf_op jit(solution)/shard_map/pallas_call | solution.py:376
  12.2 0.0 collective-permute-done
  12.2 0.0 collective-permute-done.1
  12.3 3.2 %collective-permute-start.3 = (bf16[3,3,16,256]{3,2,1,0:T(8,128)(2,1)S(1)}, bf16[3,3,16,256]{3,2,1,0:T(8,128)(2,1)S(1)}, u32[]{:S(2)}, u32[]{:S(2)}) collective-permute-start(bf16[3,3,16,256]{3,2,1,0:T(8,128)(2,1)S(1)} %pad_maximum_fusion.2), channel_id=1, source_target_pairs={{8,0},{16,8},{24,16},{0,24},{9,1},{17,9},{25,17},{1,25},{10,2},{18... | collective-permute-start | bytes 221192 | tf_op jit(solution)/shard_map/ppermute | solution.py:464
  15.5 0.1 collective-permute-start.2
  15.6 1.9 %collective-permute-done.3 = bf16[3,3,16,256]{3,2,1,0:T(8,128)(2,1)S(1)} collective-permute-done((bf16[3,3,16,256]{3,2,1,0:T(8,128)(2,1)S(1)}, bf16[3,3,16,256]{3,2,1,0:T(8,128)(2,1)S(1)}, u32[]{:S(2)}, u32[]{:S(2)}) %collective-permute-start.3) | collective-permute-done | bytes 73760 | tf_op jit(solution)/shard_map/ppermute | solution.py:464
  17.5 3.7 %collective-permute-done.2 = bf16[3,3,16,256]{3,2,1,0:T(8,128)(2,1)S(1)} collective-permute-done((bf16[3,3,16,256]{3,2,1,0:T(8,128)(2,1)S(1)}, bf16[3,3,16,256]{3,2,1,0:T(8,128)(2,1)S(1)}, u32[]{:S(2)}, u32[]{:S(2)}) %collective-permute-start.2) | collective-permute-done | bytes 73760 | tf_op jit(solution)/shard_map/ppermute | solution.py:459
  21.1 1.6 %collective-permute-start.4 = (bf16[3,3,16,256]{3,2,1,0:T(8,128)(2,1)S(1)}, bf16[3,3,16,256]{3,2,1,0:T(8,128)(2,1)S(1)}, u32[]{:S(2)}, u32[]{:S(2)}) collective-permute-start(bf16[3,3,16,256]{3,2,1,0:T(8,128)(2,1)S(1)} %pad_maximum_fusion.3), channel_id=1, source_target_pairs={{0,1},{1,2},{2,3},{3,4},{4,5},{5,6},{6,7},{7,0},{8,9},{9,10},{10,1... | collective-permute-start | bytes 221192 | tf_op jit(solution)/shard_map/ppermute | solution.py:459
  22.7 4.9 %collective-permute-start.5 = (bf16[3,3,16,256]{3,2,1,0:T(8,128)(2,1)S(1)}, bf16[3,3,16,256]{3,2,1,0:T(8,128)(2,1)S(1)}, u32[]{:S(2)}, u32[]{:S(2)}) collective-permute-start(bf16[3,3,16,256]{3,2,1,0:T(8,128)(2,1)S(1)} %pad_maximum_fusion.5), channel_id=1, source_target_pairs={{1,0},{2,1},{3,2},{4,3},{5,4},{6,5},{7,6},{0,7},{9,8},{10,9},{11,1... | collective-permute-start | bytes 221192 | tf_op jit(solution)/shard_map/ppermute | solution.py:464
  27.6 0.6 pad_maximum_fusion.4
  28.2 1.4 %collective-permute-done.4 = bf16[3,3,16,256]{3,2,1,0:T(8,128)(2,1)S(1)} collective-permute-done((bf16[3,3,16,256]{3,2,1,0:T(8,128)(2,1)S(1)}, bf16[3,3,16,256]{3,2,1,0:T(8,128)(2,1)S(1)}, u32[]{:S(2)}, u32[]{:S(2)}) %collective-permute-start.4) | collective-permute-done | bytes 73760 | tf_op jit(solution)/shard_map/ppermute | solution.py:459
  29.6 0.0 copy-start
  29.6 0.0 collective-permute-done.5
  29.6 0.0 copy-start.1
  29.6 0.6 copy-done
  30.2 0.0 copy-done.1
  30.3 64.0 %shard_map.186 = (bf16[768,256]{1,0:T(8,128)(2,1)}, f32[1,32]{1,0:T(1,128)}, f32[8,768]{1,0:T(8,128)}, f32[8,144]{1,0:T(8,128)}, f32[8,144]{1,0:T(8,128)}, /*index=5*/f32[8,144]{1,0:T(8,128)}) custom-call(f32[768,256]{1,0:T(8,128)} %get-tuple-element.20.base, bf16[144,256]{1,0:T(8,128)(2,1)} %bitcast.33, bf16[144,256]{1,0:T(8,128)(2,1)} %bitcast.23, ...), custom_call_target="tpu_custom_call" | custom-call | tf_op jit(solution)/shard_map/pallas_call | solution.py:376
  94.3 0.0 copy-start.4
  94.3 0.1 collective-permute-start.6
  94.4 1.7 %collective-permute-start.7 = (f32[8,144]{1,0:T(8,128)}, f32[8,144]{1,0:T(8,128)S(1)}, u32[]{:S(2)}, u32[]{:S(2)}) collective-permute-start(f32[8,144]{1,0:T(8,128)} %get-tuple-element.34), channel_id=1, source_target_pairs={{32,0},{64,32},{96,64},{0,96},{33,1},{65,33},{97,65},{1,97},{34,2}... | collective-permute-start | bytes 13832 | tf_op jit(solution)/shard_map/ppermute | solution.py:464
  96.1 1.5 %collective-permute-done.6 = f32[8,144]{1,0:T(8,128)S(1)} collective-permute-done((f32[8,144]{1,0:T(8,128)}, f32[8,144]{1,0:T(8,128)S(1)}, u32[]{:S(2)}, u32[]{:S(2)}) %collective-permute-start.6) | collective-permute-done | bytes 4640 | tf_op jit(solution)/shard_map/ppermute | solution.py:459
  97.6 0.0 collective-permute-done.7
  97.7 0.0 copy-done.4
  97.7 0.1 fusion.7
  97.8 0.0 collective-permute-start.8
  97.8 3.2 %collective-permute-start.9 = (f32[3,8,48]{2,1,0:T(8,128)S(1)}, f32[3,8,48]{2,1,0:T(8,128)S(1)}, u32[]{:S(2)}, u32[]{:S(2)}) collective-permute-start(f32[3,8,48]{2,1,0:T(8,128)S(1)} %get-tuple-element.57), channel_id=1, source_target_pairs={{8,0},{16,8},{24,16},{0,24},{9,1},{17,9},{25,17},{1,25},{10,2},{18... | collective-permute-start | bytes 13832 | tf_op jit(solution)/shard_map/ppermute | solution.py:464
  101.0 1.7 %collective-permute-done.8 = f32[3,8,48]{2,1,0:T(8,128)S(1)} collective-permute-done((f32[3,8,48]{2,1,0:T(8,128)S(1)}, f32[3,8,48]{2,1,0:T(8,128)S(1)}, u32[]{:S(2)}, u32[]{:S(2)}) %collective-permute-start.8) | collective-permute-done | bytes 4640 | tf_op jit(solution)/shard_map/ppermute | solution.py:459
  102.7 0.0 collective-permute-done.9
  102.7 0.7 fusion.6
  103.4 5.9 %collective-permute-start.11 = (f32[3,3,8,16]{3,2,1,0:T(8,128)S(1)}, f32[3,3,8,16]{3,2,1,0:T(8,128)S(1)}, u32[]{:S(2)}, u32[]{:S(2)}) collective-permute-start(f32[3,3,8,16]{3,2,1,0:T(8,128)S(1)} %get-tuple-element.53), channel_id=1, source_target_pairs={{1,0},{2,1},{3,2},{4,3},{5,4},{6,5},{7,6},{0,7},{9,8},{10,9},{11,1... | collective-permute-start | bytes 13832 | tf_op jit(solution)/shard_map/ppermute | solution.py:464
  109.3 0.0 collective-permute-start.10
  109.3 2.2 %shard_map.187.partial = f32[8,32]{1,0:T(8,128)} custom-call(f32[8,768]{1,0:T(8,128)} %get-tuple-element.30.grad, s32[1,768]{1,0:T(1,128)} %reshape.46.slot, f32[8,768]{1,0:T(8,128)} %get-tuple-element.26.rows), custom_call_target="tpu_custom_call" | custom-call | tf_op jit(solution)/shard_map/pallas_call | solution.py:376
  111.5 0.0 collective-permute-done.11.l
  111.5 0.0 copy-start.2
  111.5 5.5 %collective-permute-done.10.r = f32[3,3,8,16]{3,2,1,0:T(8,128)S(1)} collective-permute-done((f32[3,3,8,16]{3,2,1,0:T(8,128)S(1)}, f32[3,3,8,16]{3,2,1,0:T(8,128)S(1)}, u32[]{:S(2)}, u32[]{:S(2)}) %collective-permute-start.10) | collective-permute-done | bytes 4640 | tf_op jit(solution)/shard_map/ppermute | solution.py:459
  117.0 0.0 copy-start.3
  117.0 0.0 copy-done.2
  117.0 0.6 copy-done.3
  117.6 1.6 %shard_map.188 = f32[3,32]{1,0:T(4,128)} custom-call(f32[8,32]{1,0:T(8,128)} %shard_map.187.partial, f32[32,432]{1,0:T(8,128)} %get-tuple-element.31.mt, f32[3,3,8,16]{3,2,1,0:T(8,128)} %copy-done.3, f32[3,3,8,16]{3,2,1,0:T(8,128)} %get-tuple-element.54.m, f32[3,3,8,16]{3,2,1,0:T(8,128)} %copy-done.2), custom_call_target="tpu_custom_call" | custom-call | tf_op jit(solution)/shard_map/pallas_call | solution.py:376
  (13 shorter events, 0.1 us)
Async XLA Ops:
  5.0 7.2 %collective-permute-start = (bf16[144,256]{1,0:T(8,128)(2,1)}, bf16[144,256]{1,0:T(8,128)(2,1)S(1)}, u32[]{:S(2)}, u32[]{:S(2)}) collective-permute-start(bf16[144,256]{1,0:T(8,128)(2,1)} %get-tuple-element.21), channel_id=1, source_target_pairs={{0,32},{32,64},{64,96},{96,0},{1,33},{33,65},{65,97},{97,1},{2,34}... | collective-permute-start | bytes 221192 | tf_op jit(solution)/shard_map/ppermute | solution.py:459
  5.0 7.2 %collective-permute-start.1 = (bf16[144,256]{1,0:T(8,128)(2,1)}, bf16[144,256]{1,0:T(8,128)(2,1)S(1)}, u32[]{:S(2)}, u32[]{:S(2)}) collective-permute-start(bf16[144,256]{1,0:T(8,128)(2,1)} %get-tuple-element.23), channel_id=1, source_target_pairs={{32,0},{64,32},{96,64},{0,96},{33,1},{65,33},{97,65},{1,97},{34,2}... | collective-permute-start | bytes 221192 | tf_op jit(solution)/shard_map/ppermute | solution.py:464
  6.7 0.8 copy-start.5
  7.5 0.7 copy-start.6
  12.3 5.1 %collective-permute-start.3 = (bf16[3,3,16,256]{3,2,1,0:T(8,128)(2,1)S(1)}, bf16[3,3,16,256]{3,2,1,0:T(8,128)(2,1)S(1)}, u32[]{:S(2)}, u32[]{:S(2)}) collective-permute-start(bf16[3,3,16,256]{3,2,1,0:T(8,128)(2,1)S(1)} %pad_maximum_fusion.2), channel_id=1, source_target_pairs={{8,0},{16,8},{24,16},{0,24},{9,1},{17,9},{25,17},{1,25},{10,2},{18... | collective-permute-start | bytes 221192 | tf_op jit(solution)/shard_map/ppermute | solution.py:464
  15.5 5.6 %collective-permute-start.2 = (bf16[3,3,16,256]{3,2,1,0:T(8,128)(2,1)S(1)}, bf16[3,3,16,256]{3,2,1,0:T(8,128)(2,1)S(1)}, u32[]{:S(2)}, u32[]{:S(2)}) collective-permute-start(bf16[3,3,16,256]{3,2,1,0:T(8,128)(2,1)S(1)} %pad_maximum_fusion), channel_id=1, source_target_pairs={{0,8},{8,16},{16,24},{24,0},{1,9},{9,17},{17,25},{25,1},{2,10},{10... | collective-permute-start | bytes 221192 | tf_op jit(solution)/shard_map/ppermute | solution.py:459
  21.1 8.5 %collective-permute-start.4 = (bf16[3,3,16,256]{3,2,1,0:T(8,128)(2,1)S(1)}, bf16[3,3,16,256]{3,2,1,0:T(8,128)(2,1)S(1)}, u32[]{:S(2)}, u32[]{:S(2)}) collective-permute-start(bf16[3,3,16,256]{3,2,1,0:T(8,128)(2,1)S(1)} %pad_maximum_fusion.3), channel_id=1, source_target_pairs={{0,1},{1,2},{2,3},{3,4},{4,5},{5,6},{6,7},{7,0},{8,9},{9,10},{10,1... | collective-permute-start | bytes 221192 | tf_op jit(solution)/shard_map/ppermute | solution.py:459
  22.7 6.9 %collective-permute-start.5 = (bf16[3,3,16,256]{3,2,1,0:T(8,128)(2,1)S(1)}, bf16[3,3,16,256]{3,2,1,0:T(8,128)(2,1)S(1)}, u32[]{:S(2)}, u32[]{:S(2)}) collective-permute-start(bf16[3,3,16,256]{3,2,1,0:T(8,128)(2,1)S(1)} %pad_maximum_fusion.5), channel_id=1, source_target_pairs={{1,0},{2,1},{3,2},{4,3},{5,4},{6,5},{7,6},{0,7},{9,8},{10,9},{11,1... | collective-permute-start | bytes 221192 | tf_op jit(solution)/shard_map/ppermute | solution.py:464
  29.6 0.6 copy-start
  29.6 0.7 copy-start.1
  94.3 3.4 %copy-start.4 = (f32[8,144]{1,0:T(8,128)S(1)}, f32[8,144]{1,0:T(8,128)}, u32[]{:S(2)}) copy-start(f32[8,144]{1,0:T(8,128)} %get-tuple-element.33) | copy-start | bytes 13828
  94.3 3.4 %collective-permute-start.6 = (f32[8,144]{1,0:T(8,128)}, f32[8,144]{1,0:T(8,128)S(1)}, u32[]{:S(2)}, u32[]{:S(2)}) collective-permute-start(f32[8,144]{1,0:T(8,128)} %get-tuple-element.32), channel_id=1, source_target_pairs={{0,32},{32,64},{64,96},{96,0},{1,33},{33,65},{65,97},{97,1},{2,34}... | collective-permute-start | bytes 13832 | tf_op jit(solution)/shard_map/ppermute | solution.py:459
  94.4 3.3 %collective-permute-start.7 = (f32[8,144]{1,0:T(8,128)}, f32[8,144]{1,0:T(8,128)S(1)}, u32[]{:S(2)}, u32[]{:S(2)}) collective-permute-start(f32[8,144]{1,0:T(8,128)} %get-tuple-element.34), channel_id=1, source_target_pairs={{32,0},{64,32},{96,64},{0,96},{33,1},{65,33},{97,65},{1,97},{34,2}... | collective-permute-start | bytes 13832 | tf_op jit(solution)/shard_map/ppermute | solution.py:464
  97.8 4.9 %collective-permute-start.8 = (f32[3,8,48]{2,1,0:T(8,128)S(1)}, f32[3,8,48]{2,1,0:T(8,128)S(1)}, u32[]{:S(2)}, u32[]{:S(2)}) collective-permute-start(f32[3,8,48]{2,1,0:T(8,128)S(1)} %get-tuple-element.56), channel_id=1, source_target_pairs={{0,8},{8,16},{16,24},{24,0},{1,9},{9,17},{17,25},{25,1},{2,10},{10... | collective-permute-start | bytes 13832 | tf_op jit(solution)/shard_map/ppermute | solution.py:459
  97.8 4.9 %collective-permute-start.9 = (f32[3,8,48]{2,1,0:T(8,128)S(1)}, f32[3,8,48]{2,1,0:T(8,128)S(1)}, u32[]{:S(2)}, u32[]{:S(2)}) collective-permute-start(f32[3,8,48]{2,1,0:T(8,128)S(1)} %get-tuple-element.57), channel_id=1, source_target_pairs={{8,0},{16,8},{24,16},{0,24},{9,1},{17,9},{25,17},{1,25},{10,2},{18... | collective-permute-start | bytes 13832 | tf_op jit(solution)/shard_map/ppermute | solution.py:464
  103.4 8.1 %collective-permute-start.11 = (f32[3,3,8,16]{3,2,1,0:T(8,128)S(1)}, f32[3,3,8,16]{3,2,1,0:T(8,128)S(1)}, u32[]{:S(2)}, u32[]{:S(2)}) collective-permute-start(f32[3,3,8,16]{3,2,1,0:T(8,128)S(1)} %get-tuple-element.53), channel_id=1, source_target_pairs={{1,0},{2,1},{3,2},{4,3},{5,4},{6,5},{7,6},{0,7},{9,8},{10,9},{11,1... | collective-permute-start | bytes 13832 | tf_op jit(solution)/shard_map/ppermute | solution.py:464
  109.3 7.7 %collective-permute-start.10 = (f32[3,3,8,16]{3,2,1,0:T(8,128)S(1)}, f32[3,3,8,16]{3,2,1,0:T(8,128)S(1)}, u32[]{:S(2)}, u32[]{:S(2)}) collective-permute-start(f32[3,3,8,16]{3,2,1,0:T(8,128)S(1)} %get-tuple-element.55), channel_id=1, source_target_pairs={{0,1},{1,2},{2,3},{3,4},{4,5},{5,6},{6,7},{7,0},{8,9},{9,10},{10,1... | collective-permute-start | bytes 13832 | tf_op jit(solution)/shard_map/ppermute | solution.py:459
  111.5 5.5 %copy-start.2 = (f32[3,3,8,16]{3,2,1,0:T(8,128)}, f32[3,3,8,16]{3,2,1,0:T(8,128)S(1)}, u32[]{:S(2)}) copy-start(f32[3,3,8,16]{3,2,1,0:T(8,128)S(1)} %collective-permute-done.11.l) | copy-start | bytes 13828
  117.0 0.6 copy-start.3
where the time goes:
time: 120 us; the launch traced here: 119 us
  Pallas kernels  74.1 us (62%)
  starting transfers between devices  22.3 us (19%)
  waiting for transfers between devices  15.7 us (13%)
  local copies, waits for them, and re-layouts  4.99 us (4%)
  other arithmetic  1.36 us (1%)
    pallas_call x5, Pallas kernels, vmem_call(): pl.pallas_call(kernel, out_shape=outs, in_specs=[spec] * len(args), out_s...  74.1 us
    ppermute x6, starting transfers between devices, to_left(): return lax.ppermute(x, axis, [((i + 1) % count, i) for i in range(count)])  20.6 us
    ppermute x6, waiting for transfers between devices, to_right(): return lax.ppermute(x, axis, [(i, (i + 1) % count) for i in range(count)])  13.8 us
  transfers between devices with their start and end apart: 12, of which 6 were waited for; matrix products, arithmetic and copies ran while one was open for 2% of the time, Pallas kernels for 5%

commit v1 on v0

--- a/solution.py
+++ b/solution.py
@@ -138,8 +138,8 @@
     return r * z - x * (r * r * r * inner)
 
 
-ROWS = 192
-GROUP = 4
+ROWS = 384
+GROUP = 16
 
 
 def layer_kernel(
@@ -211,20 +211,23 @@
 
         @pl.loop(0, atoms // GROUP)
         def _(step):
-            for u in range(GROUP):
-                span = pl.ds(pl.multiple_of(step * (GROUP * NBR) + u * NBR, 8), NBR)
-                weight = kwb[span, :]
-                for g in range(2):
-                    c = 128 * g
-                    q = spread(qkv[layer, span, c : c + 128])
-                    k = qkv[layer, span, D + c : D + c + 128].astype(BF)
-                    v = qkv[layer, span, 2 * D + c : 2 * D + c + 128].astype(BF)
-                    t = jnp.tanh(dot_nt(k, q) * score_scale)
-                    e = weight * jnp.exp(score_cap * t)
-                    p = e * (1.0 / jnp.sum(e, axis=0, keepdims=True))
-                    probs[layer, span, c : c + 128] = p
-                    slope[layer, span, c : c + 128] = (1.0 - t * t) * slope_scale
-                    att[span, c : c + 128] = gather_heads(dot_tn(p.astype(BF), v))
+            spans = [
+                pl.ds(pl.multiple_of(step * (GROUP * NBR) + u * NBR, 8), NBR) for u in range(GROUP)
+            ]
+            at = [(s, 128 * g) for s in spans for g in range(2)]
+            q = [spread(qkv[layer, s, c : c + 128]) for s, c in at]
+            k = [qkv[layer, s, D + c : D + c + 128].astype(BF) for s, c in at]
+            v = [qkv[layer, s, 2 * D + c : 2 * D + c + 128].astype(BF) for s, c in at]
+            t = [dot_nt(kk, qq) for kk, qq in zip(k, q)]
+            t = [jnp.tanh(tt * score_scale) for tt in t]
+            e = [kwb[s, :] * jnp.exp(score_cap * tt) for (s, c), tt in zip(at, t)]
+            p = [ee * (1.0 / jnp.sum(ee, axis=0, keepdims=True)) for ee in e]
+            o = [dot_tn(pp.astype(BF), vv) for pp, vv in zip(p, v)]
+            o = [gather_heads(oo) for oo in o]
+            for i, (s, c) in enumerate(at):
+                probs[layer, s, c : c + 128] = p[i]
+                slope[layer, s, c : c + 128] = (1.0 - t[i] * t[i]) * slope_scale
+                att[s, c : c + 128] = o[i]
 
         x = [xs[2 * layer, b, :] + dot_nn(att[b, :].astype(BF), w_out[layer]) for b in blocks]
         for b, v in zip(blocks, x):
@@ -281,28 +284,29 @@
 
         @pl.loop(0, atoms // GROUP)
         def _(step):
-            for u in range(GROUP):
-                span = pl.ds(pl.multiple_of(step * (GROUP * NBR) + u * NBR, 8), NBR)
-                total = None
-                for g in range(2):
-                    c = 128 * g
-                    q = spread(qkv[layer, span, c : c + 128])
-                    k = qkv[layer, span, D + c : D + c + 128].astype(BF)
-                    v = qkv[layer, span, 2 * D + c : 2 * D + c + 128].astype(BF)
-                    do = spread(att[span, c : c + 128])
-                    p = probs[layer, span, c : c + 128]
-                    dp = dot_nt(v, do)
-                    inner = jnp.sum(p * dp, axis=0, keepdims=True)
-                    dl = p * (dp - inner)
-                    total = dl if total is None else total + dl
-                    ds = (dl * slope[layer, span, c : c + 128]).astype(BF)
-                    dqkv[span, c : c + 128] = gather_heads(dot_tn(ds, k))
-                    dqkv[span, D + c : D + c + 128] = dot_nn(ds, q)
-                    dqkv[span, 2 * D + c : 2 * D + c + 128] = dot_nn(p.astype(BF), do)
-                if layer == 1:
-                    acc[span, :] = total
-                else:
-                    acc[span, :] = acc[span, :] + total
+            spans = [
+                pl.ds(pl.multiple_of(step * (GROUP * NBR) + u * NBR, 8), NBR) for u in range(GROUP)
+            ]
+            at = [(s, 128 * g) for s in spans for g in range(2)]
+            do = [spread(att[s, c : c + 128]) for s, c in at]
+            v = [qkv[layer, s, 2 * D + c : 2 * D + c + 128].astype(BF) for s, c in at]
+            p = [probs[layer, s, c : c + 128] for s, c in at]
+            dp = [dot_nt(vv, dd) for vv, dd in zip(v, do)]
+            dv = [dot_nn(pp.astype(BF), dd) for pp, dd in zip(p, do)]
+            q = [spread(qkv[layer, s, c : c + 128]) for s, c in at]
+            k = [qkv[layer, s, D + c : D + c + 128].astype(BF) for s, c in at]
+            dl = [pp * (dd - jnp.sum(pp * dd, axis=0, keepdims=True)) for pp, dd in zip(p, dp)]
+            ds = [(dd * slope[layer, s, c : c + 128]).astype(BF) for (s, c), dd in zip(at, dl)]
+            dk = [dot_nn(dd, qq) for dd, qq in zip(ds, q)]
+            dq = [gather_heads(dot_tn(dd, kk)) for dd, kk in zip(ds, k)]
+            old = [acc[s, :] for s in spans] if layer == 0 else None
+            for i, (s, c) in enumerate(at):
+                dqkv[s, c : c + 128] = dq[i]
+                dqkv[s, D + c : D + c + 128] = dk[i]
+                dqkv[s, 2 * D + c : 2 * D + c + 128] = dv[i]
+            for u, s in enumerate(spans):
+                total = dl[2 * u] + dl[2 * u + 1]
+                acc[s, :] = total if layer == 1 else old[u] + total
 
         gain = gains[2 * layer : 2 * layer + 1, :]
         dnorm = [dot_nt(dqkv[b, :].astype(BF), w_qkv[layer]) * gain for b in blocks]

time: 120 us -> 77.5 us (0.65)
  Pallas kernels: 74.1 us -> 31 us
    pallas_call x5, Pallas kernels: 74.1 us -> 31 us  [vmem_call(): pl.pallas_call(kernel, out_shape=outs, in_specs=[spec] * len(args), out_s...]
  transfers between devices with their start and end apart: 12 -> 12, of which waited for: 6 -> 6; matrix products, arithmetic and copies ran while one was open for 2% -> 3% of each run, Pallas kernels for 5% -> 7%
where the time goes in v1:
time: 77.5 us; the launch traced here: 76.4 us
  Pallas kernels  31 us (40%)
  starting transfers between devices  22.5 us (29%)
  waiting for transfers between devices  15.7 us (20%)
  local copies, waits for them, and re-layouts  4.99 us (6%)
  other arithmetic  1.36 us (2%)
    pallas_call x5, Pallas kernels, vmem_call(): pl.pallas_call(kernel, out_shape=outs, in_specs=[spec] * len(args), out_s...  31 us
    ppermute x6, starting transfers between devices, to_left(): return lax.ppermute(x, axis, [((i + 1) % count, i) for i in range(count)])  20.6 us
    ppermute x6, waiting for transfers between devices, to_right(): return lax.ppermute(x, axis, [(i, (i + 1) % count) for i in range(count)])  13.8 us
    ppermute x6, starting transfers between devices, to_right(): return lax.ppermute(x, axis, [(i, (i + 1) % count) for i in range(count)])  1.95 us
    ppermute x6, waiting for transfers between devices, to_left(): return lax.ppermute(x, axis, [((i + 1) % count, i) for i in range(count)])  1.93 us
  transfers between devices with their start and end apart: 12, of which 6 were waited for; matrix products, arithmetic and copies ran while one was open for 3% of the time, Pallas kernels for 7%

profile of v1, /device:TPU:0, one launch (start us, length us, event | category | flops | bytes accessed | tf_op | source)
XLA Modules:
  0.0 76.4 jit_solution(13480955756436743096)
XLA Ops:
  0.6 0.8 %fusion.8 = (s32[208]{0:T(256)S(1)}, s32[208]{0:T(256)S(1)}) fusion(s32[416]{0:T(512)} %param.20), kind=kLoop, calls=%fused_computation.18 | loop fusion | bytes 3328 | tf_op jit(solution)/shard_map/slice | solution.py:491
  1.5 0.7 pad_add_fusion
  2.1 2.9 %shard_map.184 = (bf16[768,256]{1,0:T(8,128)(2,1)}, bf16[144,256]{1,0:T(8,128)(2,1)}, bf16[144,256]{1,0:T(8,128)(2,1)}, bf16[144,256]{1,0:T(8,128)(2,1)}) custom-call(bf16[32,256]{1,0:T(8,128)(2,1)} %state.1, bf16[256,256]{1,0:T(8,128)(2,1)} %w_neigh.1, bf16[768,256]{1,0:T(8,128)(2,1)} %prev.1, s32[1,432]{1,0:T(1,128)} %bitcast.35), custom_call_target="tpu_custom_call" | custom-call | tf_op jit(solution)/shard_map/pallas_call | solution.py:380
  5.0 0.0 collective-permute-start
  5.0 1.7 %collective-permute-start.1 = (bf16[144,256]{1,0:T(8,128)(2,1)}, bf16[144,256]{1,0:T(8,128)(2,1)S(1)}, u32[]{:S(2)}, u32[]{:S(2)}) collective-permute-start(bf16[144,256]{1,0:T(8,128)(2,1)} %get-tuple-element.23), channel_id=1, source_target_pairs={{32,0},{64,32},{96,64},{0,96},{33,1},{65,33},{97,65},{1,97},{34,2}... | collective-permute-start | bytes 221192 | tf_op jit(solution)/shard_map/ppermute | solution.py:468
  6.7 0.0 copy-start.5
  6.7 0.8 %fusion.4 = (bf16[48,256]{1,0:T(8,128)(2,1)S(1)}, bf16[48,256]{1,0:T(8,128)(2,1)S(1)}, bf16[48,256]{1,0:T(8,128)(2,1)S(1)}) fusion(bf16[144,256]{1,0:T(8,128)(2,1)} %get-tuple-element.22), kind=kLoop, calls=%fused_computation.14 | loop fusion | bytes 147456 | tf_op jit(solution)/shard_map/slice | solution.py:507
  7.5 0.0 copy-done.5
  7.5 0.0 copy-start.6
  7.5 0.6 reshape.46.slot
  8.1 0.1 copy-done.6
  8.2 0.6 reshape.45.mask
  8.8 3.4 %shard_map.185 = (f32[768,256]{1,0:T(8,128)}, f32[768,128]{1,0:T(8,128)}, f32[72,768]{1,0:T(8,128)}, f32[8,768]{1,0:T(8,128)}, f32[32,432]{1,0:T(8,128)}, /*index=5*/f32[72,256]{1,0:T(8,128)}) custom-call(f32[3,768]{1,0:T(4,128)} %disp.1, s32[1,768]{1,0:T(1,128)} %reshape.45.mask, s32[1,768]{1,0:T(1,128)} %reshape.46.slot, s32[1,32]{1,0:T(1,128)} %bitcast.43, ...), custom_call_target="tpu_custom_call" | custom-call | tf_op jit(solution)/shard_map/pallas_call | solution.py:380
  12.2 0.0 collective-permute-done
  12.2 0.0 collective-permute-done.1
  12.3 3.2 %collective-permute-start.3 = (bf16[3,3,16,256]{3,2,1,0:T(8,128)(2,1)S(1)}, bf16[3,3,16,256]{3,2,1,0:T(8,128)(2,1)S(1)}, u32[]{:S(2)}, u32[]{:S(2)}) collective-permute-start(bf16[3,3,16,256]{3,2,1,0:T(8,128)(2,1)S(1)} %pad_maximum_fusion.2), channel_id=1, source_target_pairs={{8,0},{16,8},{24,16},{0,24},{9,1},{17,9},{25,17},{1,25},{10,2},{18... | collective-permute-start | bytes 221192 | tf_op jit(solution)/shard_map/ppermute | solution.py:468
  15.5 0.1 collective-permute-start.2
  15.6 1.9 %collective-permute-done.3 = bf16[3,3,16,256]{3,2,1,0:T(8,128)(2,1)S(1)} collective-permute-done((bf16[3,3,16,256]{3,2,1,0:T(8,128)(2,1)S(1)}, bf16[3,3,16,256]{3,2,1,0:T(8,128)(2,1)S(1)}, u32[]{:S(2)}, u32[]{:S(2)}) %collective-permute-start.3) | collective-permute-done | bytes 73760 | tf_op jit(solution)/shard_map/ppermute | solution.py:468
  17.5 3.7 %collective-permute-done.2 = bf16[3,3,16,256]{3,2,1,0:T(8,128)(2,1)S(1)} collective-permute-done((bf16[3,3,16,256]{3,2,1,0:T(8,128)(2,1)S(1)}, bf16[3,3,16,256]{3,2,1,0:T(8,128)(2,1)S(1)}, u32[]{:S(2)}, u32[]{:S(2)}) %collective-permute-start.2) | collective-permute-done | bytes 73760 | tf_op jit(solution)/shard_map/ppermute | solution.py:463
  21.1 1.6 %collective-permute-start.4 = (bf16[3,3,16,256]{3,2,1,0:T(8,128)(2,1)S(1)}, bf16[3,3,16,256]{3,2,1,0:T(8,128)(2,1)S(1)}, u32[]{:S(2)}, u32[]{:S(2)}) collective-permute-start(bf16[3,3,16,256]{3,2,1,0:T(8,128)(2,1)S(1)} %pad_maximum_fusion.3), channel_id=1, source_target_pairs={{0,1},{1,2},{2,3},{3,4},{4,5},{5,6},{6,7},{7,0},{8,9},{9,10},{10,1... | collective-permute-start | bytes 221192 | tf_op jit(solution)/shard_map/ppermute | solution.py:463
  22.7 4.9 %collective-permute-start.5 = (bf16[3,3,16,256]{3,2,1,0:T(8,128)(2,1)S(1)}, bf16[3,3,16,256]{3,2,1,0:T(8,128)(2,1)S(1)}, u32[]{:S(2)}, u32[]{:S(2)}) collective-permute-start(bf16[3,3,16,256]{3,2,1,0:T(8,128)(2,1)S(1)} %pad_maximum_fusion.5), channel_id=1, source_target_pairs={{1,0},{2,1},{3,2},{4,3},{5,4},{6,5},{7,6},{0,7},{9,8},{10,9},{11,1... | collective-permute-start | bytes 221192 | tf_op jit(solution)/shard_map/ppermute | solution.py:468
  27.6 0.6 pad_maximum_fusion.4
  28.2 1.4 %collective-permute-done.4 = bf16[3,3,16,256]{3,2,1,0:T(8,128)(2,1)S(1)} collective-permute-done((bf16[3,3,16,256]{3,2,1,0:T(8,128)(2,1)S(1)}, bf16[3,3,16,256]{3,2,1,0:T(8,128)(2,1)S(1)}, u32[]{:S(2)}, u32[]{:S(2)}) %collective-permute-start.4) | collective-permute-done | bytes 73760 | tf_op jit(solution)/shard_map/ppermute | solution.py:463
  29.6 0.0 copy-start
  29.6 0.0 collective-permute-done.5
  29.6 0.0 copy-start.1
  29.6 0.6 copy-done
  30.2 0.0 copy-done.1
  30.3 20.9 %shard_map.186 = (bf16[768,256]{1,0:T(8,128)(2,1)}, f32[1,32]{1,0:T(1,128)}, f32[8,768]{1,0:T(8,128)}, f32[8,144]{1,0:T(8,128)}, f32[8,144]{1,0:T(8,128)}, /*index=5*/f32[8,144]{1,0:T(8,128)}) custom-call(f32[768,256]{1,0:T(8,128)} %get-tuple-element.20.base, bf16[144,256]{1,0:T(8,128)(2,1)} %bitcast.33, bf16[144,256]{1,0:T(8,128)(2,1)} %bitcast.23, ...), custom_call_target="tpu_custom_call" | custom-call | tf_op jit(solution)/shard_map/pallas_call | solution.py:380
  51.2 0.0 copy-start.4
  51.2 0.3 collective-permute-start.6
  51.5 1.7 %collective-permute-start.7 = (f32[8,144]{1,0:T(8,128)}, f32[8,144]{1,0:T(8,128)S(1)}, u32[]{:S(2)}, u32[]{:S(2)}) collective-permute-start(f32[8,144]{1,0:T(8,128)} %get-tuple-element.34), channel_id=1, source_target_pairs={{32,0},{64,32},{96,64},{0,96},{33,1},{65,33},{97,65},{1,97},{34,2}... | collective-permute-start | bytes 13832 | tf_op jit(solution)/shard_map/ppermute | solution.py:468
  53.2 1.5 %collective-permute-done.6 = f32[8,144]{1,0:T(8,128)S(1)} collective-permute-done((f32[8,144]{1,0:T(8,128)}, f32[8,144]{1,0:T(8,128)S(1)}, u32[]{:S(2)}, u32[]{:S(2)}) %collective-permute-start.6) | collective-permute-done | bytes 4640 | tf_op jit(solution)/shard_map/ppermute | solution.py:463
  54.8 0.0 collective-permute-done.7
  54.8 0.0 copy-done.4
  54.8 0.1 fusion.7
  54.9 0.0 collective-permute-start.8
  54.9 3.2 %collective-permute-start.9 = (f32[3,8,48]{2,1,0:T(8,128)S(1)}, f32[3,8,48]{2,1,0:T(8,128)S(1)}, u32[]{:S(2)}, u32[]{:S(2)}) collective-permute-start(f32[3,8,48]{2,1,0:T(8,128)S(1)} %get-tuple-element.57), channel_id=1, source_target_pairs={{8,0},{16,8},{24,16},{0,24},{9,1},{17,9},{25,17},{1,25},{10,2},{18... | collective-permute-start | bytes 13832 | tf_op jit(solution)/shard_map/ppermute | solution.py:468
  58.1 1.7 %collective-permute-done.8 = f32[3,8,48]{2,1,0:T(8,128)S(1)} collective-permute-done((f32[3,8,48]{2,1,0:T(8,128)S(1)}, f32[3,8,48]{2,1,0:T(8,128)S(1)}, u32[]{:S(2)}, u32[]{:S(2)}) %collective-permute-start.8) | collective-permute-done | bytes 4640 | tf_op jit(solution)/shard_map/ppermute | solution.py:463
  59.8 0.0 collective-permute-done.9
  59.8 0.7 fusion.6
  60.5 5.9 %collective-permute-start.11 = (f32[3,3,8,16]{3,2,1,0:T(8,128)S(1)}, f32[3,3,8,16]{3,2,1,0:T(8,128)S(1)}, u32[]{:S(2)}, u32[]{:S(2)}) collective-permute-start(f32[3,3,8,16]{3,2,1,0:T(8,128)S(1)} %get-tuple-element.53), channel_id=1, source_target_pairs={{1,0},{2,1},{3,2},{4,3},{5,4},{6,5},{7,6},{0,7},{9,8},{10,9},{11,1... | collective-permute-start | bytes 13832 | tf_op jit(solution)/shard_map/ppermute | solution.py:468
  66.4 0.0 collective-permute-start.10
  66.4 2.2 %shard_map.187.partial = f32[8,32]{1,0:T(8,128)} custom-call(f32[8,768]{1,0:T(8,128)} %get-tuple-element.30.grad, s32[1,768]{1,0:T(1,128)} %reshape.46.slot, f32[8,768]{1,0:T(8,128)} %get-tuple-element.26.rows), custom_call_target="tpu_custom_call" | custom-call | tf_op jit(solution)/shard_map/pallas_call | solution.py:380
  68.6 0.0 collective-permute-done.11.l
  68.6 0.0 copy-start.2
  68.6 5.5 %collective-permute-done.10.r = f32[3,3,8,16]{3,2,1,0:T(8,128)S(1)} collective-permute-done((f32[3,3,8,16]{3,2,1,0:T(8,128)S(1)}, f32[3,3,8,16]{3,2,1,0:T(8,128)S(1)}, u32[]{:S(2)}, u32[]{:S(2)}) %collective-permute-start.10) | collective-permute-done | bytes 4640 | tf_op jit(solution)/shard_map/ppermute | solution.py:463
  74.1 0.0 copy-start.3
  74.1 0.0 copy-done.2
  74.1 0.6 copy-done.3
  74.7 1.6 %shard_map.188 = f32[3,32]{1,0:T(4,128)} custom-call(f32[8,32]{1,0:T(8,128)} %shard_map.187.partial, f32[32,432]{1,0:T(8,128)} %get-tuple-element.31.mt, f32[3,3,8,16]{3,2,1,0:T(8,128)} %copy-done.3, f32[3,3,8,16]{3,2,1,0:T(8,128)} %get-tuple-element.54.m, f32[3,3,8,16]{3,2,1,0:T(8,128)} %copy-done.2), custom_call_target="tpu_custom_call" | custom-call | tf_op jit(solution)/shard_map/pallas_call | solution.py:380
  (13 shorter events, 0.1 us)
Async XLA Ops:
  5.0 7.2 %collective-permute-start = (bf16[144,256]{1,0:T(8,128)(2,1)}, bf16[144,256]{1,0:T(8,128)(2,1)S(1)}, u32[]{:S(2)}, u32[]{:S(2)}) collective-permute-start(bf16[144,256]{1,0:T(8,128)(2,1)} %get-tuple-element.21), channel_id=1, source_target_pairs={{0,32},{32,64},{64,96},{96,0},{1,33},{33,65},{65,97},{97,1},{2,34}... | collective-permute-start | bytes 221192 | tf_op jit(solution)/shard_map/ppermute | solution.py:463
  5.0 7.2 %collective-permute-start.1 = (bf16[144,256]{1,0:T(8,128)(2,1)}, bf16[144,256]{1,0:T(8,128)(2,1)S(1)}, u32[]{:S(2)}, u32[]{:S(2)}) collective-permute-start(bf16[144,256]{1,0:T(8,128)(2,1)} %get-tuple-element.23), channel_id=1, source_target_pairs={{32,0},{64,32},{96,64},{0,96},{33,1},{65,33},{97,65},{1,97},{34,2}... | collective-permute-start | bytes 221192 | tf_op jit(solution)/shard_map/ppermute | solution.py:468
  6.7 0.8 %copy-start.5 = (s32[768]{0:T(1024)S(1)}, s32[768]{0:T(1024)}, u32[]{:S(2)}) copy-start(s32[768]{0:T(1024)} %param.19) | copy-start | bytes 9220
  7.5 0.7 copy-start.6
  12.3 5.1 %collective-permute-start.3 = (bf16[3,3,16,256]{3,2,1,0:T(8,128)(2,1)S(1)}, bf16[3,3,16,256]{3,2,1,0:T(8,128)(2,1)S(1)}, u32[]{:S(2)}, u32[]{:S(2)}) collective-permute-start(bf16[3,3,16,256]{3,2,1,0:T(8,128)(2,1)S(1)} %pad_maximum_fusion.2), channel_id=1, source_target_pairs={{8,0},{16,8},{24,16},{0,24},{9,1},{17,9},{25,17},{1,25},{10,2},{18... | collective-permute-start | bytes 221192 | tf_op jit(solution)/shard_map/ppermute | solution.py:468
  15.5 5.6 %collective-permute-start.2 = (bf16[3,3,16,256]{3,2,1,0:T(8,128)(2,1)S(1)}, bf16[3,3,16,256]{3,2,1,0:T(8,128)(2,1)S(1)}, u32[]{:S(2)}, u32[]{:S(2)}) collective-permute-start(bf16[3,3,16,256]{3,2,1,0:T(8,128)(2,1)S(1)} %pad_maximum_fusion), channel_id=1, source_target_pairs={{0,8},{8,16},{16,24},{24,0},{1,9},{9,17},{17,25},{25,1},{2,10},{10... | collective-permute-start | bytes 221192 | tf_op jit(solution)/shard_map/ppermute | solution.py:463
  21.1 8.5 %collective-permute-start.4 = (bf16[3,3,16,256]{3,2,1,0:T(8,128)(2,1)S(1)}, bf16[3,3,16,256]{3,2,1,0:T(8,128)(2,1)S(1)}, u32[]{:S(2)}, u32[]{:S(2)}) collective-permute-start(bf16[3,3,16,256]{3,2,1,0:T(8,128)(2,1)S(1)} %pad_maximum_fusion.3), channel_id=1, source_target_pairs={{0,1},{1,2},{2,3},{3,4},{4,5},{5,6},{6,7},{7,0},{8,9},{9,10},{10,1... | collective-permute-start | bytes 221192 | tf_op jit(solution)/shard_map/ppermute | solution.py:463
  22.7 6.9 %collective-permute-start.5 = (bf16[3,3,16,256]{3,2,1,0:T(8,128)(2,1)S(1)}, bf16[3,3,16,256]{3,2,1,0:T(8,128)(2,1)S(1)}, u32[]{:S(2)}, u32[]{:S(2)}) collective-permute-start(bf16[3,3,16,256]{3,2,1,0:T(8,128)(2,1)S(1)} %pad_maximum_fusion.5), channel_id=1, source_target_pairs={{1,0},{2,1},{3,2},{4,3},{5,4},{6,5},{7,6},{0,7},{9,8},{10,9},{11,1... | collective-permute-start | bytes 221192 | tf_op jit(solution)/shard_map/ppermute | solution.py:468
  29.6 0.6 copy-start
  29.6 0.7 copy-start.1
  51.2 3.6 %copy-start.4 = (f32[8,144]{1,0:T(8,128)S(1)}, f32[8,144]{1,0:T(8,128)}, u32[]{:S(2)}) copy-start(f32[8,144]{1,0:T(8,128)} %get-tuple-element.33) | copy-start | bytes 13828
  51.2 3.6 %collective-permute-start.6 = (f32[8,144]{1,0:T(8,128)}, f32[8,144]{1,0:T(8,128)S(1)}, u32[]{:S(2)}, u32[]{:S(2)}) collective-permute-start(f32[8,144]{1,0:T(8,128)} %get-tuple-element.32), channel_id=1, source_target_pairs={{0,32},{32,64},{64,96},{96,0},{1,33},{33,65},{65,97},{97,1},{2,34}... | collective-permute-start | bytes 13832 | tf_op jit(solution)/shard_map/ppermute | solution.py:463
  51.5 3.3 %collective-permute-start.7 = (f32[8,144]{1,0:T(8,128)}, f32[8,144]{1,0:T(8,128)S(1)}, u32[]{:S(2)}, u32[]{:S(2)}) collective-permute-start(f32[8,144]{1,0:T(8,128)} %get-tuple-element.34), channel_id=1, source_target_pairs={{32,0},{64,32},{96,64},{0,96},{33,1},{65,33},{97,65},{1,97},{34,2}... | collective-permute-start | bytes 13832 | tf_op jit(solution)/shard_map/ppermute | solution.py:468
  54.9 4.9 %collective-permute-start.8 = (f32[3,8,48]{2,1,0:T(8,128)S(1)}, f32[3,8,48]{2,1,0:T(8,128)S(1)}, u32[]{:S(2)}, u32[]{:S(2)}) collective-permute-start(f32[3,8,48]{2,1,0:T(8,128)S(1)} %get-tuple-element.56), channel_id=1, source_target_pairs={{0,8},{8,16},{16,24},{24,0},{1,9},{9,17},{17,25},{25,1},{2,10},{10... | collective-permute-start | bytes 13832 | tf_op jit(solution)/shard_map/ppermute | solution.py:463
  54.9 4.9 %collective-permute-start.9 = (f32[3,8,48]{2,1,0:T(8,128)S(1)}, f32[3,8,48]{2,1,0:T(8,128)S(1)}, u32[]{:S(2)}, u32[]{:S(2)}) collective-permute-start(f32[3,8,48]{2,1,0:T(8,128)S(1)} %get-tuple-element.57), channel_id=1, source_target_pairs={{8,0},{16,8},{24,16},{0,24},{9,1},{17,9},{25,17},{1,25},{10,2},{18... | collective-permute-start | bytes 13832 | tf_op jit(solution)/shard_map/ppermute | solution.py:468
  60.5 8.1 %collective-permute-start.11 = (f32[3,3,8,16]{3,2,1,0:T(8,128)S(1)}, f32[3,3,8,16]{3,2,1,0:T(8,128)S(1)}, u32[]{:S(2)}, u32[]{:S(2)}) collective-permute-start(f32[3,3,8,16]{3,2,1,0:T(8,128)S(1)} %get-tuple-element.53), channel_id=1, source_target_pairs={{1,0},{2,1},{3,2},{4,3},{5,4},{6,5},{7,6},{0,7},{9,8},{10,9},{11,1... | collective-permute-start | bytes 13832 | tf_op jit(solution)/shard_map/ppermute | solution.py:468
  66.4 7.7 %collective-permute-start.10 = (f32[3,3,8,16]{3,2,1,0:T(8,128)S(1)}, f32[3,3,8,16]{3,2,1,0:T(8,128)S(1)}, u32[]{:S(2)}, u32[]{:S(2)}) collective-permute-start(f32[3,3,8,16]{3,2,1,0:T(8,128)S(1)} %get-tuple-element.55), channel_id=1, source_target_pairs={{0,1},{1,2},{2,3},{3,4},{4,5},{5,6},{6,7},{7,0},{8,9},{9,10},{10,1... | collective-permute-start | bytes 13832 | tf_op jit(solution)/shard_map/ppermute | solution.py:463
  68.6 5.5 %copy-start.2 = (f32[3,3,8,16]{3,2,1,0:T(8,128)}, f32[3,3,8,16]{3,2,1,0:T(8,128)S(1)}, u32[]{:S(2)}) copy-start(f32[3,3,8,16]{3,2,1,0:T(8,128)S(1)} %collective-permute-done.11.l) | copy-start | bytes 13828
  74.1 0.6 copy-start.3

commit v2 on v1

--- a/solution.py
+++ b/solution.py
@@ -21,6 +21,7 @@
 score_cap = 8.0
 cutoff_radius = 5.0
 norm_eps = 1e-06
+AXES = ("gx", "gy", "gz")
 
 BF = jnp.bfloat16
 F32 = jnp.float32
@@ -64,7 +65,7 @@
     return jnp.where(lanes == column, 1.0, 0.0).astype(BF)
 
 
-def message_kernel(state, w_neigh, prev, send, message, low, mid, high):
+def message_kernel(state, w_neigh, prev, send, message, low, mid, high, where, order):
     projected = dot_nn(state[...], w_neigh[...])
     expand = atom_rows(ATOMS_DEV)
     hi, lo = split2(projected)
@@ -72,8 +73,22 @@
     wide = dot_nn(expand, hi) + dot_nn(expand, lo) + dot_nn(expand, rest)
     out = (prev[...].astype(F32) + wide).astype(BF)
     message[...] = out
-    pick = one_hot_lanes(as_column(send[...].astype(F32)), EDGE_DEV)
-    payload = dot_nn(pick, out).astype(BF)
+    count = 26 * SLOTS
+    sent = jnp.broadcast_to(send[...].reshape(1, count).astype(F32), (8, count)).T
+    flips = [lax.axis_index(axis) & 1 for axis in AXES]
+    for bucket in range(27):
+        place = 0
+        for axis, digit in enumerate((bucket // 9, bucket // 3 % 3, bucket % 3)):
+            place = place * 3 + digit + flips[axis] * (2 - 2 * digit)
+        rows = pl.ds(pl.multiple_of(place * SLOTS, SLOTS), SLOTS)
+        if bucket == 13:
+            order[rows, :] = jnp.full((SLOTS, 8), -1.0, F32)
+        else:
+            start = (bucket - (bucket > 13)) * SLOTS
+            order[rows, :] = sent[start : start + SLOTS]
+    column = order[...]
+    where[...] = column
+    payload = dot_nn(one_hot_lanes(column[:, 0:1], EDGE_DEV), out).astype(BF)
     low[...] = payload[0:SIDE]
     mid[...] = payload[SIDE : 2 * SIDE]
     high[...] = payload[2 * SIDE : 3 * SIDE]
@@ -83,8 +98,13 @@
     far = slot - EDGE_DEV
     bucket = far >> 4
     pair = (bucket * 11) >> 5
-    third = bucket - 3 * pair
-    return jnp.where(far >= 0, third * SIDE + pair * SLOTS + (far & 15), -1).astype(F32)
+    first = (pair * 11) >> 5
+    digits = [first, pair - 3 * first, bucket - 3 * pair]
+    for i, axis in enumerate(AXES):
+        flip = lax.axis_index(axis) & 1
+        digits[i] = digits[i] + flip * (2 - 2 * digits[i])
+    place = digits[2] * SIDE + (digits[0] * 3 + digits[1]) * SLOTS + (far & 15)
+    return jnp.where(far >= 0, place, -1).astype(F32)
 
 
 def geometry_kernel(
@@ -94,7 +114,7 @@
     dist = jnp.sqrt(jnp.sum(d * d, axis=0, keepdims=True) + 0.5)
     angle = (math.pi / cutoff_radius) * dist
     cut = 0.5 * (jnp.cos(angle) + 1.0)
-    live = mask[...].astype(F32)
+    live = mask[...].reshape(1, EDGE_DEV).astype(F32)
     kw = live * cut
     centres = 0.5 + 4.0 * iota((NB, 1), 0).astype(F32) / (NB - 1)
     offset = dist - centres
@@ -117,10 +137,10 @@
     w = wfeat[...]
     whi = w.astype(BF).astype(F32)
     right = jnp.concatenate([whi, whi, w - whi], axis=0).astype(BF)
-    kind = jnp.where(iota((NSPEC, ATOMS_DEV), 0) == species[...], 1.0, 0.0).astype(BF)
+    kind = jnp.where(iota((NSPEC, ATOMS_DEV), 0) == species[...].reshape(1, ATOMS_DEV), 1.0, 0.0).astype(BF)
     centre = dot_tn(kind, table[...]).astype(BF)
     expand = atom_rows(ATOMS_DEV)
-    slot_row = slot[...]
+    slot_row = slot[...].reshape(1, EDGE_DEV)
     local = one_hot_lanes(as_column(slot_row.astype(F32)), EDGE_DEV)
     base[...] = dot_nn(left, right) + dot_nn(expand, centre) + dot_nn(local, message[...])
     kwb[...] = jnp.broadcast_to(as_column(kw), (EDGE_DEV, 128))
@@ -197,7 +217,7 @@
             out = jnp.where(head_lanes[h], wide[h * NBR : (h + 1) * NBR], out)
         return out
 
-    far = one_hot_lanes(as_column(remote_index(slot[...])), 3 * SIDE)
+    far = one_hot_lanes(as_column(remote_index(slot[...].reshape(1, EDGE_DEV))), 3 * SIDE)
     arrived = jnp.concatenate([arr_r[...], arr_m[...], arr_l[...]], axis=0)
     x = [base[b, :] + dot_nn(far[b], arrived) for b in blocks]
 
@@ -341,8 +361,7 @@
     grad[...] = g
     ghi = g.astype(BF).astype(F32)
     both = jnp.concatenate([ghi, g - ghi], axis=0).astype(BF)
-    pick = jnp.where(iota((edges, 3 * SIDE), 0) == send[...], 1.0, 0.0).astype(BF)
-    out = dot_nn(both, pick)
+    out = dot_nt(both, one_hot_lanes(send[:, 0:1], edges))
     out = out[0:8] + out[8:16]
     low[...] = out[:, 0:SIDE]
     mid[...] = out[:, SIDE : 2 * SIDE]
@@ -353,7 +372,7 @@
     g = grad[...]
     ghi = g.astype(BF).astype(F32)
     both = jnp.concatenate([ghi, g - ghi], axis=0).astype(BF)
-    local = one_hot_lanes(as_column(slot[...].astype(F32)), EDGE_DEV)
+    local = one_hot_lanes(as_column(slot[...].reshape(1, EDGE_DEV).astype(F32)), EDGE_DEV)
     partner = dot_nt(both, local)
     diff = (g - partner[0:8] - partner[8:16]) * rows[2:3, :]
     hi = diff.astype(BF).astype(F32)
@@ -395,11 +414,12 @@
     side = shape((SIDE, D), BF)
     return vmem_call(
         message_kernel,
-        [shape((EDGE_DEV, D), BF), side, side, side],
+        [shape((EDGE_DEV, D), BF), side, side, side, shape((3 * SIDE, 8))],
         atom_state,
         w_neigh,
         prev_tokens,
         send,
+        scratch=[VMEM((3 * SIDE, 8), F32)],
     )
 
 
@@ -458,14 +478,11 @@
     )
 
 
-def to_right(x, axis):
+def exchange(low, high, axis):
     count = lax.axis_size(axis)
-    return lax.ppermute(x, axis, [(i, (i + 1) % count) for i in range(count)])
-
-
-def to_left(x, axis):
-    count = lax.axis_size(axis)
-    return lax.ppermute(x, axis, [((i + 1) % count, i) for i in range(count)])
+    outer = [(i, (i + 1 if i % 2 else i - 1) % count) for i in range(count)]
+    inner = [(i, i + 1 if i % 2 == 0 else i - 1) for i in range(count)]
+    return lax.ppermute(low, axis, outer), lax.ppermute(high, axis, inner)
 
 
 def on_device(
@@ -487,33 +504,24 @@
     w_down,
     w_energy,
 ):
-    centre = jnp.full((SLOTS,), -1, jnp.int32)
-    send = jnp.concatenate([send_edges[: 13 * SLOTS], centre, send_edges[13 * SLOTS :]])
-    send = send.reshape(1, 3 * SIDE)
-    slot = reverse_slot.reshape(1, EDGE_DEV)
-    message, low, mid, high = messages(atom_state, w_neigh, prev_tokens, send)
-    right, left = to_right(high, "gx"), to_left(low, "gx")
+    message, low, mid, high, where = messages(atom_state, w_neigh, prev_tokens, send_edges)
+    low, high = exchange(low, high, "gx")
+    cells = [v.reshape(3, 3, SLOTS, D) for v in (low, mid, high)]
+    low, mid, high = (jnp.stack([v[i] for v in cells]) for i in range(3))
+    low, mid, high = lax.optimization_barrier((low, mid, high))
+    low, high = exchange(low, high, "gy")
+    cells = (low, mid, high)
+    low, mid, high = (jnp.stack([v[:, i] for v in cells], axis=1) for i in range(3))
+    low, mid, high, late = lax.optimization_barrier((low, mid, high, displacement))
+    low, high = exchange(low, high, "gz")
     base, kwb, feat, rows, mt, wfeat = geometry(
-        displacement,
-        neighbour_mask.reshape(1, EDGE_DEV),
-        slot,
-        species.reshape(1, ATOMS_DEV),
-        message,
-        species_table,
-        w_vec,
-        w_rbf,
-    )
-    cells = [v.reshape(3, 3, SLOTS, D) for v in (right, mid, left)]
-    high, mid, low = (jnp.stack([v[i] for v in cells]) for i in (2, 1, 0))
-    right, left = to_right(high, "gy"), to_left(low, "gy")
-    cells = (right, mid, left)
-    high, mid, low = (jnp.stack([v[:, i] for v in cells], axis=1) for i in (2, 1, 0))
-    right, left = to_right(high, "gz"), to_left(low, "gz")
-    arr = [v.reshape(SIDE, D) for v in (right, mid, left)]
+        late, neighbour_mask, reverse_slot, species, message, species_table, w_vec, w_rbf
+    )
+    arr = [v.reshape(SIDE, D) for v in (low, mid, high)]
     tokens, energy, grad, low, mid, high = layers(
         base,
         arr,
-        slot,
+        reverse_slot,
         kwb,
         feat,
         rows,
@@ -524,18 +532,22 @@
         w_up,
         w_down,
         w_energy.reshape(1, D),
-        send,
-    )
-    right, left = to_right(high, "gx"), to_left(low, "gx")
-    partial = vmem_call(local_force_kernel, shape((8, ATOMS_DEV)), grad, slot, rows)
-    cells = jnp.stack([right, mid, left])
+        where,
+    )
+    low, high = exchange(low, high, "gx")
+    cells = jnp.stack([low, mid, high])
     cut = 3 * SLOTS
-    right, left = to_right(cells[:, :, 2 * cut :], "gy"), to_left(cells[:, :, :cut], "gy")
-    cells = jnp.stack([right, cells[:, :, cut : 2 * cut], left])
+    low, mid, high = (cells[:, :, i * cut : (i + 1) * cut] for i in range(3))
+    low, high = exchange(low, high, "gy")
+    cells = jnp.stack([low, mid, high])
     cut = SLOTS
-    right, left = to_right(cells[..., 2 * cut :], "gz"), to_left(cells[..., :cut], "gz")
-    mid = cells[..., cut : 2 * cut]
-    forces = vmem_call(force_kernel, shape((3, ATOMS_DEV)), partial, mt, right, mid, left)
+    low, mid, high = (cells[..., i * cut : (i + 1) * cut] for i in range(3))
+    low, mid, high, late = lax.optimization_barrier((low, mid, high, grad))
+    low, high = exchange(low, high, "gz")
+    partial = vmem_call(
+        local_force_kernel, shape((8, ATOMS_DEV)), late, reverse_slot, rows
+    )
+    forces = vmem_call(force_kernel, shape((3, ATOMS_DEV)), partial, mt, low, mid, high)
     return (tokens, energy.reshape(ATOMS_DEV), forces)
 
 

time: 77.5 us -> 68.1 us (0.88); the launches traced: 76.4 us -> 67.8 us
  starting transfers between devices: 22.5 us -> 18 us
  local copies, waits for them, and re-layouts: 4.99 us -> 2.81 us
  waiting for transfers between devices: 15.7 us -> 14 us
    ppermute x12, starting transfers between devices: 22.5 us -> 18 us  [exchange(): return (lax.ppermute(low, axis, outer), lax.ppermute(high, axis, inner))]
    ppermute x12, waiting for transfers between devices: 15.7 us -> 14 us  [exchange(): return (lax.ppermute(low, axis, outer), lax.ppermute(high, axis, inner))]
    reshape x2 -> x0, local copies, waits for them, and re-layouts: 1.18 us -> none  [the longest x1 0.6 us: on_device(): neighbour_mask.reshape(1, EDGE_DEV)]
    slice x6 -> x5, local copies, waits for them, and re-layouts: 2.4 us -> 1.56 us  [the longest x3 0.79 us: on_device(): low, mid, high = (jnp.stack([v[i] for v in cells]) for i in range(3))]
  transfers between devices with their start and end apart: 12 -> 12, of which waited for: 6 -> 7; matrix products, arithmetic and copies ran while one was open for 3% -> 1% of each run, Pallas kernels for 7% -> 8%
where the time goes in v2:
time: 68.1 us; the launch traced here: 67.8 us
  Pallas kernels  31.5 us (46%)
  starting transfers between devices  18 us (26%)
  waiting for transfers between devices  14 us (21%)
  local copies, waits for them, and re-layouts  2.81 us (4%)
  between operations  0.71 us (1%)
  other arithmetic  0.69 us (1%)
    pallas_call x5, Pallas kernels, vmem_call(): pl.pallas_call(kernel, out_shape=outs, in_specs=[spec] * len(args), out_s...  31.5 us
    ppermute x12, starting transfers between devices, exchange(): return (lax.ppermute(low, axis, outer), lax.ppermute(high, axis, inner))  18 us
    ppermute x12, waiting for transfers between devices, exchange(): return (lax.ppermute(low, axis, outer), lax.ppermute(high, axis, inner))  14 us
  transfers between devices with their start and end apart: 12, of which 7 were waited for; matrix products, arithmetic and copies ran while one was open for 1% of the time, Pallas kernels for 8%

profile of v2, /device:TPU:0, one launch (start us, length us, event | category | flops | bytes accessed | tf_op | source)
XLA Modules:
  0.0 67.8 jit_solution(12186009193952694538)
XLA Ops:
  0.6 3.0 %shard_map.184 = (bf16[768,256]{1,0:T(8,128)(2,1)}, bf16[144,256]{1,0:T(8,128)(2,1)}, bf16[144,256]{1,0:T(8,128)(2,1)}, bf16[144,256]{1,0:T(8,128)(2,1)}, f32[432,8]{1,0:T(8,128)}) custom-call(bf16[32,256]{1,0:T(8,128)(2,1)} %state.1, bf16[256,256]{1,0:T(8,128)(2,1)} %w_neigh.1, bf16[768,256]{1,0:T(8,128)(2,1)} %prev.1, s32[416]{0:T(512)} %send.1), custom_call_target="tpu_custom_call" | custom-call | tf_op jit(solution)/shard_map/pallas_call | solution.py:399
  3.6 1.4 %collective-permute-start = (bf16[144,256]{1,0:T(8,128)(2,1)}, bf16[144,256]{1,0:T(8,128)(2,1)S(1)}, u32[]{:S(2)}, u32[]{:S(2)}) collective-permute-start(bf16[144,256]{1,0:T(8,128)(2,1)} %get-tuple-element.31), channel_id=1, source_target_pairs={{0,96},{32,64},{64,32},{96,0},{1,97},{33,65},{65,33},{97,1},{2,98}... | collective-permute-start | bytes 221192 | tf_op jit(solution)/shard_map/ppermute | solution.py:485
  5.0 0.7 collective-permute-start.1
  5.7 0.8 %fusion.4 = (bf16[48,256]{1,0:T(8,128)(2,1)S(1)}, bf16[48,256]{1,0:T(8,128)(2,1)S(1)}, bf16[48,256]{1,0:T(8,128)(2,1)S(1)}) fusion(bf16[144,256]{1,0:T(8,128)(2,1)} %get-tuple-element.32), kind=kLoop, calls=%fused_computation.13 | loop fusion | bytes 147456 | tf_op jit(solution)/shard_map/slice | solution.py:510
  6.5 1.5 %collective-permute-done = bf16[144,256]{1,0:T(8,128)(2,1)S(1)} collective-permute-done((bf16[144,256]{1,0:T(8,128)(2,1)}, bf16[144,256]{1,0:T(8,128)(2,1)S(1)}, u32[]{:S(2)}, u32[]{:S(2)}) %collective-permute-start) | collective-permute-done | bytes 73760 | tf_op jit(solution)/shard_map/ppermute | solution.py:485
  8.0 0.0 collective-permute-done.1
  8.1 3.2 %collective-permute-start.2 = (bf16[3,3,16,256]{3,2,1,0:T(8,128)(2,1)S(1)}, bf16[3,3,16,256]{3,2,1,0:T(8,128)(2,1)S(1)}, u32[]{:S(2)}, u32[]{:S(2)}) collective-permute-start(bf16[3,3,16,256]{3,2,1,0:T(8,128)(2,1)S(1)} %get-tuple-element.34), channel_id=1, source_target_pairs={{0,24},{8,16},{16,8},{24,0},{1,25},{9,17},{17,9},{25,1},{2,26},{10... | collective-permute-start | bytes 221192 | tf_op jit(solution)/shard_map/ppermute | solution.py:485
  11.2 0.1 collective-permute-start.3
  11.4 2.5 %collective-permute-done.2 = bf16[3,3,16,256]{3,2,1,0:T(8,128)(2,1)S(1)} collective-permute-done((bf16[3,3,16,256]{3,2,1,0:T(8,128)(2,1)S(1)}, bf16[3,3,16,256]{3,2,1,0:T(8,128)(2,1)S(1)}, u32[]{:S(2)}, u32[]{:S(2)}) %collective-permute-start.2) | collective-permute-done | bytes 73760 | tf_op jit(solution)/shard_map/ppermute | solution.py:485
  13.9 1.7 %collective-permute-done.3 = bf16[3,3,16,256]{3,2,1,0:T(8,128)(2,1)S(1)} collective-permute-done((bf16[3,3,16,256]{3,2,1,0:T(8,128)(2,1)S(1)}, bf16[3,3,16,256]{3,2,1,0:T(8,128)(2,1)S(1)}, u32[]{:S(2)}, u32[]{:S(2)}) %collective-permute-start.3) | collective-permute-done | bytes 73760 | tf_op jit(solution)/shard_map/ppermute | solution.py:485
  15.6 0.6 pad_maximum_fusion.4
  16.2 6.4 %collective-permute-start.4 = (bf16[3,3,16,256]{3,2,1,0:T(8,128)(2,1)S(1)}, bf16[3,3,16,256]{3,2,1,0:T(8,128)(2,1)S(1)}, u32[]{:S(2)}, u32[]{:S(2)}) collective-permute-start(bf16[3,3,16,256]{3,2,1,0:T(8,128)(2,1)S(1)} %pad_maximum_fusion.3), channel_id=1, source_target_pairs={{0,7},{1,2},{2,1},{3,4},{4,3},{5,6},{6,5},{7,0},{8,15},{9,10},{10,... | collective-permute-start | bytes 221192 | tf_op jit(solution)/shard_map/ppermute | solution.py:485
  22.6 0.0 collective-permute-start.5
  22.6 3.4 %shard_map.185 = (f32[768,256]{1,0:T(8,128)}, f32[768,128]{1,0:T(8,128)}, f32[72,768]{1,0:T(8,128)}, f32[8,768]{1,0:T(8,128)}, f32[32,432]{1,0:T(8,128)}, /*index=5*/f32[72,256]{1,0:T(8,128)}) custom-call(f32[3,768]{1,0:T(4,128)} %disp, s32[768]{0:T(1024)} %mask.1, s32[768]{0:T(1024)} %slot.5, s32[32]{0:T(128)} %species.1, ...), custom_call_target="tpu_custom_call" | custom-call | tf_op jit(solution)/shard_map/pallas_call | solution.py:399
  26.1 0.0 collective-permute-done.4
  26.1 0.0 copy-start
  26.1 0.9 %collective-permute-done.5 = bf16[3,3,16,256]{3,2,1,0:T(8,128)(2,1)S(1)} collective-permute-done((bf16[3,3,16,256]{3,2,1,0:T(8,128)(2,1)S(1)}, bf16[3,3,16,256]{3,2,1,0:T(8,128)(2,1)S(1)}, u32[]{:S(2)}, u32[]{:S(2)}) %collective-permute-start.5) | collective-permute-done | bytes 73760 | tf_op jit(solution)/shard_map/ppermute | solution.py:485
  27.0 0.0 copy-start.1
  27.0 0.0 copy-done
  27.0 0.6 copy-done.1
  27.6 21.2 %shard_map.186 = (bf16[768,256]{1,0:T(8,128)(2,1)}, f32[1,32]{1,0:T(1,128)}, f32[8,768]{1,0:T(8,128)}, f32[8,144]{1,0:T(8,128)}, f32[8,144]{1,0:T(8,128)}, /*index=5*/f32[8,144]{1,0:T(8,128)}) custom-call(f32[768,256]{1,0:T(8,128)} %get-tuple-element.39.base, bf16[144,256]{1,0:T(8,128)(2,1)} %bitcast.31, bf16[144,256]{1,0:T(8,128)(2,1)} %bitcast.21, ...), custom_call_target="tpu_custom_call" | custom-call | tf_op jit(solution)/shard_map/pallas_call | solution.py:399
  48.8 0.0 copy-start.4
  48.8 0.1 collective-permute-start.6
  48.9 1.3 %collective-permute-start.7 = (f32[8,144]{1,0:T(8,128)}, f32[8,144]{1,0:T(8,128)S(1)}, u32[]{:S(2)}, u32[]{:S(2)}) collective-permute-start(f32[8,144]{1,0:T(8,128)} %get-tuple-element.52), channel_id=1, source_target_pairs={{0,32},{32,0},{64,96},{96,64},{1,33},{33,1},{65,97},{97,65},{2,34}... | collective-permute-start | bytes 13832 | tf_op jit(solution)/shard_map/ppermute | solution.py:485
  50.2 2.0 %collective-permute-done.6 = f32[8,144]{1,0:T(8,128)S(1)} collective-permute-done((f32[8,144]{1,0:T(8,128)}, f32[8,144]{1,0:T(8,128)S(1)}, u32[]{:S(2)}, u32[]{:S(2)}) %collective-permute-start.6) | collective-permute-done | bytes 4640 | tf_op jit(solution)/shard_map/ppermute | solution.py:485
  52.2 0.0 collective-permute-done.7
  52.2 0.0 copy-done.4
  52.2 0.1 fusion.7
  52.3 1.3 %collective-permute-start.8 = (f32[3,8,48]{2,1,0:T(8,128)S(1)}, f32[3,8,48]{2,1,0:T(8,128)S(1)}, u32[]{:S(2)}, u32[]{:S(2)}) collective-permute-start(f32[3,8,48]{2,1,0:T(8,128)S(1)} %get-tuple-element.80), channel_id=1, source_target_pairs={{0,24},{8,16},{16,8},{24,0},{1,25},{9,17},{17,9},{25,1},{2,26},{10... | collective-permute-start | bytes 13832 | tf_op jit(solution)/shard_map/ppermute | solution.py:485
  53.5 0.0 collective-permute-start.9
  53.5 3.7 %collective-permute-done.8 = f32[3,8,48]{2,1,0:T(8,128)S(1)} collective-permute-done((f32[3,8,48]{2,1,0:T(8,128)S(1)}, f32[3,8,48]{2,1,0:T(8,128)S(1)}, u32[]{:S(2)}, u32[]{:S(2)}) %collective-permute-start.8) | collective-permute-done | bytes 4640 | tf_op jit(solution)/shard_map/ppermute | solution.py:485
  57.2 0.0 collective-permute-done.9
  57.2 0.7 %fusion.6 = (f32[3,3,8,16]{3,2,1,0:T(8,128)S(1)}, f32[3,3,8,16]{3,2,1,0:T(8,128)}, f32[3,3,8,16]{3,2,1,0:T(8,128)S(1)}) fusion(f32[3,3,8,48]{3,2,1,0:T(8,128)S(1)} %pad_maximum_fusion.6), kind=kLoop, calls=%fused_computation.15 | loop fusion | bytes 27648 | tf_op jit(solution)/shard_map/slice | solution.py:544
  57.9 3.6 %collective-permute-start.10 = (f32[3,3,8,16]{3,2,1,0:T(8,128)S(1)}, f32[3,3,8,16]{3,2,1,0:T(8,128)S(1)}, u32[]{:S(2)}, u32[]{:S(2)}) collective-permute-start(f32[3,3,8,16]{3,2,1,0:T(8,128)S(1)} %get-tuple-element.56), channel_id=1, source_target_pairs={{0,7},{1,2},{2,1},{3,4},{4,3},{5,6},{6,5},{7,0},{8,15},{9,10},{10,... | collective-permute-start | bytes 13832 | tf_op jit(solution)/shard_map/ppermute | solution.py:485
  61.6 0.0 collective-permute-start.11
  61.6 2.3 %shard_map.187.partial = f32[8,32]{1,0:T(8,128)} custom-call(f32[8,768]{1,0:T(8,128)} %get-tuple-element.54.grad, s32[768]{0:T(1024)} %slot.5, f32[8,768]{1,0:T(8,128)} %get-tuple-element.45.rows), custom_call_target="tpu_custom_call" | custom-call | tf_op jit(solution)/shard_map/pallas_call | solution.py:399
  63.8 1.7 %collective-permute-done.10.r = f32[3,3,8,16]{3,2,1,0:T(8,128)S(1)} collective-permute-done((f32[3,3,8,16]{3,2,1,0:T(8,128)S(1)}, f32[3,3,8,16]{3,2,1,0:T(8,128)S(1)}, u32[]{:S(2)}, u32[]{:S(2)}) %collective-permute-start.10) | collective-permute-done | bytes 4640 | tf_op jit(solution)/shard_map/ppermute | solution.py:485
  65.5 0.0 copy-start.2
  65.5 0.0 collective-permute-done.11.l
  65.5 0.0 copy-start.3
  65.5 0.6 copy-done.2
  66.1 0.0 copy-done.3
  66.1 1.6 %shard_map.188 = f32[3,32]{1,0:T(4,128)} custom-call(f32[8,32]{1,0:T(8,128)} %shard_map.187.partial, f32[32,432]{1,0:T(8,128)} %get-tuple-element.55.mt, f32[3,3,8,16]{3,2,1,0:T(8,128)} %copy-done.2, f32[3,3,8,16]{3,2,1,0:T(8,128)} %get-tuple-element.57.m, f32[3,3,8,16]{3,2,1,0:T(8,128)} %copy-done.3), custom_call_target="tpu_custom_call" | custom-call | tf_op jit(solution)/shard_map/pallas_call | solution.py:399
  (11 shorter events, 0.1 us)
Async XLA Ops:
  3.6 4.4 %collective-permute-start = (bf16[144,256]{1,0:T(8,128)(2,1)}, bf16[144,256]{1,0:T(8,128)(2,1)S(1)}, u32[]{:S(2)}, u32[]{:S(2)}) collective-permute-start(bf16[144,256]{1,0:T(8,128)(2,1)} %get-tuple-element.31), channel_id=1, source_target_pairs={{0,96},{32,64},{64,32},{96,0},{1,97},{33,65},{65,33},{97,1},{2,98}... | collective-permute-start | bytes 221192 | tf_op jit(solution)/shard_map/ppermute | solution.py:485
  5.0 3.0 %collective-permute-start.1 = (bf16[144,256]{1,0:T(8,128)(2,1)}, bf16[144,256]{1,0:T(8,128)(2,1)S(1)}, u32[]{:S(2)}, u32[]{:S(2)}) collective-permute-start(bf16[144,256]{1,0:T(8,128)(2,1)} %get-tuple-element.33), channel_id=1, source_target_pairs={{0,32},{32,0},{64,96},{96,64},{1,33},{33,1},{65,97},{97,65},{2,34}... | collective-permute-start | bytes 221192 | tf_op jit(solution)/shard_map/ppermute | solution.py:485
  8.1 5.8 %collective-permute-start.2 = (bf16[3,3,16,256]{3,2,1,0:T(8,128)(2,1)S(1)}, bf16[3,3,16,256]{3,2,1,0:T(8,128)(2,1)S(1)}, u32[]{:S(2)}, u32[]{:S(2)}) collective-permute-start(bf16[3,3,16,256]{3,2,1,0:T(8,128)(2,1)S(1)} %get-tuple-element.34), channel_id=1, source_target_pairs={{0,24},{8,16},{16,8},{24,0},{1,25},{9,17},{17,9},{25,1},{2,26},{10... | collective-permute-start | bytes 221192 | tf_op jit(solution)/shard_map/ppermute | solution.py:485
  11.2 4.4 %collective-permute-start.3 = (bf16[3,3,16,256]{3,2,1,0:T(8,128)(2,1)S(1)}, bf16[3,3,16,256]{3,2,1,0:T(8,128)(2,1)S(1)}, u32[]{:S(2)}, u32[]{:S(2)}) collective-permute-start(bf16[3,3,16,256]{3,2,1,0:T(8,128)(2,1)S(1)} %pad_maximum_fusion.2), channel_id=1, source_target_pairs={{0,8},{8,0},{16,24},{24,16},{1,9},{9,1},{17,25},{25,17},{2,10},{10... | collective-permute-start | bytes 221192 | tf_op jit(solution)/shard_map/ppermute | solution.py:485
  16.2 9.8 %collective-permute-start.4 = (bf16[3,3,16,256]{3,2,1,0:T(8,128)(2,1)S(1)}, bf16[3,3,16,256]{3,2,1,0:T(8,128)(2,1)S(1)}, u32[]{:S(2)}, u32[]{:S(2)}) collective-permute-start(bf16[3,3,16,256]{3,2,1,0:T(8,128)(2,1)S(1)} %pad_maximum_fusion.3), channel_id=1, source_target_pairs={{0,7},{1,2},{2,1},{3,4},{4,3},{5,6},{6,5},{7,0},{8,15},{9,10},{10,... | collective-permute-start | bytes 221192 | tf_op jit(solution)/shard_map/ppermute | solution.py:485
  22.6 4.4 %collective-permute-start.5 = (bf16[3,3,16,256]{3,2,1,0:T(8,128)(2,1)S(1)}, bf16[3,3,16,256]{3,2,1,0:T(8,128)(2,1)S(1)}, u32[]{:S(2)}, u32[]{:S(2)}) collective-permute-start(bf16[3,3,16,256]{3,2,1,0:T(8,128)(2,1)S(1)} %pad_maximum_fusion.5), channel_id=1, source_target_pairs={{0,1},{1,0},{2,3},{3,2},{4,5},{5,4},{6,7},{7,6},{8,9},{9,8},{10,11... | collective-permute-start | bytes 221192 | tf_op jit(solution)/shard_map/ppermute | solution.py:485
  26.1 0.9 %copy-start = (bf16[3,3,16,256]{3,2,1,0:T(8,128)(2,1)}, bf16[3,3,16,256]{3,2,1,0:T(8,128)(2,1)S(1)}, u32[]{:S(2)}) copy-start(bf16[3,3,16,256]{3,2,1,0:T(8,128)(2,1)S(1)} %collective-permute-done.4) | copy-start | bytes 221188
  27.0 0.6 copy-start.1
  48.8 3.4 %copy-start.4 = (f32[8,144]{1,0:T(8,128)S(1)}, f32[8,144]{1,0:T(8,128)}, u32[]{:S(2)}) copy-start(f32[8,144]{1,0:T(8,128)} %get-tuple-element.51) | copy-start | bytes 13828
  48.8 3.4 %collective-permute-start.6 = (f32[8,144]{1,0:T(8,128)}, f32[8,144]{1,0:T(8,128)S(1)}, u32[]{:S(2)}, u32[]{:S(2)}) collective-permute-start(f32[8,144]{1,0:T(8,128)} %get-tuple-element.50), channel_id=1, source_target_pairs={{0,96},{32,64},{64,32},{96,0},{1,97},{33,65},{65,33},{97,1},{2,98}... | collective-permute-start | bytes 13832 | tf_op jit(solution)/shard_map/ppermute | solution.py:485
  48.9 3.3 %collective-permute-start.7 = (f32[8,144]{1,0:T(8,128)}, f32[8,144]{1,0:T(8,128)S(1)}, u32[]{:S(2)}, u32[]{:S(2)}) collective-permute-start(f32[8,144]{1,0:T(8,128)} %get-tuple-element.52), channel_id=1, source_target_pairs={{0,32},{32,0},{64,96},{96,64},{1,33},{33,1},{65,97},{97,65},{2,34}... | collective-permute-start | bytes 13832 | tf_op jit(solution)/shard_map/ppermute | solution.py:485
  52.3 4.9 %collective-permute-start.8 = (f32[3,8,48]{2,1,0:T(8,128)S(1)}, f32[3,8,48]{2,1,0:T(8,128)S(1)}, u32[]{:S(2)}, u32[]{:S(2)}) collective-permute-start(f32[3,8,48]{2,1,0:T(8,128)S(1)} %get-tuple-element.80), channel_id=1, source_target_pairs={{0,24},{8,16},{16,8},{24,0},{1,25},{9,17},{17,9},{25,1},{2,26},{10... | collective-permute-start | bytes 13832 | tf_op jit(solution)/shard_map/ppermute | solution.py:485
  53.5 3.7 %collective-permute-start.9 = (f32[3,8,48]{2,1,0:T(8,128)S(1)}, f32[3,8,48]{2,1,0:T(8,128)S(1)}, u32[]{:S(2)}, u32[]{:S(2)}) collective-permute-start(f32[3,8,48]{2,1,0:T(8,128)S(1)} %get-tuple-element.81), channel_id=1, source_target_pairs={{0,8},{8,0},{16,24},{24,16},{1,9},{9,1},{17,25},{25,17},{2,10},{10... | collective-permute-start | bytes 13832 | tf_op jit(solution)/shard_map/ppermute | solution.py:485
  57.9 7.6 %collective-permute-start.10 = (f32[3,3,8,16]{3,2,1,0:T(8,128)S(1)}, f32[3,3,8,16]{3,2,1,0:T(8,128)S(1)}, u32[]{:S(2)}, u32[]{:S(2)}) collective-permute-start(f32[3,3,8,16]{3,2,1,0:T(8,128)S(1)} %get-tuple-element.56), channel_id=1, source_target_pairs={{0,7},{1,2},{2,1},{3,4},{4,3},{5,6},{6,5},{7,0},{8,15},{9,10},{10,... | collective-permute-start | bytes 13832 | tf_op jit(solution)/shard_map/ppermute | solution.py:485
  61.6 4.0 %collective-permute-start.11 = (f32[3,3,8,16]{3,2,1,0:T(8,128)S(1)}, f32[3,3,8,16]{3,2,1,0:T(8,128)S(1)}, u32[]{:S(2)}, u32[]{:S(2)}) collective-permute-start(f32[3,3,8,16]{3,2,1,0:T(8,128)S(1)} %get-tuple-element.58), channel_id=1, source_target_pairs={{0,1},{1,0},{2,3},{3,2},{4,5},{5,4},{6,7},{7,6},{8,9},{9,8},{10,11... | collective-permute-start | bytes 13832 | tf_op jit(solution)/shard_map/ppermute | solution.py:485
  65.5 0.6 copy-start.2
  65.5 0.6 copy-start.3

commit v3 on v2

--- a/solution.py
+++ b/solution.py
@@ -107,8 +107,18 @@
     return jnp.where(far >= 0, place, -1).astype(F32)
 
 
+def lookup_kernel(slot, mask, where, far, pick, mt):
+    slot_row = slot[...].reshape(1, EDGE_DEV)
+    live = mask[...].reshape(1, EDGE_DEV).astype(F32)
+    hot = one_hot_lanes(as_column(remote_index(slot_row)), 3 * SIDE)
+    far[...] = hot
+    pick[...] = one_hot_lanes(where[:, 0:1], EDGE_DEV)
+    live_rows = atom_rows(ATOMS_DEV, F32) * as_column(live)
+    mt[...] = dot_tn(live_rows.astype(BF), hot)
+
+
 def geometry_kernel(
-    disp, mask, slot, species, message, table, w_vec, w_rbf, base, kwb, feat, rows, mt, wfeat
+    disp, mask, slot, species, message, table, w_vec, w_rbf, base, kwb, feat, rows, wfeat
 ):
     d = disp[...]
     dist = jnp.sqrt(jnp.sum(d * d, axis=0, keepdims=True) + 0.5)
@@ -144,9 +154,10 @@
     local = one_hot_lanes(as_column(slot_row.astype(F32)), EDGE_DEV)
     base[...] = dot_nn(left, right) + dot_nn(expand, centre) + dot_nn(local, message[...])
     kwb[...] = jnp.broadcast_to(as_column(kw), (EDGE_DEV, 128))
-    far = one_hot_lanes(as_column(remote_index(slot_row)), 3 * SIDE)
-    live_rows = expand.astype(F32) * as_column(live)
-    mt[...] = dot_tn(live_rows.astype(BF), far)
+
+
+def sigmoid(u):
+    return 0.5 * jnp.tanh(0.5 * u) + 0.5
 
 
 def rms_factor(x):
@@ -158,6 +169,7 @@
     return r * z - x * (r * r * r * inner)
 
 
+LIMIT = 40 * 2**20
 ROWS = 384
 GROUP = 16
 
@@ -167,7 +179,7 @@
     arr_r,
     arr_m,
     arr_l,
-    slot,
+    far,
     kwb,
     feat,
     rows,
@@ -178,9 +190,9 @@
     w_up,
     w_down,
     w_energy,
-    send,
+    pick,
     tokens,
-    energy,
+    reads,
     grad,
     low,
     mid,
@@ -217,9 +229,8 @@
             out = jnp.where(head_lanes[h], wide[h * NBR : (h + 1) * NBR], out)
         return out
 
-    far = one_hot_lanes(as_column(remote_index(slot[...].reshape(1, EDGE_DEV))), 3 * SIDE)
     arrived = jnp.concatenate([arr_r[...], arr_m[...], arr_l[...]], axis=0)
-    x = [base[b, :] + dot_nn(far[b], arrived) for b in blocks]
+    x = [base[b, :] + dot_nn(far[b, :], arrived) for b in blocks]
 
     for layer in range(2):
         for b, v in zip(blocks, x):
@@ -257,7 +268,7 @@
         up = [dot_nn(v, w_up[layer]) for v in normed]
         for b, v in zip(blocks, up):
             ups[layer, b, :] = v
-        hidden = [(u / (1.0 + jnp.exp(-u))).astype(BF) for u in up]
+        hidden = [(u * sigmoid(u)).astype(BF) for u in up]
         x = [v + dot_nn(h, w_down[layer]) for v, h in zip(x, hidden)]
 
     read = gains[4:5, :] * w_energy[...]
@@ -276,21 +287,14 @@
         dx.append((kw_col * r) * (read - scaled * total))
     readout = jnp.concatenate(readout, axis=1)[0:1]
     live = rows[2:3, :]
-    kw = rows[3:4, :]
-    parts = kw * readout
-    part_hi = parts.astype(BF).astype(F32)
-    stacked = jnp.concatenate(
-        [jnp.broadcast_to(part_hi, (8, edges)), jnp.broadcast_to(parts - part_hi, (8, edges))], axis=0
-    ).astype(BF)
-    summed = dot_nn(stacked, atom_rows(atoms))
-    energy[...] = summed[0:1] + summed[8:9]
+    reads[...] = readout
 
     for layer in (1, 0):
         dhid = [dot_nt(v.astype(BF), w_down[layer]) for v in dx]
         dup = []
         for b, dh in zip(blocks, dhid):
             u = ups[layer, b, :]
-            sig = 1.0 / (1.0 + jnp.exp(-u))
+            sig = sigmoid(u)
             dup.append((dh * (sig * (1.0 + u * (1.0 - sig)))).astype(BF))
         gain = gains[2 * layer + 1 : 2 * layer + 2, :]
         dnorm = [dot_nt(v, w_up[layer]) * gain for v in dup]
@@ -361,14 +365,20 @@
     grad[...] = g
     ghi = g.astype(BF).astype(F32)
     both = jnp.concatenate([ghi, g - ghi], axis=0).astype(BF)
-    out = dot_nt(both, one_hot_lanes(send[:, 0:1], edges))
+    out = dot_nt(both, pick[...])
     out = out[0:8] + out[8:16]
     low[...] = out[:, 0:SIDE]
     mid[...] = out[:, SIDE : 2 * SIDE]
     high[...] = out[:, 2 * SIDE : 3 * SIDE]
 
 
-def local_force_kernel(grad, slot, rows, out):
+def local_force_kernel(grad, slot, rows, reads, out, energy):
+    parts = rows[3:4, :] * reads[...]
+    hi = parts.astype(BF).astype(F32)
+    wide = jnp.broadcast_to(hi, (8, EDGE_DEV))
+    rest = jnp.broadcast_to(parts - hi, (8, EDGE_DEV))
+    summed = dot_nn(jnp.concatenate([wide, rest], axis=0).astype(BF), atom_rows(ATOMS_DEV))
+    energy[...] = summed[0:1] + summed[8:9]
     g = grad[...]
     ghi = g.astype(BF).astype(F32)
     both = jnp.concatenate([ghi, g - ghi], axis=0).astype(BF)
@@ -394,7 +404,7 @@
     forces[...] = (partial[...] - far[0:8] - far[8:16])[0:3]
 
 
-def vmem_call(kernel, outs, *args, scratch=(), limit=60 * 2**20):
+def vmem_call(kernel, outs, *args, scratch=(), limit=12 * 2**20):
     spec = pl.BlockSpec(memory_space=VMEM)
     return pl.pallas_call(
         kernel,
@@ -431,7 +441,6 @@
             shape((EDGE_DEV, 128)),
             shape((NFEAT, EDGE_DEV)),
             shape((8, EDGE_DEV)),
-            shape((ATOMS_DEV, 3 * SIDE)),
             shape((NFEAT, D)),
         ],
         disp,
@@ -445,15 +454,20 @@
     )
 
 
-def layers(base, arr, slot, kwb, feat, rows, wfeat, gains, w_qkv, w_out, w_up, w_down, w_energy, send):
+def lookups(slot, mask, where):
+    outs = [shape((EDGE_DEV, 3 * SIDE), BF), shape((3 * SIDE, EDGE_DEV), BF), shape((ATOMS_DEV, 3 * SIDE))]
+    return vmem_call(lookup_kernel, outs, slot, mask, where)
+
+
+def layers(base, arr, far, kwb, feat, rows, wfeat, gains, w_qkv, w_out, w_up, w_down, w_energy, pick):
     side = shape((8, SIDE))
     n = EDGE_DEV
     return vmem_call(
         layer_kernel,
-        [shape((n, D), BF), shape((1, ATOMS_DEV)), shape((8, n)), side, side, side],
+        [shape((n, D), BF), shape((1, n)), shape((8, n)), side, side, side],
         base,
         *arr,
-        slot,
+        far,
         kwb,
         feat,
         rows,
@@ -464,7 +478,8 @@
         w_up,
         w_down,
         w_energy,
-        send,
+        pick,
+        limit=LIMIT,
         scratch=[
             VMEM((4, n, D), F32),
             VMEM((2, n, 3 * D), F32),
@@ -508,20 +523,21 @@
     low, high = exchange(low, high, "gx")
     cells = [v.reshape(3, 3, SLOTS, D) for v in (low, mid, high)]
     low, mid, high = (jnp.stack([v[i] for v in cells]) for i in range(3))
-    low, mid, high = lax.optimization_barrier((low, mid, high))
+    low, high, where = lax.optimization_barrier((low, high, where))
     low, high = exchange(low, high, "gy")
+    far, pick, mt = lookups(reverse_slot, neighbour_mask, where)
     cells = (low, mid, high)
     low, mid, high = (jnp.stack([v[:, i] for v in cells], axis=1) for i in range(3))
-    low, mid, high, late = lax.optimization_barrier((low, mid, high, displacement))
+    low, high, late = lax.optimization_barrier((low, high, displacement))
     low, high = exchange(low, high, "gz")
-    base, kwb, feat, rows, mt, wfeat = geometry(
+    base, kwb, feat, rows, wfeat = geometry(
         late, neighbour_mask, reverse_slot, species, message, species_table, w_vec, w_rbf
     )
     arr = [v.reshape(SIDE, D) for v in (low, mid, high)]
-    tokens, energy, grad, low, mid, high = layers(
+    tokens, reads, grad, low, mid, high = layers(
         base,
         arr,
-        reverse_slot,
+        far,
         kwb,
         feat,
         rows,
@@ -532,7 +548,7 @@
         w_up,
         w_down,
         w_energy.reshape(1, D),
-        where,
+        pick,
     )
     low, high = exchange(low, high, "gx")
     cells = jnp.stack([low, mid, high])
@@ -542,10 +558,15 @@
     cells = jnp.stack([low, mid, high])
     cut = SLOTS
     low, mid, high = (cells[..., i * cut : (i + 1) * cut] for i in range(3))
-    low, mid, high, late = lax.optimization_barrier((low, mid, high, grad))
+    low, high, late = lax.optimization_barrier((low, high, grad))
     low, high = exchange(low, high, "gz")
-    partial = vmem_call(
-        local_force_kernel, shape((8, ATOMS_DEV)), late, reverse_slot, rows
+    partial, energy = vmem_call(
+        local_force_kernel,
+        [shape((8, ATOMS_DEV)), shape((1, ATOMS_DEV))],
+        late,
+        reverse_slot,
+        rows,
+        reads,
     )
     forces = vmem_call(force_kernel, shape((3, ATOMS_DEV)), partial, mt, low, mid, high)
     return (tokens, energy.reshape(ATOMS_DEV), forces)

time: 68.1 us -> 63.1 us (0.927)
  Pallas kernels: 31.5 us -> 23.4 us
  waiting for transfers between devices: 14 us -> 16.8 us
  local copies, waits for them, and re-layouts: 2.81 us -> 3.56 us
    pallas_call x5 -> x6, Pallas kernels: 31.5 us -> 23.4 us  [vmem_call(): pl.pallas_call(kernel, out_shape=outs, in_specs=[spec] * len(args), out_s...]
    ppermute x12, waiting for transfers between devices: 14 us -> 16.8 us  [exchange(): return (lax.ppermute(low, axis, outer), lax.ppermute(high, axis, inner))]
    unnamed x10 -> x34, local copies, waits for them, and re-layouts: 1.24 us -> 3.37 us
    slice x3, local copies, waits for them, and re-layouts: 0.79 us -> 0.02 us  [on_device(): low, mid, high = (jnp.stack([v[i] for v in cells]) for i in range(3))]
  transfers between devices with their start and end apart: 12 -> 12, of which waited for: 7 -> 8; matrix products, arithmetic and copies ran while one was open for 1% -> 0% of each run, Pallas kernels for 8% -> 5%
where the time goes in v3:
time: 63.1 us; the launch traced here: 62.9 us
  Pallas kernels  23.4 us (37%)
  starting transfers between devices  18.2 us (29%)
  waiting for transfers between devices  16.8 us (27%)
  local copies, waits for them, and re-layouts  3.56 us (6%)
  between operations  0.88 us (1%)
    pallas_call x6, Pallas kernels, vmem_call(): pl.pallas_call(kernel, out_shape=outs, in_specs=[spec] * len(args), out_s...  23.4 us
    ppermute x12, starting transfers between devices, exchange(): return (lax.ppermute(low, axis, outer), lax.ppermute(high, axis, inner))  18.2 us
    ppermute x12, waiting for transfers between devices, exchange(): return (lax.ppermute(low, axis, outer), lax.ppermute(high, axis, inner))  16.8 us
    unnamed x34, local copies, waits for them, and re-layouts  3.37 us
  transfers between devices with their start and end apart: 12, of which 8 were waited for; matrix products, arithmetic and copies ran while one was open for 0% of the time, Pallas kernels for 5%

profile of v3, /device:TPU:0, one launch (start us, length us, event | category | flops | bytes accessed | tf_op | source)
XLA Modules:
  0.0 62.9 jit_solution(11121862798962293378)
XLA Ops:
  0.6 0.0 copy-start.3
  0.6 1.0 %copy-done.3 = bf16[768,256]{1,0:T(8,128)(2,1)S(1)} copy-done((bf16[768,256]{1,0:T(8,128)(2,1)S(1)}, bf16[768,256]{1,0:T(8,128)(2,1)}, u32[]{:S(2)}) %copy-start.3) | copy-done | bytes 393240
  1.6 0.0 copy-start.5
  1.6 0.9 %copy-done.5 = bf16[256,256]{1,0:T(8,128)(2,1)S(1)} copy-done((bf16[256,256]{1,0:T(8,128)(2,1)S(1)}, bf16[256,256]{1,0:T(8,128)(2,1)}, u32[]{:S(2)}) %copy-start.5) | copy-done | bytes 131096
  2.5 0.0 copy-start.10
  2.5 0.7 %copy-done.10 = bf16[32,256]{1,0:T(8,128)(2,1)S(1)} copy-done((bf16[32,256]{1,0:T(8,128)(2,1)S(1)}, bf16[32,256]{1,0:T(8,128)(2,1)}, u32[]{:S(2)}) %copy-start.10) | copy-done | bytes 16408
  3.3 0.0 copy-start.14
  3.3 0.7 %copy-done.14 = s32[416]{0:T(512)S(1)} copy-done((s32[416]{0:T(512)S(1)}, s32[416]{0:T(512)}, u32[]{:S(2)}) %copy-start.14) | copy-done | bytes 1688
  3.9 1.1 %shard_map.184 = (bf16[768,256]{1,0:T(8,128)(2,1)S(1)}, bf16[144,256]{1,0:T(8,128)(2,1)S(1)}, bf16[144,256]{1,0:T(8,128)(2,1)S(1)}, bf16[144,256]{1,0:T(8,128)(2,1)S(1)}, f32[432,8]{1,0:T(8,128)S(1)}) custom-call(bf16[32,256]{1,0:T(8,128)(2,1)S(1)} %copy-done.10, bf16[256,256]{1,0:T(8,128)(2,1)S(1)} %copy-done.5, bf16[768,256]{1,0:T(8,128)(2,1)S(1)} %copy-done.3, ...), custom_call_target="tpu_custom_call" | custom-call | tf_op jit(solution)/shard_map/pallas_call | solution.py:409
  5.1 1.5 %collective-permute-start = (bf16[144,256]{1,0:T(8,128)(2,1)S(1)}, bf16[144,256]{1,0:T(8,128)(2,1)S(1)}, u32[]{:S(2)}, u32[]{:S(2)}) collective-permute-start(bf16[144,256]{1,0:T(8,128)(2,1)S(1)} %get-tuple-element.33), channel_id=1, source_target_pairs={{0,96},{32,64},{64,32},{96,0},{1,97},{33,65},{65,33},{97,1},{2,98}... | collective-permute-start | bytes 221192 | tf_op jit(solution)/shard_map/ppermute | solution.py:500
  6.6 0.7 %collective-permute-start.1 = (bf16[144,256]{1,0:T(8,128)(2,1)S(1)}, bf16[144,256]{1,0:T(8,128)(2,1)S(1)}, u32[]{:S(2)}, u32[]{:S(2)}) collective-permute-start(bf16[144,256]{1,0:T(8,128)(2,1)S(1)} %get-tuple-element.35), channel_id=1, source_target_pairs={{0,32},{32,0},{64,96},{96,64},{1,33},{33,1},{65,97},{97,65},{2,34}... | collective-permute-start | bytes 221192 | tf_op jit(solution)/shard_map/ppermute | solution.py:500
  7.3 2.0 %collective-permute-done = bf16[144,256]{1,0:T(8,128)(2,1)S(1)} collective-permute-done((bf16[144,256]{1,0:T(8,128)(2,1)S(1)}, bf16[144,256]{1,0:T(8,128)(2,1)S(1)}, u32[]{:S(2)}, u32[]{:S(2)}) %collective-permute-start) | collective-permute-done | bytes 73760 | tf_op jit(solution)/shard_map/ppermute | solution.py:500
  9.3 0.0 collective-permute-done.1
  9.3 0.0 copy-start.6
  9.3 0.0 copy-start.11
  9.3 0.0 copy-start.13
  9.3 0.0 copy-start.16
  9.3 0.0 copy-start.12
  9.4 0.0 copy-start.8
  9.4 0.0 copy-start.9
  9.4 0.0 copy-start.7
  9.4 0.0 copy-start.4
  9.4 0.0 copy-start.15
  9.4 3.3 %collective-permute-start.2 = (bf16[3,3,16,256]{3,2,1,0:T(8,128)(2,1)S(1)}, bf16[3,3,16,256]{3,2,1,0:T(8,128)(2,1)S(1)}, u32[]{:S(2)}, u32[]{:S(2)}) collective-permute-start(bf16[3,3,16,256]{3,2,1,0:T(8,128)(2,1)S(1)} %get-tuple-element.37), channel_id=1, source_target_pairs={{0,24},{8,16},{16,8},{24,0},{1,25},{9,17},{17,9},{25,1},{2,26},{10... | collective-permute-start | bytes 221192 | tf_op jit(solution)/shard_map/ppermute | solution.py:500
  12.7 0.0 copy-start
  12.7 0.2 collective-permute-start.3
  13.0 0.0 copy-done.8
  13.0 0.0 copy-done.9
  13.0 1.0 %shard_map.186 = (bf16[768,432]{1,0:T(8,128)(2,1)S(1)}, bf16[432,768]{1,0:T(8,128)(2,1)S(1)}, f32[32,432]{1,0:T(8,128)S(1)}) custom-call(s32[768]{0:T(1024)S(1)} %copy-done.8, s32[768]{0:T(1024)S(1)} %copy-done.9, f32[432,8]{1,0:T(8,128)S(1)} %get-tuple-element.44.where), custom_call_target="tpu_custom_call" | custom-call | tf_op jit(solution)/shard_map/pallas_call | solution.py:409
  13.9 1.4 %collective-permute-done.2 = bf16[3,3,16,256]{3,2,1,0:T(8,128)(2,1)S(1)} collective-permute-done((bf16[3,3,16,256]{3,2,1,0:T(8,128)(2,1)S(1)}, bf16[3,3,16,256]{3,2,1,0:T(8,128)(2,1)S(1)}, u32[]{:S(2)}, u32[]{:S(2)}) %collective-permute-start.2) | collective-permute-done | bytes 73760 | tf_op jit(solution)/shard_map/ppermute | solution.py:500
  15.4 1.8 %collective-permute-done.3 = bf16[3,3,16,256]{3,2,1,0:T(8,128)(2,1)S(1)} collective-permute-done((bf16[3,3,16,256]{3,2,1,0:T(8,128)(2,1)S(1)}, bf16[3,3,16,256]{3,2,1,0:T(8,128)(2,1)S(1)}, u32[]{:S(2)}, u32[]{:S(2)}) %collective-permute-start.3) | collective-permute-done | bytes 73760 | tf_op jit(solution)/shard_map/ppermute | solution.py:500
  17.2 6.4 %collective-permute-start.4 = (bf16[3,3,16,256]{3,2,1,0:T(8,128)(2,1)S(1)}, bf16[3,3,16,256]{3,2,1,0:T(8,128)(2,1)S(1)}, u32[]{:S(2)}, u32[]{:S(2)}) collective-permute-start(bf16[3,3,16,256]{3,2,1,0:T(8,128)(2,1)S(1)} %pad_maximum_fusion.3), channel_id=1, source_target_pairs={{0,7},{1,2},{2,1},{3,4},{4,3},{5,6},{6,5},{7,0},{8,15},{9,10},{10,... | collective-permute-start | bytes 221192 | tf_op jit(solution)/shard_map/ppermute | solution.py:500
  23.6 0.0 collective-permute-start.5
  23.6 0.0 copy-done.6
  23.6 0.0 copy-done.11
  23.6 0.0 copy-done.13
  23.6 0.0 copy-done.16
  23.6 0.0 copy-done.7
  23.6 1.0 %shard_map.185 = (f32[768,256]{1,0:T(8,128)S(1)}, f32[768,128]{1,0:T(8,128)S(1)}, f32[72,768]{1,0:T(8,128)S(1)}, f32[8,768]{1,0:T(8,128)S(1)}, f32[72,256]{1,0:T(8,128)S(1)}) custom-call(f32[3,768]{1,0:T(4,128)S(1)} %copy-done.11, s32[768]{0:T(1024)S(1)} %copy-done.9, s32[768]{0:T(1024)S(1)} %copy-done.8, s32[32]{0:T(128)S(1)} %copy-done.16, ...), custom_call_target="tpu_custom_call" | custom-call | tf_op jit(solution)/shard_map/pallas_call | solution.py:409
  24.7 1.2 %collective-permute-done.4 = bf16[3,3,16,256]{3,2,1,0:T(8,128)(2,1)S(1)} collective-permute-done((bf16[3,3,16,256]{3,2,1,0:T(8,128)(2,1)S(1)}, bf16[3,3,16,256]{3,2,1,0:T(8,128)(2,1)S(1)}, u32[]{:S(2)}, u32[]{:S(2)}) %collective-permute-start.4) | collective-permute-done | bytes 73760 | tf_op jit(solution)/shard_map/ppermute | solution.py:500
  25.9 2.0 %collective-permute-done.5 = bf16[3,3,16,256]{3,2,1,0:T(8,128)(2,1)S(1)} collective-permute-done((bf16[3,3,16,256]{3,2,1,0:T(8,128)(2,1)S(1)}, bf16[3,3,16,256]{3,2,1,0:T(8,128)(2,1)S(1)}, u32[]{:S(2)}, u32[]{:S(2)}) %collective-permute-start.5) | collective-permute-done | bytes 73760 | tf_op jit(solution)/shard_map/ppermute | solution.py:500
  27.9 0.0 copy-done.12
  27.9 0.0 copy-done.4
  27.9 0.0 copy-done.15
  28.0 0.0 copy-done.2
  28.0 0.0 copy-done
  28.0 0.0 copy-done.1
  28.0 18.2 %shard_map.187 = (bf16[768,256]{1,0:T(8,128)(2,1)}, f32[1,768]{1,0:T(1,128)S(1)}, f32[8,768]{1,0:T(8,128)S(1)}, f32[8,144]{1,0:T(8,128)S(1)}, f32[8,144]{1,0:T(8,128)S(1)}, /*index=5*/f32[8,144]{1,0:T(8,128)S(1)}) custom-call(f32[768,256]{1,0:T(8,128)S(1)} %get-tuple-element.41.base, bf16[144,256]{1,0:T(8,128)(2,1)S(1)} %bitcast.22, ...), custom_call_target="tpu_custom_call" | custom-call | tf_op jit(solution)/shard_map/pallas_call | solution.py:409
  46.2 0.0 collective-permute-start.6
  46.2 1.3 %collective-permute-start.7 = (f32[8,144]{1,0:T(8,128)S(1)}, f32[8,144]{1,0:T(8,128)S(1)}, u32[]{:S(2)}, u32[]{:S(2)}) collective-permute-start(f32[8,144]{1,0:T(8,128)S(1)} %get-tuple-element.54), channel_id=1, source_target_pairs={{0,32},{32,0},{64,96},{96,64},{1,33},{33,1},{65,97},{97,65},{2,34}... | collective-permute-start | bytes 13832 | tf_op jit(solution)/shard_map/ppermute | solution.py:500
  47.5 1.8 %collective-permute-done.6 = f32[8,144]{1,0:T(8,128)S(1)} collective-permute-done((f32[8,144]{1,0:T(8,128)S(1)}, f32[8,144]{1,0:T(8,128)S(1)}, u32[]{:S(2)}, u32[]{:S(2)}) %collective-permute-start.6) | collective-permute-done | bytes 4640 | tf_op jit(solution)/shard_map/ppermute | solution.py:500
  49.3 0.0 collective-permute-done.7
  49.3 0.1 fusion.7
  49.4 1.1 %collective-permute-start.8 = (f32[3,8,48]{2,1,0:T(8,128)S(1)}, f32[3,8,48]{2,1,0:T(8,128)S(1)}, u32[]{:S(2)}, u32[]{:S(2)}) collective-permute-start(f32[3,8,48]{2,1,0:T(8,128)S(1)} %get-tuple-element.84), channel_id=1, source_target_pairs={{0,24},{8,16},{16,8},{24,0},{1,25},{9,17},{17,9},{25,1},{2,26},{10... | collective-permute-start | bytes 13832 | tf_op jit(solution)/shard_map/ppermute | solution.py:500
  50.5 0.0 collective-permute-start.9
  50.5 3.8 %collective-permute-done.8 = f32[3,8,48]{2,1,0:T(8,128)S(1)} collective-permute-done((f32[3,8,48]{2,1,0:T(8,128)S(1)}, f32[3,8,48]{2,1,0:T(8,128)S(1)}, u32[]{:S(2)}, u32[]{:S(2)}) %collective-permute-start.8) | collective-permute-done | bytes 4640 | tf_op jit(solution)/shard_map/ppermute | solution.py:500
  54.3 0.0 collective-permute-done.9
  54.3 0.1 fusion.6
  54.4 3.7 %collective-permute-start.10 = (f32[3,3,8,16]{3,2,1,0:T(8,128)S(1)}, f32[3,3,8,16]{3,2,1,0:T(8,128)S(1)}, u32[]{:S(2)}, u32[]{:S(2)}) collective-permute-start(f32[3,3,8,16]{3,2,1,0:T(8,128)S(1)} %get-tuple-element.61), channel_id=1, source_target_pairs={{0,7},{1,2},{2,1},{3,4},{4,3},{5,6},{6,5},{7,0},{8,15},{9,10},{10,... | collective-permute-start | bytes 13832 | tf_op jit(solution)/shard_map/ppermute | solution.py:500
  58.1 0.0 collective-permute-start.11
  58.1 1.2 %shard_map.188 = (f32[8,32]{1,0:T(8,128)S(1)}, f32[1,32]{1,0:T(1,128)}) custom-call(f32[8,768]{1,0:T(8,128)S(1)} %get-tuple-element.56.grad, s32[768]{0:T(1024)S(1)} %copy-done.8, f32[8,768]{1,0:T(8,128)S(1)} %get-tuple-element.48.rows, f32[1,768]{1,0:T(1,128)S(1)} %get-tuple-element.57.reads), custom_call_target="tpu_custom_call" | custom-call | tf_op jit(solution)/shard_map/pallas_call | solution.py:409
  59.3 2.7 %collective-permute-done.10.r = f32[3,3,8,16]{3,2,1,0:T(8,128)S(1)} collective-permute-done((f32[3,3,8,16]{3,2,1,0:T(8,128)S(1)}, f32[3,3,8,16]{3,2,1,0:T(8,128)S(1)}, u32[]{:S(2)}, u32[]{:S(2)}) %collective-permute-start.10) | collective-permute-done | bytes 4640 | tf_op jit(solution)/shard_map/ppermute | solution.py:500
  62.1 0.0 collective-permute-done.11.l
  62.1 0.8 %shard_map.189 = f32[3,32]{1,0:T(4,128)} custom-call(f32[8,32]{1,0:T(8,128)S(1)} %get-tuple-element.59.partial, f32[32,432]{1,0:T(8,128)S(1)} %get-tuple-element.60.mt, f32[3,3,8,16]{3,2,1,0:T(8,128)S(1)} %collective-permute-done.10.r, f32[3,3,8,16]{3,2,1,0:T(8,128)S(1)} %get-tuple-element.81.m, f32[3,3,8,16]{3,2,1,0:T(8,128)S(1)} %collective-permute-done.11.l), custom_call_target="tpu_custom_call" | custom-call | tf_op jit(solution)/shard_map/pallas_call | solution.py:409
  (15 shorter events, 0.1 us)
Async XLA Ops:
  0.6 1.0 %copy-start.3 = (bf16[768,256]{1,0:T(8,128)(2,1)S(1)}, bf16[768,256]{1,0:T(8,128)(2,1)}, u32[]{:S(2)}) copy-start(bf16[768,256]{1,0:T(8,128)(2,1)} %prev.1) | copy-start | bytes 1179652
  1.6 0.9 %copy-start.5 = (bf16[256,256]{1,0:T(8,128)(2,1)S(1)}, bf16[256,256]{1,0:T(8,128)(2,1)}, u32[]{:S(2)}) copy-start(bf16[256,256]{1,0:T(8,128)(2,1)} %w_neigh.1) | copy-start | bytes 393220
  2.5 0.7 %copy-start.10 = (bf16[32,256]{1,0:T(8,128)(2,1)S(1)}, bf16[32,256]{1,0:T(8,128)(2,1)}, u32[]{:S(2)}) copy-start(bf16[32,256]{1,0:T(8,128)(2,1)} %state.1) | copy-start | bytes 49156
  3.3 0.7 %copy-start.14 = (s32[416]{0:T(512)S(1)}, s32[416]{0:T(512)}, u32[]{:S(2)}) copy-start(s32[416]{0:T(512)} %send.1) | copy-start | bytes 4996
  5.1 4.2 %collective-permute-start = (bf16[144,256]{1,0:T(8,128)(2,1)S(1)}, bf16[144,256]{1,0:T(8,128)(2,1)S(1)}, u32[]{:S(2)}, u32[]{:S(2)}) collective-permute-start(bf16[144,256]{1,0:T(8,128)(2,1)S(1)} %get-tuple-element.33), channel_id=1, source_target_pairs={{0,96},{32,64},{64,32},{96,0},{1,97},{33,65},{65,33},{97,1},{2,98}... | collective-permute-start | bytes 221192 | tf_op jit(solution)/shard_map/ppermute | solution.py:500
  6.6 2.7 %collective-permute-start.1 = (bf16[144,256]{1,0:T(8,128)(2,1)S(1)}, bf16[144,256]{1,0:T(8,128)(2,1)S(1)}, u32[]{:S(2)}, u32[]{:S(2)}) collective-permute-start(bf16[144,256]{1,0:T(8,128)(2,1)S(1)} %get-tuple-element.35), channel_id=1, source_target_pairs={{0,32},{32,0},{64,96},{96,64},{1,33},{33,1},{65,97},{97,65},{2,34}... | collective-permute-start | bytes 221192 | tf_op jit(solution)/shard_map/ppermute | solution.py:500
  9.3 14.3 %copy-start.6 = (f32[64,256]{1,0:T(8,128)S(1)}, f32[64,256]{1,0:T(8,128)}, u32[]{:S(2)}) copy-start(f32[64,256]{1,0:T(8,128)} %w_rbf.1) | copy-start | bytes 196612
  9.3 14.3 %copy-start.11 = (f32[3,768]{1,0:T(4,128)S(1)}, f32[3,768]{1,0:T(4,128)}, u32[]{:S(2)}) copy-start(f32[3,768]{1,0:T(4,128)} %disp) | copy-start | bytes 27652
  9.3 14.3 %copy-start.13 = (f32[3,256]{1,0:T(4,128)S(1)}, f32[3,256]{1,0:T(4,128)}, u32[]{:S(2)}) copy-start(f32[3,256]{1,0:T(4,128)} %w_vec.1) | copy-start | bytes 9220
  9.3 14.3 %copy-start.16 = (s32[32]{0:T(128)S(1)}, s32[32]{0:T(128)}, u32[]{:S(2)}) copy-start(s32[32]{0:T(128)} %species.1) | copy-start | bytes 388
  9.3 18.6 %copy-start.12 = (f32[5,256]{1,0:T(8,128)S(1)}, f32[5,256]{1,0:T(8,128)}, u32[]{:S(2)}) copy-start(f32[5,256]{1,0:T(8,128)} %gains.1) | copy-start | bytes 15364
  9.4 3.6 %copy-start.8 = (s32[768]{0:T(1024)S(1)}, s32[768]{0:T(1024)}, u32[]{:S(2)}) copy-start(s32[768]{0:T(1024)} %slot.5) | copy-start | bytes 9220
  9.4 3.6 %copy-start.9 = (s32[768]{0:T(1024)S(1)}, s32[768]{0:T(1024)}, u32[]{:S(2)}) copy-start(s32[768]{0:T(1024)} %mask.3) | copy-start | bytes 9220
  9.4 14.2 %copy-start.7 = (bf16[85,256]{1,0:T(8,128)(2,1)S(1)}, bf16[85,256]{1,0:T(8,128)(2,1)}, u32[]{:S(2)}) copy-start(bf16[85,256]{1,0:T(8,128)(2,1)} %table.1) | copy-start | bytes 130564
  9.4 18.6 %copy-start.4 = (bf16[2,256,256]{2,1,0:T(8,128)(2,1)S(1)}, bf16[2,256,256]{2,1,0:T(8,128)(2,1)}, u32[]{:S(2)}) copy-start(bf16[2,256,256]{2,1,0:T(8,128)(2,1)} %w_out.1) | copy-start | bytes 786436
  9.4 18.5 %copy-start.15 = (f32[256]{0:T(256)S(1)}, f32[256]{0:T(256)}, u32[]{:S(2)}) copy-start(f32[256]{0:T(256)} %param.33) | copy-start | bytes 3076
  9.4 5.9 %collective-permute-start.2 = (bf16[3,3,16,256]{3,2,1,0:T(8,128)(2,1)S(1)}, bf16[3,3,16,256]{3,2,1,0:T(8,128)(2,1)S(1)}, u32[]{:S(2)}, u32[]{:S(2)}) collective-permute-start(bf16[3,3,16,256]{3,2,1,0:T(8,128)(2,1)S(1)} %get-tuple-element.37), channel_id=1, source_target_pairs={{0,24},{8,16},{16,8},{24,0},{1,25},{9,17},{17,9},{25,1},{2,26},{10... | collective-permute-start | bytes 221192 | tf_op jit(solution)/shard_map/ppermute | solution.py:500
  12.7 15.3 %copy-start.2 = (bf16[2,512,256]{2,1,0:T(8,128)(2,1)S(1)}, bf16[2,512,256]{2,1,0:T(8,128)(2,1)}, u32[]{:S(2)}) copy-start(bf16[2,512,256]{2,1,0:T(8,128)(2,1)} %w_down.1) | copy-start | bytes 1572868
  12.7 15.2 %copy-start = (bf16[2,256,768]{2,1,0:T(8,128)(2,1)S(1)}, bf16[2,256,768]{2,1,0:T(8,128)(2,1)}, u32[]{:S(2)}) copy-start(bf16[2,256,768]{2,1,0:T(8,128)(2,1)} %w_qkv.1) | copy-start | bytes 2359300
  12.7 4.4 %collective-permute-start.3 = (bf16[3,3,16,256]{3,2,1,0:T(8,128)(2,1)S(1)}, bf16[3,3,16,256]{3,2,1,0:T(8,128)(2,1)S(1)}, u32[]{:S(2)}, u32[]{:S(2)}) collective-permute-start(bf16[3,3,16,256]{3,2,1,0:T(8,128)(2,1)S(1)} %get-tuple-element.38), channel_id=1, source_target_pairs={{0,8},{8,0},{16,24},{24,16},{1,9},{9,1},{17,25},{25,17},{2,10},{10... | collective-permute-start | bytes 221192 | tf_op jit(solution)/shard_map/ppermute | solution.py:500
  17.2 10.8 %copy-start.1 = (bf16[2,256,512]{2,1,0:T(8,128)(2,1)S(1)}, bf16[2,256,512]{2,1,0:T(8,128)(2,1)}, u32[]{:S(2)}) copy-start(bf16[2,256,512]{2,1,0:T(8,128)(2,1)} %w_up.1) | copy-start | bytes 1572868
  17.2 8.7 %collective-permute-start.4 = (bf16[3,3,16,256]{3,2,1,0:T(8,128)(2,1)S(1)}, bf16[3,3,16,256]{3,2,1,0:T(8,128)(2,1)S(1)}, u32[]{:S(2)}, u32[]{:S(2)}) collective-permute-start(bf16[3,3,16,256]{3,2,1,0:T(8,128)(2,1)S(1)} %pad_maximum_fusion.3), channel_id=1, source_target_pairs={{0,7},{1,2},{2,1},{3,4},{4,3},{5,6},{6,5},{7,0},{8,15},{9,10},{10,... | collective-permute-start | bytes 221192 | tf_op jit(solution)/shard_map/ppermute | solution.py:500
  23.6 4.4 %collective-permute-start.5 = (bf16[3,3,16,256]{3,2,1,0:T(8,128)(2,1)S(1)}, bf16[3,3,16,256]{3,2,1,0:T(8,128)(2,1)S(1)}, u32[]{:S(2)}, u32[]{:S(2)}) collective-permute-start(bf16[3,3,16,256]{3,2,1,0:T(8,128)(2,1)S(1)} %pad_maximum_fusion.4), channel_id=1, source_target_pairs={{0,1},{1,0},{2,3},{3,2},{4,5},{5,4},{6,7},{7,6},{8,9},{9,8},{10,11... | collective-permute-start | bytes 221192 | tf_op jit(solution)/shard_map/ppermute | solution.py:500
  46.2 3.1 %collective-permute-start.6 = (f32[8,144]{1,0:T(8,128)S(1)}, f32[8,144]{1,0:T(8,128)S(1)}, u32[]{:S(2)}, u32[]{:S(2)}) collective-permute-start(f32[8,144]{1,0:T(8,128)S(1)} %get-tuple-element.52), channel_id=1, source_target_pairs={{0,96},{32,64},{64,32},{96,0},{1,97},{33,65},{65,33},{97,1},{2,98}... | collective-permute-start | bytes 13832 | tf_op jit(solution)/shard_map/ppermute | solution.py:500
  46.2 3.1 %collective-permute-start.7 = (f32[8,144]{1,0:T(8,128)S(1)}, f32[8,144]{1,0:T(8,128)S(1)}, u32[]{:S(2)}, u32[]{:S(2)}) collective-permute-start(f32[8,144]{1,0:T(8,128)S(1)} %get-tuple-element.54), channel_id=1, source_target_pairs={{0,32},{32,0},{64,96},{96,64},{1,33},{33,1},{65,97},{97,65},{2,34}... | collective-permute-start | bytes 13832 | tf_op jit(solution)/shard_map/ppermute | solution.py:500
  49.4 4.9 %collective-permute-start.8 = (f32[3,8,48]{2,1,0:T(8,128)S(1)}, f32[3,8,48]{2,1,0:T(8,128)S(1)}, u32[]{:S(2)}, u32[]{:S(2)}) collective-permute-start(f32[3,8,48]{2,1,0:T(8,128)S(1)} %get-tuple-element.84), channel_id=1, source_target_pairs={{0,24},{8,16},{16,8},{24,0},{1,25},{9,17},{17,9},{25,1},{2,26},{10... | collective-permute-start | bytes 13832 | tf_op jit(solution)/shard_map/ppermute | solution.py:500
  50.5 3.8 %collective-permute-start.9 = (f32[3,8,48]{2,1,0:T(8,128)S(1)}, f32[3,8,48]{2,1,0:T(8,128)S(1)}, u32[]{:S(2)}, u32[]{:S(2)}) collective-permute-start(f32[3,8,48]{2,1,0:T(8,128)S(1)} %get-tuple-element.85), channel_id=1, source_target_pairs={{0,8},{8,0},{16,24},{24,16},{1,9},{9,1},{17,25},{25,17},{2,10},{10... | collective-permute-start | bytes 13832 | tf_op jit(solution)/shard_map/ppermute | solution.py:500
  54.4 7.7 %collective-permute-start.10 = (f32[3,3,8,16]{3,2,1,0:T(8,128)S(1)}, f32[3,3,8,16]{3,2,1,0:T(8,128)S(1)}, u32[]{:S(2)}, u32[]{:S(2)}) collective-permute-start(f32[3,3,8,16]{3,2,1,0:T(8,128)S(1)} %get-tuple-element.61), channel_id=1, source_target_pairs={{0,7},{1,2},{2,1},{3,4},{4,3},{5,6},{6,5},{7,0},{8,15},{9,10},{10,... | collective-permute-start | bytes 13832 | tf_op jit(solution)/shard_map/ppermute | solution.py:500
  58.1 4.0 %collective-permute-start.11 = (f32[3,3,8,16]{3,2,1,0:T(8,128)S(1)}, f32[3,3,8,16]{3,2,1,0:T(8,128)S(1)}, u32[]{:S(2)}, u32[]{:S(2)}) collective-permute-start(f32[3,3,8,16]{3,2,1,0:T(8,128)S(1)} %get-tuple-element.62), channel_id=1, source_target_pairs={{0,1},{1,0},{2,3},{3,2},{4,5},{5,4},{6,7},{7,6},{8,9},{9,8},{10,11... | collective-permute-start | bytes 13832 | tf_op jit(solution)/shard_map/ppermute | solution.py:500

commit v4 on v3

--- a/solution.py
+++ b/solution.py
@@ -65,14 +65,33 @@
     return jnp.where(lanes == column, 1.0, 0.0).astype(BF)
 
 
-def message_kernel(state, w_neigh, prev, send, message, low, mid, high, where, order):
-    projected = dot_nn(state[...], w_neigh[...])
+def message_kernel(
+    state_far,
+    w_far,
+    prev_far,
+    send_far,
+    message,
+    low,
+    mid,
+    high,
+    where,
+    order,
+    send,
+    state,
+    w_neigh,
+    prev,
+    sems,
+):
+    moves = [
+        pltpu.make_async_copy(src, dst, sems.at[i])
+        for i, (src, dst) in enumerate(
+            ((send_far, send), (state_far, state), (w_far, w_neigh), (prev_far, prev))
+        )
+    ]
+    for move in moves:
+        move.start()
     expand = atom_rows(ATOMS_DEV)
-    hi, lo = split2(projected)
-    rest = (projected - hi.astype(F32) - lo.astype(F32)).astype(BF)
-    wide = dot_nn(expand, hi) + dot_nn(expand, lo) + dot_nn(expand, rest)
-    out = (prev[...].astype(F32) + wide).astype(BF)
-    message[...] = out
+    moves[0].wait()
     count = 26 * SLOTS
     sent = jnp.broadcast_to(send[...].reshape(1, count).astype(F32), (8, count)).T
     flips = [lax.axis_index(axis) & 1 for axis in AXES]
@@ -88,7 +107,17 @@
             order[rows, :] = sent[start : start + SLOTS]
     column = order[...]
     where[...] = column
-    payload = dot_nn(one_hot_lanes(column[:, 0:1], EDGE_DEV), out).astype(BF)
+    pick = one_hot_lanes(column[:, 0:1], EDGE_DEV)
+    moves[1].wait()
+    moves[2].wait()
+    projected = dot_nn(state[...], w_neigh[...])
+    hi, lo = split2(projected)
+    rest = (projected - hi.astype(F32) - lo.astype(F32)).astype(BF)
+    wide = dot_nn(expand, hi) + dot_nn(expand, lo) + dot_nn(expand, rest)
+    moves[3].wait()
+    out = (prev[...].astype(F32) + wide).astype(BF)
+    message[...] = out
+    payload = dot_nn(pick, out).astype(BF)
     low[...] = payload[0:SIDE]
     mid[...] = payload[SIDE : 2 * SIDE]
     high[...] = payload[2 * SIDE : 3 * SIDE]
@@ -169,9 +198,174 @@
     return r * z - x * (r * r * r * inner)
 
 
-LIMIT = 40 * 2**20
-ROWS = 384
-GROUP = 16
+LIMIT = 36 * 2**20
+INNER = 4 * NBR
+OUTER = EDGE_DEV - INNER
+
+
+def block_list(edges, parts):
+    step = edges // parts
+    return [slice(i, i + step) for i in range(0, edges, step)]
+
+
+def shifted(block, offset):
+    return slice(block.start + offset, block.stop + offset)
+
+
+def atom_spans(edges, offset=0):
+    return [slice(i + offset, i + offset + NBR) for i in range(0, edges, NBR)]
+
+
+def spread(x):
+    tall = jnp.concatenate([x, jnp.zeros((32 - NBR, 128), F32)], axis=0).astype(BF)
+    head = iota((32, 128), 1) >> 5
+    return jnp.concatenate(
+        [tall * jnp.where(head == h, 1.0, 0.0).astype(BF) for h in range(4)], axis=0
+    )
+
+
+def gather_heads(wide):
+    head = iota((1, 128), 1) >> 5
+    out = jnp.where(head == 0, wide[0:NBR], 0.0)
+    for h in range(1, 4):
+        out = jnp.where(head == h, wide[32 * h : 32 * h + NBR], out)
+    return out
+
+
+def forward(x, blocks, offset, kwb, gains, w_qkv, w_out, w_up, w_down, xs, qkv, ups, probs, slope, att):
+    edges = blocks[-1].stop
+    score_scale = 1.0 / (math.sqrt(D // HEADS) * score_cap)
+    slope_scale = 1.0 / math.sqrt(D // HEADS)
+    at = [(s, 128 * g) for s in atom_spans(edges) for g in range(2)]
+    for layer in range(2):
+        for b, v in zip(blocks, x):
+            xs[2 * layer, b, :] = v
+        gain = gains[2 * layer : 2 * layer + 1, :]
+        normed = [(v * rms_factor(v) * gain).astype(BF) for v in x]
+        for b, v in zip(blocks, normed):
+            qkv[layer, b, :] = dot_nn(v, w_qkv[layer])
+        q = [spread(qkv[layer, s, c : c + 128]) for s, c in at]
+        k = [qkv[layer, s, D + c : D + c + 128].astype(BF) for s, c in at]
+        v = [qkv[layer, s, 2 * D + c : 2 * D + c + 128].astype(BF) for s, c in at]
+        t = [dot_nt(kk, qq) for kk, qq in zip(k, q)]
+        t = [jnp.tanh(tt * score_scale) for tt in t]
+        e = [kwb[shifted(s, offset), :] * jnp.exp(score_cap * tt) for (s, c), tt in zip(at, t)]
+        p = [ee * (1.0 / jnp.sum(ee, axis=0, keepdims=True)) for ee in e]
+        o = [dot_tn(pp.astype(BF), vv) for pp, vv in zip(p, v)]
+        o = [gather_heads(oo) for oo in o]
+        for i, (s, c) in enumerate(at):
+            probs[layer, s, c : c + 128] = p[i]
+            slope[layer, s, c : c + 128] = (1.0 - t[i] * t[i]) * slope_scale
+            att[s, c : c + 128] = o[i]
+        x = [xs[2 * layer, b, :] + dot_nn(att[b, :].astype(BF), w_out[layer]) for b in blocks]
+        for b, v in zip(blocks, x):
+            xs[2 * layer + 1, b, :] = v
+        gain = gains[2 * layer + 1 : 2 * layer + 2, :]
+        normed = [(v * rms_factor(v) * gain).astype(BF) for v in x]
+        up = [dot_nn(v, w_up[layer]) for v in normed]
+        for b, v in zip(blocks, up):
+            ups[layer, b, :] = v
+        hidden = [(u * sigmoid(u)).astype(BF) for u in up]
+        x = [v + dot_nn(h, w_down[layer]) for v, h in zip(x, hidden)]
+    return x
+
+
+def backward(
+    x, blocks, offset, kwb, gains, w_energy, w_qkv, w_out, w_up, w_down, xs, qkv, ups, probs, slope, att, dqkv, acc
+):
+    edges = blocks[-1].stop
+    spans = atom_spans(edges)
+    at = [(s, 128 * g) for s in spans for g in range(2)]
+    read = gains[4:5, :] * w_energy[...]
+    readout = []
+    dx = []
+    for b, v in zip(blocks, x):
+        r = rms_factor(v)
+        scaled = v * r
+        terms = scaled * read
+        readout.append(terms[:, 0:128] + terms[:, 128:256])
+        total = jnp.sum(terms, axis=-1, keepdims=True) * (1.0 / D)
+        dx.append((kwb[shifted(b, offset), 0:1] * r) * (read - scaled * total))
+    for layer in (1, 0):
+        dhid = [dot_nt(v.astype(BF), w_down[layer]) for v in dx]
+        dup = []
+        for b, dh in zip(blocks, dhid):
+            u = ups[layer, b, :]
+            sig = sigmoid(u)
+            dup.append((dh * (sig * (1.0 + u * (1.0 - sig)))).astype(BF))
+        gain = gains[2 * layer + 1 : 2 * layer + 2, :]
+        dnorm = [dot_nt(v, w_up[layer]) * gain for v in dup]
+        new = []
+        for b, v, dn in zip(blocks, dx, dnorm):
+            xv = xs[2 * layer + 1, b, :]
+            new.append(v + rms_back(xv, rms_factor(xv), dn))
+        dx = new
+        for b, v in zip(blocks, dx):
+            att[b, :] = dot_nt(v.astype(BF), w_out[layer])
+        do = [spread(att[s, c : c + 128]) for s, c in at]
+        v = [qkv[layer, s, 2 * D + c : 2 * D + c + 128].astype(BF) for s, c in at]
+        p = [probs[layer, s, c : c + 128] for s, c in at]
+        dp = [dot_nt(vv, dd) for vv, dd in zip(v, do)]
+        dv = [dot_nn(pp.astype(BF), dd) for pp, dd in zip(p, do)]
+        q = [spread(qkv[layer, s, c : c + 128]) for s, c in at]
+        k = [qkv[layer, s, D + c : D + c + 128].astype(BF) for s, c in at]
+        dl = [pp * (dd - jnp.sum(pp * dd, axis=0, keepdims=True)) for pp, dd in zip(p, dp)]
+        ds = [(dd * slope[layer, s, c : c + 128]).astype(BF) for (s, c), dd in zip(at, dl)]
+        dk = [dot_nn(dd, qq) for dd, qq in zip(ds, q)]
+        dq = [gather_heads(dot_tn(dd, kk)) for dd, kk in zip(ds, k)]
+        for i, (s, c) in enumerate(at):
+            dqkv[s, c : c + 128] = dq[i]
+            dqkv[s, D + c : D + c + 128] = dk[i]
+            dqkv[s, 2 * D + c : 2 * D + c + 128] = dv[i]
+        for u, s in enumerate(spans):
+            total = dl[2 * u] + dl[2 * u + 1]
+            acc[s, :] = total if layer == 1 else acc[s, :] + total
+        gain = gains[2 * layer : 2 * layer + 1, :]
+        dnorm = [dot_nt(dqkv[b, :].astype(BF), w_qkv[layer]) * gain for b in blocks]
+        new = []
+        for b, v, dn in zip(blocks, dx, dnorm):
+            xv = xs[2 * layer, b, :]
+            new.append(v + rms_back(xv, rms_factor(xv), dn))
+        dx = new
+    return readout, dx
+
+
+def inner_forward_kernel(
+    base, kwb, gains, w_qkv, w_out, w_up, w_down, last, xs, qkv, ups, probs, slope, att
+):
+    blocks = block_list(INNER, 1)
+    x = forward(
+        [base[0:INNER, :]], blocks, 0, kwb, gains, w_qkv, w_out, w_up, w_down, xs, qkv, ups, probs, slope, att
+    )
+    last[...] = x[0]
+
+
+def inner_backward_kernel(
+    last, xs, qkv, ups, probs, slope, kwb, gains, w_energy, w_qkv, w_out, w_up, w_down, terms, dx, acc, att, dqkv
+):
+    blocks = block_list(INNER, 1)
+    readout, out = backward(
+        [last[...]],
+        blocks,
+        0,
+        kwb,
+        gains,
+        w_energy,
+        w_qkv,
+        w_out,
+        w_up,
+        w_down,
+        xs,
+        qkv,
+        ups,
+        probs,
+        slope,
+        att,
+        dqkv,
+        acc,
+    )
+    terms[...] = readout[0]
+    dx[...] = out[0]
 
 
 def layer_kernel(
@@ -191,6 +385,10 @@
     w_down,
     w_energy,
     pick,
+    inner_last,
+    inner_terms,
+    inner_dx,
+    inner_acc,
     tokens,
     reads,
     grad,
@@ -206,152 +404,35 @@
     dqkv,
     acc,
 ):
-    edges = base.shape[0]
-    atoms = edges // NBR
-    blocks = [slice(i, i + ROWS) for i in range(0, edges, ROWS)]
-    lane_head = iota((1, 128), 1) >> 5
-    head_lanes = [lane_head == h for h in range(4)]
-    row_head = iota((128, 128), 0)
-    mask_low = (iota((128, 128), 1) >> 5) * NBR
-    block_mask = jnp.where(
-        (row_head >= mask_low) & (row_head < mask_low + NBR), 1.0, 0.0
-    ).astype(BF)
-    score_scale = 1.0 / (math.sqrt(D // HEADS) * score_cap)
-    slope_scale = 1.0 / math.sqrt(D // HEADS)
-
-    def spread(x):
-        two = jnp.concatenate([x, x], axis=0).astype(BF)
-        return jnp.concatenate([two, two, jnp.zeros((32, 128), BF)], axis=0) * block_mask
-
-    def gather_heads(wide):
-        out = jnp.where(head_lanes[0], wide[0:NBR], 0.0)
-        for h in range(1, 4):
-            out = jnp.where(head_lanes[h], wide[h * NBR : (h + 1) * NBR], out)
-        return out
-
+    blocks = block_list(OUTER, 2)
     arrived = jnp.concatenate([arr_r[...], arr_m[...], arr_l[...]], axis=0)
-    x = [base[b, :] + dot_nn(far[b, :], arrived) for b in blocks]
-
-    for layer in range(2):
-        for b, v in zip(blocks, x):
-            xs[2 * layer, b, :] = v
-        gain = gains[2 * layer : 2 * layer + 1, :]
-        normed = [(v * rms_factor(v) * gain).astype(BF) for v in x]
-        for b, v in zip(blocks, normed):
-            qkv[layer, b, :] = dot_nn(v, w_qkv[layer])
-
-        @pl.loop(0, atoms // GROUP)
-        def _(step):
-            spans = [
-                pl.ds(pl.multiple_of(step * (GROUP * NBR) + u * NBR, 8), NBR) for u in range(GROUP)
-            ]
-            at = [(s, 128 * g) for s in spans for g in range(2)]
-            q = [spread(qkv[layer, s, c : c + 128]) for s, c in at]
-            k = [qkv[layer, s, D + c : D + c + 128].astype(BF) for s, c in at]
-            v = [qkv[layer, s, 2 * D + c : 2 * D + c + 128].astype(BF) for s, c in at]
-            t = [dot_nt(kk, qq) for kk, qq in zip(k, q)]
-            t = [jnp.tanh(tt * score_scale) for tt in t]
-            e = [kwb[s, :] * jnp.exp(score_cap * tt) for (s, c), tt in zip(at, t)]
-            p = [ee * (1.0 / jnp.sum(ee, axis=0, keepdims=True)) for ee in e]
-            o = [dot_tn(pp.astype(BF), vv) for pp, vv in zip(p, v)]
-            o = [gather_heads(oo) for oo in o]
-            for i, (s, c) in enumerate(at):
-                probs[layer, s, c : c + 128] = p[i]
-                slope[layer, s, c : c + 128] = (1.0 - t[i] * t[i]) * slope_scale
-                att[s, c : c + 128] = o[i]
-
-        x = [xs[2 * layer, b, :] + dot_nn(att[b, :].astype(BF), w_out[layer]) for b in blocks]
-        for b, v in zip(blocks, x):
-            xs[2 * layer + 1, b, :] = v
-        gain = gains[2 * layer + 1 : 2 * layer + 2, :]
-        normed = [(v * rms_factor(v) * gain).astype(BF) for v in x]
-        up = [dot_nn(v, w_up[layer]) for v in normed]
-        for b, v in zip(blocks, up):
-            ups[layer, b, :] = v
-        hidden = [(u * sigmoid(u)).astype(BF) for u in up]
-        x = [v + dot_nn(h, w_down[layer]) for v, h in zip(x, hidden)]
-
-    read = gains[4:5, :] * w_energy[...]
-    ones8 = jnp.ones((8, 128), BF)
-    readout = []
-    dx = []
+    x = []
+    for b in blocks:
+        here = shifted(b, INNER)
+        x.append(base[here, :] + dot_nn(far[here, :], arrived))
+    stores = (xs, qkv, ups, probs, slope, att)
+    weights = (w_qkv, w_out, w_up, w_down)
+    x = forward(x, blocks, INNER, kwb, gains, *weights, *stores)
+    tokens[0:INNER, :] = inner_last[...].astype(BF)
     for b, v in zip(blocks, x):
-        tokens[b, :] = v.astype(BF)
-        r = rms_factor(v)
-        scaled = v * r
-        terms = scaled * read
-        part_hi, part_lo = split2(terms[:, 0:128] + terms[:, 128:256])
-        readout.append(dot_nt(ones8, part_hi) + dot_nt(ones8, part_lo))
-        total = jnp.sum(terms, axis=-1, keepdims=True) * (1.0 / D)
-        kw_col = kwb[b, 0:1]
-        dx.append((kw_col * r) * (read - scaled * total))
-    readout = jnp.concatenate(readout, axis=1)[0:1]
-    live = rows[2:3, :]
-    reads[...] = readout
-
-    for layer in (1, 0):
-        dhid = [dot_nt(v.astype(BF), w_down[layer]) for v in dx]
-        dup = []
-        for b, dh in zip(blocks, dhid):
-            u = ups[layer, b, :]
-            sig = sigmoid(u)
-            dup.append((dh * (sig * (1.0 + u * (1.0 - sig)))).astype(BF))
-        gain = gains[2 * layer + 1 : 2 * layer + 2, :]
-        dnorm = [dot_nt(v, w_up[layer]) * gain for v in dup]
-        new = []
-        for b, v, dn in zip(blocks, dx, dnorm):
-            xv = xs[2 * layer + 1, b, :]
-            new.append(v + rms_back(xv, rms_factor(xv), dn))
-        dx = new
-        for b, v in zip(blocks, dx):
-            att[b, :] = dot_nt(v.astype(BF), w_out[layer])
-
-        @pl.loop(0, atoms // GROUP)
-        def _(step):
-            spans = [
-                pl.ds(pl.multiple_of(step * (GROUP * NBR) + u * NBR, 8), NBR) for u in range(GROUP)
-            ]
-            at = [(s, 128 * g) for s in spans for g in range(2)]
-            do = [spread(att[s, c : c + 128]) for s, c in at]
-            v = [qkv[layer, s, 2 * D + c : 2 * D + c + 128].astype(BF) for s, c in at]
-            p = [probs[layer, s, c : c + 128] for s, c in at]
-            dp = [dot_nt(vv, dd) for vv, dd in zip(v, do)]
-            dv = [dot_nn(pp.astype(BF), dd) for pp, dd in zip(p, do)]
-            q = [spread(qkv[layer, s, c : c + 128]) for s, c in at]
-            k = [qkv[layer, s, D + c : D + c + 128].astype(BF) for s, c in at]
-            dl = [pp * (dd - jnp.sum(pp * dd, axis=0, keepdims=True)) for pp, dd in zip(p, dp)]
-            ds = [(dd * slope[layer, s, c : c + 128]).astype(BF) for (s, c), dd in zip(at, dl)]
-            dk = [dot_nn(dd, qq) for dd, qq in zip(ds, q)]
-            dq = [gather_heads(dot_tn(dd, kk)) for dd, kk in zip(ds, k)]
-            old = [acc[s, :] for s in spans] if layer == 0 else None
-            for i, (s, c) in enumerate(at):
-                dqkv[s, c : c + 128] = dq[i]
-                dqkv[s, D + c : D + c + 128] = dk[i]
-                dqkv[s, 2 * D + c : 2 * D + c + 128] = dv[i]
-            for u, s in enumerate(spans):
-                total = dl[2 * u] + dl[2 * u + 1]
-                acc[s, :] = total if layer == 1 else old[u] + total
-
-        gain = gains[2 * layer : 2 * layer + 1, :]
-        dnorm = [dot_nt(dqkv[b, :].astype(BF), w_qkv[layer]) * gain for b in blocks]
-        new = []
-        for b, v, dn in zip(blocks, dx, dnorm):
-            xv = xs[2 * layer, b, :]
-            new.append(v + rms_back(xv, rms_factor(xv), dn))
-        dx = new
+        tokens[shifted(b, INNER), :] = v.astype(BF)
+    terms, dx = backward(x, blocks, INNER, kwb, gains, w_energy, *weights, *stores, dqkv, acc)
 
     w = wfeat[...]
     whi = w.astype(BF)
     wlo = (w - whi.astype(F32)).astype(BF)
-    back = []
-    acc_row = []
-    for b, v in zip(blocks, dx):
-        hi, lo = split2(v)
-        back.append(dot_nt(whi, hi) + dot_nt(whi, lo) + dot_nt(wlo, hi))
-        part_hi, part_lo = split2(acc[b, :])
-        acc_row.append(dot_nt(ones8, part_hi) + dot_nt(ones8, part_lo))
-    back = jnp.concatenate(back, axis=1)
-    acc_row = jnp.concatenate(acc_row, axis=1)[0:1]
+    ones8 = jnp.ones((8, 128), BF)
+
+    def to_row(parts):
+        hi, lo = split2(jnp.concatenate(parts, axis=0))
+        return (dot_nt(ones8, hi) + dot_nt(ones8, lo))[0:1]
+
+    hi, lo = split2(jnp.concatenate([inner_dx[...]] + dx, axis=0))
+    back = dot_nt(whi, hi) + dot_nt(whi, lo) + dot_nt(wlo, hi)
+    readout = to_row([inner_terms[...]] + terms)
+    reads[...] = readout
+    acc_row = to_row([inner_acc[...], acc[...]])
+    live = rows[2:3, :]
     dist = rows[0:1, :]
     cut = rows[1:2, :]
     f = feat[...]
@@ -404,12 +485,12 @@
     forces[...] = (partial[...] - far[0:8] - far[8:16])[0:3]
 
 
-def vmem_call(kernel, outs, *args, scratch=(), limit=12 * 2**20):
+def vmem_call(kernel, outs, *args, scratch=(), limit=12 * 2**20, place=VMEM):
     spec = pl.BlockSpec(memory_space=VMEM)
     return pl.pallas_call(
         kernel,
         out_shape=outs,
-        in_specs=[spec] * len(args),
+        in_specs=[pl.BlockSpec(memory_space=place)] * len(args),
         out_specs=jax.tree.map(lambda _: spec, outs),
         scratch_shapes=list(scratch),
         compiler_params=pltpu.CompilerParams(vmem_limit_bytes=limit),
@@ -429,7 +510,16 @@
         w_neigh,
         prev_tokens,
         send,
-        scratch=[VMEM((3 * SIDE, 8), F32)],
+        scratch=[
+            VMEM((3 * SIDE, 8), F32),
+            VMEM((26 * SLOTS,), jnp.int32),
+            VMEM((ATOMS_DEV, D), BF),
+            VMEM((D, D), BF),
+            VMEM((EDGE_DEV, D), BF),
+            pltpu.SemaphoreType.DMA((4,)),
+        ],
+        place=pltpu.HBM,
+        limit=62 * 2**20,
     )
 
 
@@ -459,7 +549,39 @@
     return vmem_call(lookup_kernel, outs, slot, mask, where)
 
 
-def layers(base, arr, far, kwb, feat, rows, wfeat, gains, w_qkv, w_out, w_up, w_down, w_energy, pick):
+def inner_stores(n):
+    return [
+        shape((4, n, D)),
+        shape((2, n, 3 * D)),
+        shape((2, n, FF)),
+        shape((2, n, D)),
+        shape((2, n, D)),
+    ]
+
+
+def inner_forward(base, kwb, gains, weights):
+    n = INNER
+    outs = [shape((n, D))] + inner_stores(n)
+    return vmem_call(
+        inner_forward_kernel, outs, base, kwb, gains, *weights, scratch=[VMEM((n, D), F32)]
+    )
+
+
+def inner_backward(saved, kwb, gains, w_energy, weights):
+    n = INNER
+    return vmem_call(
+        inner_backward_kernel,
+        [shape((n, 128)), shape((n, D)), shape((n, 128))],
+        *saved,
+        kwb,
+        gains,
+        w_energy,
+        *weights,
+        scratch=[VMEM((n, D), F32), VMEM((n, 3 * D), F32)],
+    )
+
+
+def layers(base, arr, far, kwb, feat, rows, wfeat, gains, weights, w_energy, pick, inner):
     side = shape((8, SIDE))
     n = EDGE_DEV
     return vmem_call(
@@ -473,23 +595,13 @@
         rows,
         wfeat,
         gains,
-        w_qkv,
-        w_out,
-        w_up,
-        w_down,
+        *weights,
         w_energy,
         pick,
+        *inner,
         limit=LIMIT,
-        scratch=[
-            VMEM((4, n, D), F32),
-            VMEM((2, n, 3 * D), F32),
-            VMEM((2, n, FF), F32),
-            VMEM((2, n, D), F32),
-            VMEM((2, n, D), F32),
-            VMEM((n, D), F32),
-            VMEM((n, 3 * D), F32),
-            VMEM((n, 128), F32),
-        ],
+        scratch=[VMEM(v.shape, F32) for v in inner_stores(OUTER)]
+        + [VMEM((OUTER, D), F32), VMEM((OUTER, 3 * D), F32), VMEM((OUTER, 128), F32)],
     )
 
 
@@ -521,18 +633,22 @@
 ):
     message, low, mid, high, where = messages(atom_state, w_neigh, prev_tokens, send_edges)
     low, high = exchange(low, high, "gx")
+    far, pick, mt = lookups(reverse_slot, neighbour_mask, where)
     cells = [v.reshape(3, 3, SLOTS, D) for v in (low, mid, high)]
     low, mid, high = (jnp.stack([v[i] for v in cells]) for i in range(3))
-    low, high, where = lax.optimization_barrier((low, high, where))
+    low, high, late = lax.optimization_barrier((low, high, displacement))
     low, high = exchange(low, high, "gy")
-    far, pick, mt = lookups(reverse_slot, neighbour_mask, where)
+    base, kwb, feat, rows, wfeat = geometry(
+        late, neighbour_mask, reverse_slot, species, message, species_table, w_vec, w_rbf
+    )
+    weights = (w_qkv, w_out, w_up, w_down)
+    w_energy = w_energy.reshape(1, D)
+    saved = inner_forward(base, kwb, gains, weights)
     cells = (low, mid, high)
     low, mid, high = (jnp.stack([v[:, i] for v in cells], axis=1) for i in range(3))
-    low, high, late = lax.optimization_barrier((low, high, displacement))
+    low, high, *saved = lax.optimization_barrier((low, high, *saved))
     low, high = exchange(low, high, "gz")
-    base, kwb, feat, rows, wfeat = geometry(
-        late, neighbour_mask, reverse_slot, species, message, species_table, w_vec, w_rbf
-    )
+    terms, dx, acc = inner_backward(saved, kwb, gains, w_energy, weights)
     arr = [v.reshape(SIDE, D) for v in (low, mid, high)]
     tokens, reads, grad, low, mid, high = layers(
         base,
@@ -543,12 +659,10 @@
         rows,
         wfeat,
         gains,
-        w_qkv,
-        w_out,
-        w_up,
-        w_down,
-        w_energy.reshape(1, D),
+        weights,
+        w_energy,
         pick,
+        (saved[0], terms, dx, acc),
     )
     low, high = exchange(low, high, "gx")
     cells = jnp.stack([low, mid, high])

time: 63.1 us -> 60.5 us (0.959)
  waiting for transfers between devices: 16.8 us -> 6.97 us
  Pallas kernels: 23.4 us -> 28.2 us
  starting transfers between devices: 18.2 us -> 21.1 us
    ppermute x12, waiting for transfers between devices: 16.8 us -> 6.97 us  [exchange(): return (lax.ppermute(low, axis, outer), lax.ppermute(high, axis, inner))]
    pallas_call x6 -> x8, Pallas kernels: 23.4 us -> 28.2 us  [vmem_call(): pl.pallas_call(kernel, out_shape=outs, in_specs=[pl.BlockSpec(memory_spac...]
    ppermute x12, starting transfers between devices: 18.2 us -> 21.1 us  [exchange(): return (lax.ppermute(low, axis, outer), lax.ppermute(high, axis, inner))]
    unnamed x34 -> x30, local copies, waits for them, and re-layouts: 3.37 us -> 1.98 us
    slice x3, local copies, waits for them, and re-layouts: 0.02 us -> 0.85 us  [on_device(): low, mid, high = (jnp.stack([v[i] for v in cells]) for i in range(3))]
  transfers between devices with their start and end apart: 12 -> 12, of which waited for: 8 -> 4; matrix products, arithmetic and copies ran while one was open for 0% -> 1% of each run, Pallas kernels for 5% -> 14%
where the time goes in v4:
time: 60.5 us; the launch traced here: 60.3 us
  Pallas kernels  28.2 us (47%)
  starting transfers between devices  21.1 us (35%)
  waiting for transfers between devices  6.97 us (12%)
  local copies, waits for them, and re-layouts  3 us (5%)
  between operations  0.99 us (2%)
    pallas_call x8, Pallas kernels, vmem_call(): pl.pallas_call(kernel, out_shape=outs, in_specs=[pl.BlockSpec(memory_spac...  28.2 us
    ppermute x12, starting transfers between devices, exchange(): return (lax.ppermute(low, axis, outer), lax.ppermute(high, axis, inner))  21.1 us
    ppermute x12, waiting for transfers between devices, exchange(): return (lax.ppermute(low, axis, outer), lax.ppermute(high, axis, inner))  6.97 us
    unnamed x30, local copies, waits for them, and re-layouts  1.98 us
  transfers between devices with their start and end apart: 12, of which 4 were waited for; matrix products, arithmetic and copies ran while one was open for 1% of the time, Pallas kernels for 14%

profile of v4, /device:TPU:0, one launch (start us, length us, event | category | flops | bytes accessed | tf_op | source)
XLA Modules:
  0.0 60.3 jit_solution(18189051918569218237)
XLA Ops:
  0.6 0.0 copy-start.9
  0.6 0.0 copy-start.10
  0.7 0.0 copy-start.7
  0.7 0.0 copy-start.8
  0.7 0.0 copy-start.11
  0.7 0.0 copy-start.12
  0.7 0.0 copy-start.14
  0.7 0.0 copy-start.3
  0.7 0.0 copy-start.6
  0.7 3.1 %shard_map.184 = (bf16[768,256]{1,0:T(8,128)(2,1)}, bf16[144,256]{1,0:T(8,128)(2,1)}, bf16[144,256]{1,0:T(8,128)(2,1)}, bf16[144,256]{1,0:T(8,128)(2,1)}, f32[432,8]{1,0:T(8,128)}) custom-call(bf16[32,256]{1,0:T(8,128)(2,1)} %state_far.1, bf16[256,256]{1,0:T(8,128)(2,1)} %w_far.1, bf16[768,256]{1,0:T(8,128)(2,1)} %prev_far.1, s32[416]{0:T(512)} %send_far.1), custom_call_target="tpu_custom_call" | custom-call | tf_op jit(solution)/shard_map/pallas_call | solution.py:490
  3.8 1.5 %collective-permute-start = (bf16[144,256]{1,0:T(8,128)(2,1)}, bf16[144,256]{1,0:T(8,128)(2,1)S(1)}, u32[]{:S(2)}, u32[]{:S(2)}) collective-permute-start(bf16[144,256]{1,0:T(8,128)(2,1)} %get-tuple-element.47), channel_id=1, source_target_pairs={{0,96},{32,64},{64,32},{96,0},{1,97},{33,65},{65,33},{97,1},{2,98}... | collective-permute-start | bytes 221192 | tf_op jit(solution)/shard_map/ppermute | solution.py:612
  5.3 0.7 %collective-permute-start.1 = (bf16[144,256]{1,0:T(8,128)(2,1)}, bf16[144,256]{1,0:T(8,128)(2,1)S(1)}, u32[]{:S(2)}, u32[]{:S(2)}) collective-permute-start(bf16[144,256]{1,0:T(8,128)(2,1)} %get-tuple-element.49), channel_id=1, source_target_pairs={{0,32},{32,0},{64,96},{96,64},{1,33},{33,1},{65,97},{97,65},{2,34}... | collective-permute-start | bytes 221192 | tf_op jit(solution)/shard_map/ppermute | solution.py:612
  6.0 0.0 copy-start.2
  6.0 0.8 %fusion.4 = (bf16[48,256]{1,0:T(8,128)(2,1)S(1)}, bf16[48,256]{1,0:T(8,128)(2,1)S(1)}, bf16[48,256]{1,0:T(8,128)(2,1)S(1)}) fusion(bf16[144,256]{1,0:T(8,128)(2,1)} %get-tuple-element.48), kind=kLoop, calls=%fused_computation.13 | loop fusion | bytes 147456 | tf_op jit(solution)/shard_map/slice | solution.py:638
  6.8 0.0 copy-done.9
  6.8 0.0 copy-done.10
  6.8 0.0 copy-start.5
  6.9 0.9 %copy-done.5 = f32[432,8]{1,0:T(8,128)S(1)} copy-done((f32[432,8]{1,0:T(8,128)S(1)}, f32[432,8]{1,0:T(8,128)}, u32[]{:S(2)}) %copy-start.5) | copy-done | bytes 13848
  7.8 1.0 %shard_map.187 = (bf16[768,432]{1,0:T(8,128)(2,1)S(1)}, bf16[432,768]{1,0:T(8,128)(2,1)S(1)}, f32[32,432]{1,0:T(8,128)S(1)}) custom-call(s32[768]{0:T(1024)S(1)} %copy-done.9, s32[768]{0:T(1024)S(1)} %copy-done.10, f32[432,8]{1,0:T(8,128)S(1)} %copy-done.5), custom_call_target="tpu_custom_call" | custom-call | tf_op jit(solution)/shard_map/pallas_call | solution.py:490
  8.8 0.0 collective-permute-done
  8.8 0.0 collective-permute-done.1
  8.8 0.0 copy-start.1
  8.8 3.1 %collective-permute-start.2 = (bf16[3,3,16,256]{3,2,1,0:T(8,128)(2,1)S(1)}, bf16[3,3,16,256]{3,2,1,0:T(8,128)(2,1)S(1)}, u32[]{:S(2)}, u32[]{:S(2)}) collective-permute-start(bf16[3,3,16,256]{3,2,1,0:T(8,128)(2,1)S(1)} %get-tuple-element.53), channel_id=1, source_target_pairs={{0,24},{8,16},{16,8},{24,0},{1,25},{9,17},{17,9},{25,1},{2,26},{10... | collective-permute-start | bytes 221192 | tf_op jit(solution)/shard_map/ppermute | solution.py:612
  11.9 0.1 collective-permute-start.3
  12.1 0.0 copy-done.7
  12.1 0.0 copy-done.8
  12.1 0.0 copy-done.11
  12.1 0.0 copy-done.12
  12.1 0.0 copy-done.14
  12.2 0.0 copy-start.4
  12.2 1.0 %copy-done.4 = bf16[768,256]{1,0:T(8,128)(2,1)S(1)} copy-done((bf16[768,256]{1,0:T(8,128)(2,1)S(1)}, bf16[768,256]{1,0:T(8,128)(2,1)}, u32[]{:S(2)}) %copy-start.4) | copy-done | bytes 393240
  13.2 1.0 %shard_map.185 = (f32[768,256]{1,0:T(8,128)S(1)}, f32[768,128]{1,0:T(8,128)S(1)}, f32[72,768]{1,0:T(8,128)S(1)}, f32[8,768]{1,0:T(8,128)S(1)}, f32[72,256]{1,0:T(8,128)S(1)}) custom-call(f32[3,768]{1,0:T(4,128)S(1)} %copy-done.11, s32[768]{0:T(1024)S(1)} %copy-done.10, s32[768]{0:T(1024)S(1)} %copy-done.9, s32[32]{0:T(128)S(1)} %copy-done.14, ...), custom_call_target="tpu_custom_call" | custom-call | tf_op jit(solution)/shard_map/pallas_call | solution.py:490
  14.2 0.0 copy-done.3
  14.2 0.0 copy-done.6
  14.2 0.0 copy-done.2
  14.2 0.0 copy-done
  14.2 0.0 copy-done.1
  14.2 2.4 %shard_map.186 = (f32[96,256]{1,0:T(8,128)S(1)}, f32[4,96,256]{2,1,0:T(8,128)S(1)}, f32[2,96,768]{2,1,0:T(8,128)S(1)}, f32[2,96,512]{2,1,0:T(8,128)S(1)}, f32[2,...) custom-call(f32[768,256]{1,0:T(8,128)S(1)} %get-tuple-element.52.base, f32[768,128]{1,0:T(8,128)S(1)} %get-tuple-element.55.kwb, ...), custom_call_target="tpu_custom_call" | custom-call | tf_op jit(solution)/shard_map/pallas_call | solution.py:490
  16.6 0.0 collective-permute-done.2
  16.6 0.0 collective-permute-done.3
  16.7 0.0 copy-start.13
  16.7 1.6 %collective-permute-start.5 = (bf16[3,3,16,256]{3,2,1,0:T(8,128)(2,1)S(1)}, bf16[3,3,16,256]{3,2,1,0:T(8,128)(2,1)S(1)}, u32[]{:S(2)}, u32[]{:S(2)}) collective-permute-start(bf16[3,3,16,256]{3,2,1,0:T(8,128)(2,1)S(1)} %pad_maximum_fusion.4), channel_id=1, source_target_pairs={{0,1},{1,0},{2,3},{3,2},{4,5},{5,4},{6,7},{7,6},{8,9},{9,8},{10,11... | collective-permute-start | bytes 221192 | tf_op jit(solution)/shard_map/ppermute | solution.py:612
  18.3 5.2 %collective-permute-start.4 = (bf16[3,3,16,256]{3,2,1,0:T(8,128)(2,1)S(1)}, bf16[3,3,16,256]{3,2,1,0:T(8,128)(2,1)S(1)}, u32[]{:S(2)}, u32[]{:S(2)}) collective-permute-start(bf16[3,3,16,256]{3,2,1,0:T(8,128)(2,1)S(1)} %pad_maximum_fusion.3), channel_id=1, source_target_pairs={{0,7},{1,2},{2,1},{3,4},{4,3},{5,6},{6,5},{7,0},{8,15},{9,10},{10,... | collective-permute-start | bytes 221192 | tf_op jit(solution)/shard_map/ppermute | solution.py:612
  23.5 0.0 copy-done.13
  23.5 2.9 %shard_map.188 = (f32[96,128]{1,0:T(8,128)S(1)}, f32[96,256]{1,0:T(8,128)S(1)}, f32[96,128]{1,0:T(8,128)S(1)}) custom-call(f32[96,256]{1,0:T(8,128)S(1)} %get-tuple-element.70.last.inner_last, f32[4,96,256]{2,1,0:T(8,128)S(1)} %get-tuple-element.71.xs, f32[2,96,768]{2,1,0:T(8,128)S(1)} %get-tuple-element.72.qkv, f32[2,96,512]{2,1,0:T(8,128)S(1)} %get-tuple-element.73.ups, ...), custom_call_target="tpu_custom_call" | custom-call | tf_op jit(solution)/shard_map/pallas_call | solution.py:490
  26.4 0.0 collective-permute-done.5
  26.4 0.0 collective-permute-done.4
  26.4 15.8 %shard_map.189 = (bf16[768,256]{1,0:T(8,128)(2,1)}, f32[1,768]{1,0:T(1,128)S(1)}, f32[8,768]{1,0:T(8,128)S(1)}, f32[8,144]{1,0:T(8,128)S(1)}, f32[8,144]{1,0:T(8,128)S(1)}, /*index=5*/f32[8,144]{1,0:T(8,128)S(1)}) custom-call(f32[768,256]{1,0:T(8,128)S(1)} %get-tuple-element.52.base, bf16[144,256]{1,0:T(8,128)(2,1)S(1)} %bitcast.23, ...), custom_call_target="tpu_custom_call" | custom-call | tf_op jit(solution)/shard_map/pallas_call | solution.py:490
  42.3 0.0 collective-permute-start.6
  42.3 1.8 %collective-permute-start.7 = (f32[8,144]{1,0:T(8,128)S(1)}, f32[8,144]{1,0:T(8,128)S(1)}, u32[]{:S(2)}, u32[]{:S(2)}) collective-permute-start(f32[8,144]{1,0:T(8,128)S(1)} %get-tuple-element.82), channel_id=1, source_target_pairs={{0,32},{32,0},{64,96},{96,64},{1,33},{33,1},{65,97},{97,65},{2,34}... | collective-permute-start | bytes 13832 | tf_op jit(solution)/shard_map/ppermute | solution.py:612
  44.1 1.3 %collective-permute-done.6 = f32[8,144]{1,0:T(8,128)S(1)} collective-permute-done((f32[8,144]{1,0:T(8,128)S(1)}, f32[8,144]{1,0:T(8,128)S(1)}, u32[]{:S(2)}, u32[]{:S(2)}) %collective-permute-start.6) | collective-permute-done | bytes 4640 | tf_op jit(solution)/shard_map/ppermute | solution.py:612
  45.4 0.0 collective-permute-done.7
  45.4 0.1 fusion.7
  45.4 1.1 %collective-permute-start.8 = (f32[3,8,48]{2,1,0:T(8,128)S(1)}, f32[3,8,48]{2,1,0:T(8,128)S(1)}, u32[]{:S(2)}, u32[]{:S(2)}) collective-permute-start(f32[3,8,48]{2,1,0:T(8,128)S(1)} %get-tuple-element.112), channel_id=1, source_target_pairs={{0,24},{8,16},{16,8},{24,0},{1,25},{9,17},{17,9},{25,1},{2,26},{10... | collective-permute-start | bytes 13832 | tf_op jit(solution)/shard_map/ppermute | solution.py:612
  46.5 0.9 %collective-permute-start.9 = (f32[3,8,48]{2,1,0:T(8,128)S(1)}, f32[3,8,48]{2,1,0:T(8,128)S(1)}, u32[]{:S(2)}, u32[]{:S(2)}) collective-permute-start(f32[3,8,48]{2,1,0:T(8,128)S(1)} %get-tuple-element.113), channel_id=1, source_target_pairs={{0,8},{8,0},{16,24},{24,16},{1,9},{9,1},{17,25},{25,17},{2,10},{10... | collective-permute-start | bytes 13832 | tf_op jit(solution)/shard_map/ppermute | solution.py:612
  47.4 2.9 %collective-permute-done.8 = f32[3,8,48]{2,1,0:T(8,128)S(1)} collective-permute-done((f32[3,8,48]{2,1,0:T(8,128)S(1)}, f32[3,8,48]{2,1,0:T(8,128)S(1)}, u32[]{:S(2)}, u32[]{:S(2)}) %collective-permute-start.8) | collective-permute-done | bytes 4640 | tf_op jit(solution)/shard_map/ppermute | solution.py:612
  50.4 0.0 collective-permute-done.9
  50.4 0.1 fusion.6
  50.5 5.1 %collective-permute-start.10 = (f32[3,3,8,16]{3,2,1,0:T(8,128)S(1)}, f32[3,3,8,16]{3,2,1,0:T(8,128)S(1)}, u32[]{:S(2)}, u32[]{:S(2)}) collective-permute-start(f32[3,3,8,16]{3,2,1,0:T(8,128)S(1)} %get-tuple-element.89), channel_id=1, source_target_pairs={{0,7},{1,2},{2,1},{3,4},{4,3},{5,6},{6,5},{7,0},{8,15},{9,10},{10,... | collective-permute-start | bytes 13832 | tf_op jit(solution)/shard_map/ppermute | solution.py:612
  55.5 0.0 collective-permute-start.11
  55.5 1.2 %shard_map.190 = (f32[8,32]{1,0:T(8,128)S(1)}, f32[1,32]{1,0:T(1,128)}) custom-call(f32[8,768]{1,0:T(8,128)S(1)} %get-tuple-element.84.grad, s32[768]{0:T(1024)S(1)} %copy-done.9, f32[8,768]{1,0:T(8,128)S(1)} %get-tuple-element.67.rows, f32[1,768]{1,0:T(1,128)S(1)} %get-tuple-element.85.reads), custom_call_target="tpu_custom_call" | custom-call | tf_op jit(solution)/shard_map/pallas_call | solution.py:490
  56.7 1.4 %collective-permute-done.10.r = f32[3,3,8,16]{3,2,1,0:T(8,128)S(1)} collective-permute-done((f32[3,3,8,16]{3,2,1,0:T(8,128)S(1)}, f32[3,3,8,16]{3,2,1,0:T(8,128)S(1)}, u32[]{:S(2)}, u32[]{:S(2)}) %collective-permute-start.10) | collective-permute-done | bytes 4640 | tf_op jit(solution)/shard_map/ppermute | solution.py:612
  58.1 1.4 %collective-permute-done.11.l = f32[3,3,8,16]{3,2,1,0:T(8,128)S(1)} collective-permute-done((f32[3,3,8,16]{3,2,1,0:T(8,128)S(1)}, f32[3,3,8,16]{3,2,1,0:T(8,128)S(1)}, u32[]{:S(2)}, u32[]{:S(2)}) %collective-permute-start.11) | collective-permute-done | bytes 4640 | tf_op jit(solution)/shard_map/ppermute | solution.py:612
  59.5 0.8 %shard_map.191 = f32[3,32]{1,0:T(4,128)} custom-call(f32[8,32]{1,0:T(8,128)S(1)} %get-tuple-element.87.partial, f32[32,432]{1,0:T(8,128)S(1)} %get-tuple-element.88.mt, f32[3,3,8,16]{3,2,1,0:T(8,128)S(1)} %collective-permute-done.10.r, f32[3,3,8,16]{3,2,1,0:T(8,128)S(1)} %get-tuple-element.109.m, f32[3,3,8,16]{3,2,1,0:T(8,128)S(1)} %collective-permute-done.11.l), custom_call_target="tpu_custom_call" | custom-call | tf_op jit(solution)/shard_map/pallas_call | solution.py:490
  (13 shorter events, 0.1 us)
Async XLA Ops:
  0.6 6.2 %copy-start.9 = (s32[768]{0:T(1024)S(1)}, s32[768]{0:T(1024)}, u32[]{:S(2)}) copy-start(s32[768]{0:T(1024)} %slot.5) | copy-start | bytes 9220
  0.6 6.2 %copy-start.10 = (s32[768]{0:T(1024)S(1)}, s32[768]{0:T(1024)}, u32[]{:S(2)}) copy-start(s32[768]{0:T(1024)} %mask.3) | copy-start | bytes 9220
  0.7 11.5 %copy-start.7 = (f32[64,256]{1,0:T(8,128)S(1)}, f32[64,256]{1,0:T(8,128)}, u32[]{:S(2)}) copy-start(f32[64,256]{1,0:T(8,128)} %w_rbf.1) | copy-start | bytes 196612
  0.7 11.5 %copy-start.8 = (bf16[85,256]{1,0:T(8,128)(2,1)S(1)}, bf16[85,256]{1,0:T(8,128)(2,1)}, u32[]{:S(2)}) copy-start(bf16[85,256]{1,0:T(8,128)(2,1)} %table.1) | copy-start | bytes 130564
  0.7 11.5 %copy-start.11 = (f32[3,768]{1,0:T(4,128)S(1)}, f32[3,768]{1,0:T(4,128)}, u32[]{:S(2)}) copy-start(f32[3,768]{1,0:T(4,128)} %disp) | copy-start | bytes 27652
  0.7 11.5 %copy-start.12 = (f32[3,256]{1,0:T(4,128)S(1)}, f32[3,256]{1,0:T(4,128)}, u32[]{:S(2)}) copy-start(f32[3,256]{1,0:T(4,128)} %w_vec.1) | copy-start | bytes 9220
  0.7 11.5 %copy-start.14 = (s32[32]{0:T(128)S(1)}, s32[32]{0:T(128)}, u32[]{:S(2)}) copy-start(s32[32]{0:T(128)} %species.1) | copy-start | bytes 388
  0.7 13.5 %copy-start.3 = (bf16[2,256,256]{2,1,0:T(8,128)(2,1)S(1)}, bf16[2,256,256]{2,1,0:T(8,128)(2,1)}, u32[]{:S(2)}) copy-start(bf16[2,256,256]{2,1,0:T(8,128)(2,1)} %w_out.5) | copy-start | bytes 786436
  0.7 13.5 %copy-start.6 = (f32[5,256]{1,0:T(8,128)S(1)}, f32[5,256]{1,0:T(8,128)}, u32[]{:S(2)}) copy-start(f32[5,256]{1,0:T(8,128)} %gains.5) | copy-start | bytes 15364
  3.8 5.0 %collective-permute-start = (bf16[144,256]{1,0:T(8,128)(2,1)}, bf16[144,256]{1,0:T(8,128)(2,1)S(1)}, u32[]{:S(2)}, u32[]{:S(2)}) collective-permute-start(bf16[144,256]{1,0:T(8,128)(2,1)} %get-tuple-element.47), channel_id=1, source_target_pairs={{0,96},{32,64},{64,32},{96,0},{1,97},{33,65},{65,33},{97,1},{2,98}... | collective-permute-start | bytes 221192 | tf_op jit(solution)/shard_map/ppermute | solution.py:612
  5.3 3.5 %collective-permute-start.1 = (bf16[144,256]{1,0:T(8,128)(2,1)}, bf16[144,256]{1,0:T(8,128)(2,1)S(1)}, u32[]{:S(2)}, u32[]{:S(2)}) collective-permute-start(bf16[144,256]{1,0:T(8,128)(2,1)} %get-tuple-element.49), channel_id=1, source_target_pairs={{0,32},{32,0},{64,96},{96,64},{1,33},{33,1},{65,97},{97,65},{2,34}... | collective-permute-start | bytes 221192 | tf_op jit(solution)/shard_map/ppermute | solution.py:612
  6.0 8.2 %copy-start.2 = (bf16[2,512,256]{2,1,0:T(8,128)(2,1)S(1)}, bf16[2,512,256]{2,1,0:T(8,128)(2,1)}, u32[]{:S(2)}) copy-start(bf16[2,512,256]{2,1,0:T(8,128)(2,1)} %w_down.5) | copy-start | bytes 1572868
  6.8 0.9 %copy-start.5 = (f32[432,8]{1,0:T(8,128)S(1)}, f32[432,8]{1,0:T(8,128)}, u32[]{:S(2)}) copy-start(f32[432,8]{1,0:T(8,128)} %get-tuple-element.64.where) | copy-start | bytes 41476
  8.8 5.5 %copy-start = (bf16[2,256,768]{2,1,0:T(8,128)(2,1)S(1)}, bf16[2,256,768]{2,1,0:T(8,128)(2,1)}, u32[]{:S(2)}) copy-start(bf16[2,256,768]{2,1,0:T(8,128)(2,1)} %w_qkv.5) | copy-start | bytes 2359300
  8.8 5.4 %copy-start.1 = (bf16[2,256,512]{2,1,0:T(8,128)(2,1)S(1)}, bf16[2,256,512]{2,1,0:T(8,128)(2,1)}, u32[]{:S(2)}) copy-start(bf16[2,256,512]{2,1,0:T(8,128)(2,1)} %w_up.5) | copy-start | bytes 1572868
  8.8 7.8 %collective-permute-start.2 = (bf16[3,3,16,256]{3,2,1,0:T(8,128)(2,1)S(1)}, bf16[3,3,16,256]{3,2,1,0:T(8,128)(2,1)S(1)}, u32[]{:S(2)}, u32[]{:S(2)}) collective-permute-start(bf16[3,3,16,256]{3,2,1,0:T(8,128)(2,1)S(1)} %get-tuple-element.53), channel_id=1, source_target_pairs={{0,24},{8,16},{16,8},{24,0},{1,25},{9,17},{17,9},{25,1},{2,26},{10... | collective-permute-start | bytes 221192 | tf_op jit(solution)/shard_map/ppermute | solution.py:612
  11.9 4.7 %collective-permute-start.3 = (bf16[3,3,16,256]{3,2,1,0:T(8,128)(2,1)S(1)}, bf16[3,3,16,256]{3,2,1,0:T(8,128)(2,1)S(1)}, u32[]{:S(2)}, u32[]{:S(2)}) collective-permute-start(bf16[3,3,16,256]{3,2,1,0:T(8,128)(2,1)S(1)} %get-tuple-element.54), channel_id=1, source_target_pairs={{0,8},{8,0},{16,24},{24,16},{1,9},{9,1},{17,25},{25,17},{2,10},{10... | collective-permute-start | bytes 221192 | tf_op jit(solution)/shard_map/ppermute | solution.py:612
  12.2 1.0 %copy-start.4 = (bf16[768,256]{1,0:T(8,128)(2,1)S(1)}, bf16[768,256]{1,0:T(8,128)(2,1)}, u32[]{:S(2)}) copy-start(bf16[768,256]{1,0:T(8,128)(2,1)} %get-tuple-element.51.message) | copy-start | bytes 1179652
  16.7 6.8 %copy-start.13 = (f32[256]{0:T(256)S(1)}, f32[256]{0:T(256)}, u32[]{:S(2)}) copy-start(f32[256]{0:T(256)} %param.33) | copy-start | bytes 3076
  16.7 9.7 %collective-permute-start.5 = (bf16[3,3,16,256]{3,2,1,0:T(8,128)(2,1)S(1)}, bf16[3,3,16,256]{3,2,1,0:T(8,128)(2,1)S(1)}, u32[]{:S(2)}, u32[]{:S(2)}) collective-permute-start(bf16[3,3,16,256]{3,2,1,0:T(8,128)(2,1)S(1)} %pad_maximum_fusion.4), channel_id=1, source_target_pairs={{0,1},{1,0},{2,3},{3,2},{4,5},{5,4},{6,7},{7,6},{8,9},{9,8},{10,11... | collective-permute-start | bytes 221192 | tf_op jit(solution)/shard_map/ppermute | solution.py:612
  18.3 8.1 %collective-permute-start.4 = (bf16[3,3,16,256]{3,2,1,0:T(8,128)(2,1)S(1)}, bf16[3,3,16,256]{3,2,1,0:T(8,128)(2,1)S(1)}, u32[]{:S(2)}, u32[]{:S(2)}) collective-permute-start(bf16[3,3,16,256]{3,2,1,0:T(8,128)(2,1)S(1)} %pad_maximum_fusion.3), channel_id=1, source_target_pairs={{0,7},{1,2},{2,1},{3,4},{4,3},{5,6},{6,5},{7,0},{8,15},{9,10},{10,... | collective-permute-start | bytes 221192 | tf_op jit(solution)/shard_map/ppermute | solution.py:612
  42.3 3.1 %collective-permute-start.6 = (f32[8,144]{1,0:T(8,128)S(1)}, f32[8,144]{1,0:T(8,128)S(1)}, u32[]{:S(2)}, u32[]{:S(2)}) collective-permute-start(f32[8,144]{1,0:T(8,128)S(1)} %get-tuple-element.80), channel_id=1, source_target_pairs={{0,96},{32,64},{64,32},{96,0},{1,97},{33,65},{65,33},{97,1},{2,98}... | collective-permute-start | bytes 13832 | tf_op jit(solution)/shard_map/ppermute | solution.py:612
  42.3 3.1 %collective-permute-start.7 = (f32[8,144]{1,0:T(8,128)S(1)}, f32[8,144]{1,0:T(8,128)S(1)}, u32[]{:S(2)}, u32[]{:S(2)}) collective-permute-start(f32[8,144]{1,0:T(8,128)S(1)} %get-tuple-element.82), channel_id=1, source_target_pairs={{0,32},{32,0},{64,96},{96,64},{1,33},{33,1},{65,97},{97,65},{2,34}... | collective-permute-start | bytes 13832 | tf_op jit(solution)/shard_map/ppermute | solution.py:612
  45.4 4.9 %collective-permute-start.8 = (f32[3,8,48]{2,1,0:T(8,128)S(1)}, f32[3,8,48]{2,1,0:T(8,128)S(1)}, u32[]{:S(2)}, u32[]{:S(2)}) collective-permute-start(f32[3,8,48]{2,1,0:T(8,128)S(1)} %get-tuple-element.112), channel_id=1, source_target_pairs={{0,24},{8,16},{16,8},{24,0},{1,25},{9,17},{17,9},{25,1},{2,26},{10... | collective-permute-start | bytes 13832 | tf_op jit(solution)/shard_map/ppermute | solution.py:612
  46.5 3.9 %collective-permute-start.9 = (f32[3,8,48]{2,1,0:T(8,128)S(1)}, f32[3,8,48]{2,1,0:T(8,128)S(1)}, u32[]{:S(2)}, u32[]{:S(2)}) collective-permute-start(f32[3,8,48]{2,1,0:T(8,128)S(1)} %get-tuple-element.113), channel_id=1, source_target_pairs={{0,8},{8,0},{16,24},{24,16},{1,9},{9,1},{17,25},{25,17},{2,10},{10... | collective-permute-start | bytes 13832 | tf_op jit(solution)/shard_map/ppermute | solution.py:612
  50.5 7.7 %collective-permute-start.10 = (f32[3,3,8,16]{3,2,1,0:T(8,128)S(1)}, f32[3,3,8,16]{3,2,1,0:T(8,128)S(1)}, u32[]{:S(2)}, u32[]{:S(2)}) collective-permute-start(f32[3,3,8,16]{3,2,1,0:T(8,128)S(1)} %get-tuple-element.89), channel_id=1, source_target_pairs={{0,7},{1,2},{2,1},{3,4},{4,3},{5,6},{6,5},{7,0},{8,15},{9,10},{10,... | collective-permute-start | bytes 13832 | tf_op jit(solution)/shard_map/ppermute | solution.py:612
  55.5 4.0 %collective-permute-start.11 = (f32[3,3,8,16]{3,2,1,0:T(8,128)S(1)}, f32[3,3,8,16]{3,2,1,0:T(8,128)S(1)}, u32[]{:S(2)}, u32[]{:S(2)}) collective-permute-start(f32[3,3,8,16]{3,2,1,0:T(8,128)S(1)} %get-tuple-element.90), channel_id=1, source_target_pairs={{0,1},{1,0},{2,3},{3,2},{4,5},{5,4},{6,7},{7,6},{8,9},{9,8},{10,11... | collective-permute-start | bytes 13832 | tf_op jit(solution)/shard_map/ppermute | solution.py:612

commit v5 on v4

--- a/solution.py
+++ b/solution.py
@@ -506,10 +506,10 @@
     return vmem_call(
         message_kernel,
         [shape((EDGE_DEV, D), BF), side, side, side, shape((3 * SIDE, 8))],
-        atom_state,
-        w_neigh,
-        prev_tokens,
-        send,
+        *(
+            pltpu.with_memory_space_constraint(v, pltpu.HBM)
+            for v in (atom_state, w_neigh, prev_tokens, send)
+        ),
         scratch=[
             VMEM((3 * SIDE, 8), F32),
             VMEM((26 * SLOTS,), jnp.int32),
@@ -519,7 +519,6 @@
             pltpu.SemaphoreType.DMA((4,)),
         ],
         place=pltpu.HBM,
-        limit=62 * 2**20,
     )
 
 

time: 60.5 us -> 59.1 us (0.977)
  local copies, waits for them, and re-layouts: 3 us -> 0.25 us
  waiting for transfers between devices: 6.97 us -> 9.24 us
  Pallas kernels: 28.2 us -> 27.5 us
    ppermute x12, waiting for transfers between devices: 6.97 us -> 9.24 us  [exchange(): return (lax.ppermute(low, axis, outer), lax.ppermute(high, axis, inner))]
    unnamed x30 -> x26, local copies, waits for them, and re-layouts: 1.98 us -> 0.06 us
    slice x3, local copies, waits for them, and re-layouts: 0.85 us -> 0.02 us  [on_device(): low, mid, high = (jnp.stack([v[i] for v in cells]) for i in range(3))]
    pallas_call x8, Pallas kernels: 28.2 us -> 27.5 us  [vmem_call(): pl.pallas_call(kernel, out_shape=outs, in_specs=[pl.BlockSpec(memory_spac...]
  transfers between devices with their start and end apart: 12 -> 12, of which waited for: 4 -> 6; matrix products, arithmetic and copies ran while one was open for 1% -> 0% of each run, Pallas kernels for 14% -> 14%
where the time goes in v5:
time: 59.1 us; the launch traced here: 59 us
  Pallas kernels  27.5 us (47%)
  starting transfers between devices  21 us (36%)
  waiting for transfers between devices  9.24 us (16%)
  between operations  0.95 us (2%)
    pallas_call x8, Pallas kernels, vmem_call(): pl.pallas_call(kernel, out_shape=outs, in_specs=[pl.BlockSpec(memory_spac...  27.5 us
    ppermute x12, starting transfers between devices, exchange(): return (lax.ppermute(low, axis, outer), lax.ppermute(high, axis, inner))  21 us
    ppermute x12, waiting for transfers between devices, exchange(): return (lax.ppermute(low, axis, outer), lax.ppermute(high, axis, inner))  9.24 us
  transfers between devices with their start and end apart: 12, of which 6 were waited for; matrix products, arithmetic and copies ran while one was open for 0% of the time, Pallas kernels for 14%

profile of v5, /device:TPU:0, one launch (start us, length us, event | category | flops | bytes accessed | tf_op | source)
XLA Modules:
  0.0 59.0 jit_solution(14339447843301381360)
XLA Ops:
  0.6 0.0 copy-start.7
  0.6 0.0 copy-start.8
  0.7 0.0 copy-start.5
  0.7 0.0 copy-start.6
  0.7 0.0 copy-start.9
  0.7 0.0 copy-start.10
  0.7 0.0 copy-start.3
  0.7 0.0 copy-start.4
  0.7 2.4 %shard_map.184 = (bf16[768,256]{1,0:T(8,128)(2,1)S(1)}, bf16[144,256]{1,0:T(8,128)(2,1)S(1)}, bf16[144,256]{1,0:T(8,128)(2,1)S(1)}, bf16[144,256]{1,0:T(8,128)(2,1)S(1)}, f32[432,8]{1,0:T(8,128)S(1)}) custom-call(bf16[32,256]{1,0:T(8,128)(2,1)} %state_far.1, bf16[256,256]{1,0:T(8,128)(2,1)} %w_far.1, bf16[768,256]{1,0:T(8,128)(2,1)} %prev_far.1, s32[416]{0:T(512)} %send_far.1), custom_call_target="tpu_custom_call" | custom-call | tf_op jit(solution)/shard_map/pallas_call | solution.py:490
  3.1 1.5 %collective-permute-start = (bf16[144,256]{1,0:T(8,128)(2,1)S(1)}, bf16[144,256]{1,0:T(8,128)(2,1)S(1)}, u32[]{:S(2)}, u32[]{:S(2)}) collective-permute-start(bf16[144,256]{1,0:T(8,128)(2,1)S(1)} %get-tuple-element.47), channel_id=1, source_target_pairs={{0,96},{32,64},{64,32},{96,0},{1,97},{33,65},{65,33},{97,1},{2,98}... | collective-permute-start | bytes 221192 | tf_op jit(solution)/shard_map/ppermute | solution.py:611
  4.6 0.7 %collective-permute-start.1 = (bf16[144,256]{1,0:T(8,128)(2,1)S(1)}, bf16[144,256]{1,0:T(8,128)(2,1)S(1)}, u32[]{:S(2)}, u32[]{:S(2)}) collective-permute-start(bf16[144,256]{1,0:T(8,128)(2,1)S(1)} %get-tuple-element.49), channel_id=1, source_target_pairs={{0,32},{32,0},{64,96},{96,64},{1,33},{33,1},{65,97},{97,65},{2,34}... | collective-permute-start | bytes 221192 | tf_op jit(solution)/shard_map/ppermute | solution.py:611
  5.3 0.0 copy-start.2
  5.3 0.0 copy-done.7
  5.3 0.0 copy-done.8
  5.3 0.0 copy-start.12
  5.3 1.0 %shard_map.187 = (bf16[768,432]{1,0:T(8,128)(2,1)S(1)}, bf16[432,768]{1,0:T(8,128)(2,1)S(1)}, f32[32,432]{1,0:T(8,128)S(1)}) custom-call(s32[768]{0:T(1024)S(1)} %copy-done.7, s32[768]{0:T(1024)S(1)} %copy-done.8, f32[432,8]{1,0:T(8,128)S(1)} %get-tuple-element.64.where), custom_call_target="tpu_custom_call" | custom-call | tf_op jit(solution)/shard_map/pallas_call | solution.py:490
  6.3 0.0 copy-start
  6.3 1.0 %collective-permute-done = bf16[144,256]{1,0:T(8,128)(2,1)S(1)} collective-permute-done((bf16[144,256]{1,0:T(8,128)(2,1)S(1)}, bf16[144,256]{1,0:T(8,128)(2,1)S(1)}, u32[]{:S(2)}, u32[]{:S(2)}) %collective-permute-start) | collective-permute-done | bytes 73760 | tf_op jit(solution)/shard_map/ppermute | solution.py:611
  7.3 0.0 collective-permute-done.1
  7.3 0.0 copy-start.1
  7.3 3.3 %collective-permute-start.2 = (bf16[3,3,16,256]{3,2,1,0:T(8,128)(2,1)S(1)}, bf16[3,3,16,256]{3,2,1,0:T(8,128)(2,1)S(1)}, u32[]{:S(2)}, u32[]{:S(2)}) collective-permute-start(bf16[3,3,16,256]{3,2,1,0:T(8,128)(2,1)S(1)} %get-tuple-element.53), channel_id=1, source_target_pairs={{0,24},{8,16},{16,8},{24,0},{1,25},{9,17},{17,9},{25,1},{2,26},{10... | collective-permute-start | bytes 221192 | tf_op jit(solution)/shard_map/ppermute | solution.py:611
  10.6 0.1 collective-permute-start.3
  10.8 0.0 copy-done.5
  10.8 0.0 copy-done.6
  10.8 0.0 copy-done.9
  10.8 0.0 copy-done.10
  10.8 0.0 copy-done.12
  10.8 1.0 %shard_map.185 = (f32[768,256]{1,0:T(8,128)S(1)}, f32[768,128]{1,0:T(8,128)S(1)}, f32[72,768]{1,0:T(8,128)S(1)}, f32[8,768]{1,0:T(8,128)S(1)}, f32[72,256]{1,0:T(8,128)S(1)}) custom-call(f32[3,768]{1,0:T(4,128)S(1)} %copy-done.9, s32[768]{0:T(1024)S(1)} %copy-done.8, s32[768]{0:T(1024)S(1)} %copy-done.7, s32[32]{0:T(128)S(1)} %copy-done.12, ...), custom_call_target="tpu_custom_call" | custom-call | tf_op jit(solution)/shard_map/pallas_call | solution.py:490
  11.9 0.0 copy-done.3
  11.9 0.0 copy-done.4
  11.9 0.0 copy-done.2
  11.9 0.0 copy-done
  11.9 0.0 copy-done.1
  11.9 2.4 %shard_map.186 = (f32[96,256]{1,0:T(8,128)S(1)}, f32[4,96,256]{2,1,0:T(8,128)S(1)}, f32[2,96,768]{2,1,0:T(8,128)S(1)}, f32[2,96,512]{2,1,0:T(8,128)S(1)}, f32[2,...) custom-call(f32[768,256]{1,0:T(8,128)S(1)} %get-tuple-element.52.base, f32[768,128]{1,0:T(8,128)S(1)} %get-tuple-element.55.kwb, ...), custom_call_target="tpu_custom_call" | custom-call | tf_op jit(solution)/shard_map/pallas_call | solution.py:490
  14.3 0.0 collective-permute-done.2
  14.3 0.6 %collective-permute-done.3 = bf16[3,3,16,256]{3,2,1,0:T(8,128)(2,1)S(1)} collective-permute-done((bf16[3,3,16,256]{3,2,1,0:T(8,128)(2,1)S(1)}, bf16[3,3,16,256]{3,2,1,0:T(8,128)(2,1)S(1)}, u32[]{:S(2)}, u32[]{:S(2)}) %collective-permute-start.3) | collective-permute-done | bytes 73760 | tf_op jit(solution)/shard_map/ppermute | solution.py:611
  15.0 0.0 copy-start.11
  15.0 1.6 %collective-permute-start.5 = (bf16[3,3,16,256]{3,2,1,0:T(8,128)(2,1)S(1)}, bf16[3,3,16,256]{3,2,1,0:T(8,128)(2,1)S(1)}, u32[]{:S(2)}, u32[]{:S(2)}) collective-permute-start(bf16[3,3,16,256]{3,2,1,0:T(8,128)(2,1)S(1)} %pad_maximum_fusion.4), channel_id=1, source_target_pairs={{0,1},{1,0},{2,3},{3,2},{4,5},{5,4},{6,7},{7,6},{8,9},{9,8},{10,11... | collective-permute-start | bytes 221192 | tf_op jit(solution)/shard_map/ppermute | solution.py:611
  16.5 5.6 %collective-permute-start.4 = (bf16[3,3,16,256]{3,2,1,0:T(8,128)(2,1)S(1)}, bf16[3,3,16,256]{3,2,1,0:T(8,128)(2,1)S(1)}, u32[]{:S(2)}, u32[]{:S(2)}) collective-permute-start(bf16[3,3,16,256]{3,2,1,0:T(8,128)(2,1)S(1)} %pad_maximum_fusion.3), channel_id=1, source_target_pairs={{0,7},{1,2},{2,1},{3,4},{4,3},{5,6},{6,5},{7,0},{8,15},{9,10},{10,... | collective-permute-start | bytes 221192 | tf_op jit(solution)/shard_map/ppermute | solution.py:611
  22.2 0.0 copy-done.11
  22.2 2.9 %shard_map.188 = (f32[96,128]{1,0:T(8,128)S(1)}, f32[96,256]{1,0:T(8,128)S(1)}, f32[96,128]{1,0:T(8,128)S(1)}) custom-call(f32[96,256]{1,0:T(8,128)S(1)} %get-tuple-element.70.last.inner_last, f32[4,96,256]{2,1,0:T(8,128)S(1)} %get-tuple-element.71.xs, f32[2,96,768]{2,1,0:T(8,128)S(1)} %get-tuple-element.72.qkv, f32[2,96,512]{2,1,0:T(8,128)S(1)} %get-tuple-element.73.ups, ...), custom_call_target="tpu_custom_call" | custom-call | tf_op jit(solution)/shard_map/pallas_call | solution.py:490
  25.1 0.0 collective-permute-done.5
  25.1 0.0 collective-permute-done.4
  25.1 15.9 %shard_map.189 = (bf16[768,256]{1,0:T(8,128)(2,1)}, f32[1,768]{1,0:T(1,128)S(1)}, f32[8,768]{1,0:T(8,128)S(1)}, f32[8,144]{1,0:T(8,128)S(1)}, f32[8,144]{1,0:T(8,128)S(1)}, /*index=5*/f32[8,144]{1,0:T(8,128)S(1)}) custom-call(f32[768,256]{1,0:T(8,128)S(1)} %get-tuple-element.52.base, bf16[144,256]{1,0:T(8,128)(2,1)S(1)} %bitcast.23, ...), custom_call_target="tpu_custom_call" | custom-call | tf_op jit(solution)/shard_map/pallas_call | solution.py:490
  41.0 0.0 collective-permute-start.6
  41.0 1.8 %collective-permute-start.7 = (f32[8,144]{1,0:T(8,128)S(1)}, f32[8,144]{1,0:T(8,128)S(1)}, u32[]{:S(2)}, u32[]{:S(2)}) collective-permute-start(f32[8,144]{1,0:T(8,128)S(1)} %get-tuple-element.82), channel_id=1, source_target_pairs={{0,32},{32,0},{64,96},{96,64},{1,33},{33,1},{65,97},{97,65},{2,34}... | collective-permute-start | bytes 13832 | tf_op jit(solution)/shard_map/ppermute | solution.py:611
  42.8 1.3 %collective-permute-done.6 = f32[8,144]{1,0:T(8,128)S(1)} collective-permute-done((f32[8,144]{1,0:T(8,128)S(1)}, f32[8,144]{1,0:T(8,128)S(1)}, u32[]{:S(2)}, u32[]{:S(2)}) %collective-permute-start.6) | collective-permute-done | bytes 4640 | tf_op jit(solution)/shard_map/ppermute | solution.py:611
  44.1 0.0 collective-permute-done.7
  44.1 0.1 fusion.7
  44.2 1.3 %collective-permute-start.8 = (f32[3,8,48]{2,1,0:T(8,128)S(1)}, f32[3,8,48]{2,1,0:T(8,128)S(1)}, u32[]{:S(2)}, u32[]{:S(2)}) collective-permute-start(f32[3,8,48]{2,1,0:T(8,128)S(1)} %get-tuple-element.112), channel_id=1, source_target_pairs={{0,24},{8,16},{16,8},{24,0},{1,25},{9,17},{17,9},{25,1},{2,26},{10... | collective-permute-start | bytes 13832 | tf_op jit(solution)/shard_map/ppermute | solution.py:611
  45.4 0.1 collective-permute-start.9
  45.5 3.6 %collective-permute-done.8 = f32[3,8,48]{2,1,0:T(8,128)S(1)} collective-permute-done((f32[3,8,48]{2,1,0:T(8,128)S(1)}, f32[3,8,48]{2,1,0:T(8,128)S(1)}, u32[]{:S(2)}, u32[]{:S(2)}) %collective-permute-start.8) | collective-permute-done | bytes 4640 | tf_op jit(solution)/shard_map/ppermute | solution.py:611
  49.1 0.0 collective-permute-done.9
  49.1 0.1 fusion.6
  49.2 5.1 %collective-permute-start.10 = (f32[3,3,8,16]{3,2,1,0:T(8,128)S(1)}, f32[3,3,8,16]{3,2,1,0:T(8,128)S(1)}, u32[]{:S(2)}, u32[]{:S(2)}) collective-permute-start(f32[3,3,8,16]{3,2,1,0:T(8,128)S(1)} %get-tuple-element.89), channel_id=1, source_target_pairs={{0,7},{1,2},{2,1},{3,4},{4,3},{5,6},{6,5},{7,0},{8,15},{9,10},{10,... | collective-permute-start | bytes 13832 | tf_op jit(solution)/shard_map/ppermute | solution.py:611
  54.3 0.0 collective-permute-start.11
  54.3 1.2 %shard_map.190 = (f32[8,32]{1,0:T(8,128)S(1)}, f32[1,32]{1,0:T(1,128)}) custom-call(f32[8,768]{1,0:T(8,128)S(1)} %get-tuple-element.84.grad, s32[768]{0:T(1024)S(1)} %copy-done.7, f32[8,768]{1,0:T(8,128)S(1)} %get-tuple-element.67.rows, f32[1,768]{1,0:T(1,128)S(1)} %get-tuple-element.85.reads), custom_call_target="tpu_custom_call" | custom-call | tf_op jit(solution)/shard_map/pallas_call | solution.py:490
  55.5 1.4 %collective-permute-done.10.r = f32[3,3,8,16]{3,2,1,0:T(8,128)S(1)} collective-permute-done((f32[3,3,8,16]{3,2,1,0:T(8,128)S(1)}, f32[3,3,8,16]{3,2,1,0:T(8,128)S(1)}, u32[]{:S(2)}, u32[]{:S(2)}) %collective-permute-start.10) | collective-permute-done | bytes 4640 | tf_op jit(solution)/shard_map/ppermute | solution.py:611
  56.9 1.4 %collective-permute-done.11.l = f32[3,3,8,16]{3,2,1,0:T(8,128)S(1)} collective-permute-done((f32[3,3,8,16]{3,2,1,0:T(8,128)S(1)}, f32[3,3,8,16]{3,2,1,0:T(8,128)S(1)}, u32[]{:S(2)}, u32[]{:S(2)}) %collective-permute-start.11) | collective-permute-done | bytes 4640 | tf_op jit(solution)/shard_map/ppermute | solution.py:611
  58.2 0.8 %shard_map.191 = f32[3,32]{1,0:T(4,128)} custom-call(f32[8,32]{1,0:T(8,128)S(1)} %get-tuple-element.87.partial, f32[32,432]{1,0:T(8,128)S(1)} %get-tuple-element.88.mt, f32[3,3,8,16]{3,2,1,0:T(8,128)S(1)} %collective-permute-done.10.r, f32[3,3,8,16]{3,2,1,0:T(8,128)S(1)} %get-tuple-element.109.m, f32[3,3,8,16]{3,2,1,0:T(8,128)S(1)} %collective-permute-done.11.l), custom_call_target="tpu_custom_call" | custom-call | tf_op jit(solution)/shard_map/pallas_call | solution.py:490
  (13 shorter events, 0.1 us)
Async XLA Ops:
  0.6 4.7 %copy-start.7 = (s32[768]{0:T(1024)S(1)}, s32[768]{0:T(1024)}, u32[]{:S(2)}) copy-start(s32[768]{0:T(1024)} %slot.5) | copy-start | bytes 9220
  0.6 4.7 %copy-start.8 = (s32[768]{0:T(1024)S(1)}, s32[768]{0:T(1024)}, u32[]{:S(2)}) copy-start(s32[768]{0:T(1024)} %mask.3) | copy-start | bytes 9220
  0.7 10.1 %copy-start.5 = (f32[64,256]{1,0:T(8,128)S(1)}, f32[64,256]{1,0:T(8,128)}, u32[]{:S(2)}) copy-start(f32[64,256]{1,0:T(8,128)} %w_rbf.1) | copy-start | bytes 196612
  0.7 10.1 %copy-start.6 = (bf16[85,256]{1,0:T(8,128)(2,1)S(1)}, bf16[85,256]{1,0:T(8,128)(2,1)}, u32[]{:S(2)}) copy-start(bf16[85,256]{1,0:T(8,128)(2,1)} %table.1) | copy-start | bytes 130564
  0.7 10.1 %copy-start.9 = (f32[3,768]{1,0:T(4,128)S(1)}, f32[3,768]{1,0:T(4,128)}, u32[]{:S(2)}) copy-start(f32[3,768]{1,0:T(4,128)} %disp) | copy-start | bytes 27652
  0.7 10.1 %copy-start.10 = (f32[3,256]{1,0:T(4,128)S(1)}, f32[3,256]{1,0:T(4,128)}, u32[]{:S(2)}) copy-start(f32[3,256]{1,0:T(4,128)} %w_vec.1) | copy-start | bytes 9220
  0.7 11.2 %copy-start.3 = (bf16[2,256,256]{2,1,0:T(8,128)(2,1)S(1)}, bf16[2,256,256]{2,1,0:T(8,128)(2,1)}, u32[]{:S(2)}) copy-start(bf16[2,256,256]{2,1,0:T(8,128)(2,1)} %w_out.5) | copy-start | bytes 786436
  0.7 11.2 %copy-start.4 = (f32[5,256]{1,0:T(8,128)S(1)}, f32[5,256]{1,0:T(8,128)}, u32[]{:S(2)}) copy-start(f32[5,256]{1,0:T(8,128)} %gains.5) | copy-start | bytes 15364
  3.1 4.2 %collective-permute-start = (bf16[144,256]{1,0:T(8,128)(2,1)S(1)}, bf16[144,256]{1,0:T(8,128)(2,1)S(1)}, u32[]{:S(2)}, u32[]{:S(2)}) collective-permute-start(bf16[144,256]{1,0:T(8,128)(2,1)S(1)} %get-tuple-element.47), channel_id=1, source_target_pairs={{0,96},{32,64},{64,32},{96,0},{1,97},{33,65},{65,33},{97,1},{2,98}... | collective-permute-start | bytes 221192 | tf_op jit(solution)/shard_map/ppermute | solution.py:611
  4.6 2.7 %collective-permute-start.1 = (bf16[144,256]{1,0:T(8,128)(2,1)S(1)}, bf16[144,256]{1,0:T(8,128)(2,1)S(1)}, u32[]{:S(2)}, u32[]{:S(2)}) collective-permute-start(bf16[144,256]{1,0:T(8,128)(2,1)S(1)} %get-tuple-element.49), channel_id=1, source_target_pairs={{0,32},{32,0},{64,96},{96,64},{1,33},{33,1},{65,97},{97,65},{2,34}... | collective-permute-start | bytes 221192 | tf_op jit(solution)/shard_map/ppermute | solution.py:611
  5.3 6.6 %copy-start.2 = (bf16[2,512,256]{2,1,0:T(8,128)(2,1)S(1)}, bf16[2,512,256]{2,1,0:T(8,128)(2,1)}, u32[]{:S(2)}) copy-start(bf16[2,512,256]{2,1,0:T(8,128)(2,1)} %w_down.5) | copy-start | bytes 1572868
  5.3 5.5 %copy-start.12 = (s32[32]{0:T(128)S(1)}, s32[32]{0:T(128)}, u32[]{:S(2)}) copy-start(s32[32]{0:T(128)} %species.1) | copy-start | bytes 388
  6.3 5.6 %copy-start = (bf16[2,256,768]{2,1,0:T(8,128)(2,1)S(1)}, bf16[2,256,768]{2,1,0:T(8,128)(2,1)}, u32[]{:S(2)}) copy-start(bf16[2,256,768]{2,1,0:T(8,128)(2,1)} %w_qkv.5) | copy-start | bytes 2359300
  7.3 4.6 %copy-start.1 = (bf16[2,256,512]{2,1,0:T(8,128)(2,1)S(1)}, bf16[2,256,512]{2,1,0:T(8,128)(2,1)}, u32[]{:S(2)}) copy-start(bf16[2,256,512]{2,1,0:T(8,128)(2,1)} %w_up.5) | copy-start | bytes 1572868
  7.3 7.0 %collective-permute-start.2 = (bf16[3,3,16,256]{3,2,1,0:T(8,128)(2,1)S(1)}, bf16[3,3,16,256]{3,2,1,0:T(8,128)(2,1)S(1)}, u32[]{:S(2)}, u32[]{:S(2)}) collective-permute-start(bf16[3,3,16,256]{3,2,1,0:T(8,128)(2,1)S(1)} %get-tuple-element.53), channel_id=1, source_target_pairs={{0,24},{8,16},{16,8},{24,0},{1,25},{9,17},{17,9},{25,1},{2,26},{10... | collective-permute-start | bytes 221192 | tf_op jit(solution)/shard_map/ppermute | solution.py:611
  10.6 4.4 %collective-permute-start.3 = (bf16[3,3,16,256]{3,2,1,0:T(8,128)(2,1)S(1)}, bf16[3,3,16,256]{3,2,1,0:T(8,128)(2,1)S(1)}, u32[]{:S(2)}, u32[]{:S(2)}) collective-permute-start(bf16[3,3,16,256]{3,2,1,0:T(8,128)(2,1)S(1)} %get-tuple-element.54), channel_id=1, source_target_pairs={{0,8},{8,0},{16,24},{24,16},{1,9},{9,1},{17,25},{25,17},{2,10},{10... | collective-permute-start | bytes 221192 | tf_op jit(solution)/shard_map/ppermute | solution.py:611
  15.0 7.2 %copy-start.11 = (f32[256]{0:T(256)S(1)}, f32[256]{0:T(256)}, u32[]{:S(2)}) copy-start(f32[256]{0:T(256)} %param.33) | copy-start | bytes 3076
  15.0 10.1 %collective-permute-start.5 = (bf16[3,3,16,256]{3,2,1,0:T(8,128)(2,1)S(1)}, bf16[3,3,16,256]{3,2,1,0:T(8,128)(2,1)S(1)}, u32[]{:S(2)}, u32[]{:S(2)}) collective-permute-start(bf16[3,3,16,256]{3,2,1,0:T(8,128)(2,1)S(1)} %pad_maximum_fusion.4), channel_id=1, source_target_pairs={{0,1},{1,0},{2,3},{3,2},{4,5},{5,4},{6,7},{7,6},{8,9},{9,8},{10,11... | collective-permute-start | bytes 221192 | tf_op jit(solution)/shard_map/ppermute | solution.py:611
  16.5 8.6 %collective-permute-start.4 = (bf16[3,3,16,256]{3,2,1,0:T(8,128)(2,1)S(1)}, bf16[3,3,16,256]{3,2,1,0:T(8,128)(2,1)S(1)}, u32[]{:S(2)}, u32[]{:S(2)}) collective-permute-start(bf16[3,3,16,256]{3,2,1,0:T(8,128)(2,1)S(1)} %pad_maximum_fusion.3), channel_id=1, source_target_pairs={{0,7},{1,2},{2,1},{3,4},{4,3},{5,6},{6,5},{7,0},{8,15},{9,10},{10,... | collective-permute-start | bytes 221192 | tf_op jit(solution)/shard_map/ppermute | solution.py:611
  41.0 3.1 %collective-permute-start.6 = (f32[8,144]{1,0:T(8,128)S(1)}, f32[8,144]{1,0:T(8,128)S(1)}, u32[]{:S(2)}, u32[]{:S(2)}) collective-permute-start(f32[8,144]{1,0:T(8,128)S(1)} %get-tuple-element.80), channel_id=1, source_target_pairs={{0,96},{32,64},{64,32},{96,0},{1,97},{33,65},{65,33},{97,1},{2,98}... | collective-permute-start | bytes 13832 | tf_op jit(solution)/shard_map/ppermute | solution.py:611
  41.0 3.1 %collective-permute-start.7 = (f32[8,144]{1,0:T(8,128)S(1)}, f32[8,144]{1,0:T(8,128)S(1)}, u32[]{:S(2)}, u32[]{:S(2)}) collective-permute-start(f32[8,144]{1,0:T(8,128)S(1)} %get-tuple-element.82), channel_id=1, source_target_pairs={{0,32},{32,0},{64,96},{96,64},{1,33},{33,1},{65,97},{97,65},{2,34}... | collective-permute-start | bytes 13832 | tf_op jit(solution)/shard_map/ppermute | solution.py:611
  44.2 4.9 %collective-permute-start.8 = (f32[3,8,48]{2,1,0:T(8,128)S(1)}, f32[3,8,48]{2,1,0:T(8,128)S(1)}, u32[]{:S(2)}, u32[]{:S(2)}) collective-permute-start(f32[3,8,48]{2,1,0:T(8,128)S(1)} %get-tuple-element.112), channel_id=1, source_target_pairs={{0,24},{8,16},{16,8},{24,0},{1,25},{9,17},{17,9},{25,1},{2,26},{10... | collective-permute-start | bytes 13832 | tf_op jit(solution)/shard_map/ppermute | solution.py:611
  45.4 3.7 %collective-permute-start.9 = (f32[3,8,48]{2,1,0:T(8,128)S(1)}, f32[3,8,48]{2,1,0:T(8,128)S(1)}, u32[]{:S(2)}, u32[]{:S(2)}) collective-permute-start(f32[3,8,48]{2,1,0:T(8,128)S(1)} %get-tuple-element.113), channel_id=1, source_target_pairs={{0,8},{8,0},{16,24},{24,16},{1,9},{9,1},{17,25},{25,17},{2,10},{10... | collective-permute-start | bytes 13832 | tf_op jit(solution)/shard_map/ppermute | solution.py:611
  49.2 7.7 %collective-permute-start.10 = (f32[3,3,8,16]{3,2,1,0:T(8,128)S(1)}, f32[3,3,8,16]{3,2,1,0:T(8,128)S(1)}, u32[]{:S(2)}, u32[]{:S(2)}) collective-permute-start(f32[3,3,8,16]{3,2,1,0:T(8,128)S(1)} %get-tuple-element.89), channel_id=1, source_target_pairs={{0,7},{1,2},{2,1},{3,4},{4,3},{5,6},{6,5},{7,0},{8,15},{9,10},{10,... | collective-permute-start | bytes 13832 | tf_op jit(solution)/shard_map/ppermute | solution.py:611
  54.3 4.0 %collective-permute-start.11 = (f32[3,3,8,16]{3,2,1,0:T(8,128)S(1)}, f32[3,3,8,16]{3,2,1,0:T(8,128)S(1)}, u32[]{:S(2)}, u32[]{:S(2)}) collective-permute-start(f32[3,3,8,16]{3,2,1,0:T(8,128)S(1)} %get-tuple-element.90), channel_id=1, source_target_pairs={{0,1},{1,0},{2,3},{3,2},{4,5},{5,4},{6,7},{7,6},{8,9},{9,8},{10,11... | collective-permute-start | bytes 13832 | tf_op jit(solution)/shard_map/ppermute | solution.py:611

commit v6 on v5

--- a/solution.py
+++ b/solution.py
@@ -193,9 +193,21 @@
     return lax.rsqrt(jnp.mean(x * x, axis=-1, keepdims=True) + norm_eps)
 
 
-def rms_back(x, r, z):
-    inner = jnp.mean(x * z, axis=-1, keepdims=True)
-    return r * z - x * (r * r * r * inner)
+def rms_all(x, blocks, xs, rs, gains, place):
+    gain = gains[place : place + 1, :]
+    out = []
+    for b, v in zip(blocks, x):
+        r = rms_factor(v)
+        scaled = v * r
+        xs[place, b, :] = scaled
+        rs[place, b, :] = jnp.broadcast_to(r, (v.shape[0], 128))
+        out.append((scaled * gain).astype(BF))
+    return out
+
+
+def rms_back(scaled, r, z):
+    inner = jnp.mean(scaled * z, axis=-1, keepdims=True)
+    return jnp.concatenate([r, r], axis=1) * (z - scaled * inner)
 
 
 LIMIT = 36 * 2**20
@@ -232,16 +244,13 @@
     return out
 
 
-def forward(x, blocks, offset, kwb, gains, w_qkv, w_out, w_up, w_down, xs, qkv, ups, probs, slope, att):
+def forward(x, blocks, offset, kwb, gains, w_qkv, w_out, w_up, w_down, xs, rs, qkv, ups, probs, slope, att):
     edges = blocks[-1].stop
     score_scale = 1.0 / (math.sqrt(D // HEADS) * score_cap)
     slope_scale = 1.0 / math.sqrt(D // HEADS)
     at = [(s, 128 * g) for s in atom_spans(edges) for g in range(2)]
     for layer in range(2):
-        for b, v in zip(blocks, x):
-            xs[2 * layer, b, :] = v
-        gain = gains[2 * layer : 2 * layer + 1, :]
-        normed = [(v * rms_factor(v) * gain).astype(BF) for v in x]
+        normed = rms_all(x, blocks, xs, rs, gains, 2 * layer)
         for b, v in zip(blocks, normed):
             qkv[layer, b, :] = dot_nn(v, w_qkv[layer])
         q = [spread(qkv[layer, s, c : c + 128]) for s, c in at]
@@ -257,21 +266,19 @@
             probs[layer, s, c : c + 128] = p[i]
             slope[layer, s, c : c + 128] = (1.0 - t[i] * t[i]) * slope_scale
             att[s, c : c + 128] = o[i]
-        x = [xs[2 * layer, b, :] + dot_nn(att[b, :].astype(BF), w_out[layer]) for b in blocks]
-        for b, v in zip(blocks, x):
-            xs[2 * layer + 1, b, :] = v
-        gain = gains[2 * layer + 1 : 2 * layer + 2, :]
-        normed = [(v * rms_factor(v) * gain).astype(BF) for v in x]
+        x = [v + dot_nn(att[b, :].astype(BF), w_out[layer]) for b, v in zip(blocks, x)]
+        normed = rms_all(x, blocks, xs, rs, gains, 2 * layer + 1)
         up = [dot_nn(v, w_up[layer]) for v in normed]
-        for b, v in zip(blocks, up):
-            ups[layer, b, :] = v
-        hidden = [(u * sigmoid(u)).astype(BF) for u in up]
-        x = [v + dot_nn(h, w_down[layer]) for v, h in zip(x, hidden)]
+        sig = [sigmoid(u) for u in up]
+        hidden = [u * s for u, s in zip(up, sig)]
+        for b, s, h in zip(blocks, sig, hidden):
+            ups[layer, b, :] = s + h * (1.0 - s)
+        x = [v + dot_nn(h.astype(BF), w_down[layer]) for v, h in zip(x, hidden)]
     return x
 
 
 def backward(
-    x, blocks, offset, kwb, gains, w_energy, w_qkv, w_out, w_up, w_down, xs, qkv, ups, probs, slope, att, dqkv, acc
+    x, blocks, offset, kwb, gains, w_energy, w_qkv, w_out, w_up, w_down, xs, rs, qkv, ups, probs, slope, att, dqkv, acc
 ):
     edges = blocks[-1].stop
     spans = atom_spans(edges)
@@ -288,17 +295,12 @@
         dx.append((kwb[shifted(b, offset), 0:1] * r) * (read - scaled * total))
     for layer in (1, 0):
         dhid = [dot_nt(v.astype(BF), w_down[layer]) for v in dx]
-        dup = []
-        for b, dh in zip(blocks, dhid):
-            u = ups[layer, b, :]
-            sig = sigmoid(u)
-            dup.append((dh * (sig * (1.0 + u * (1.0 - sig)))).astype(BF))
+        dup = [(dh * ups[layer, b, :]).astype(BF) for b, dh in zip(blocks, dhid)]
         gain = gains[2 * layer + 1 : 2 * layer + 2, :]
         dnorm = [dot_nt(v, w_up[layer]) * gain for v in dup]
         new = []
         for b, v, dn in zip(blocks, dx, dnorm):
-            xv = xs[2 * layer + 1, b, :]
-            new.append(v + rms_back(xv, rms_factor(xv), dn))
+            new.append(v + rms_back(xs[2 * layer + 1, b, :], rs[2 * layer + 1, b, :], dn))
         dx = new
         for b, v in zip(blocks, dx):
             att[b, :] = dot_nt(v.astype(BF), w_out[layer])
@@ -324,24 +326,23 @@
         dnorm = [dot_nt(dqkv[b, :].astype(BF), w_qkv[layer]) * gain for b in blocks]
         new = []
         for b, v, dn in zip(blocks, dx, dnorm):
-            xv = xs[2 * layer, b, :]
-            new.append(v + rms_back(xv, rms_factor(xv), dn))
+            new.append(v + rms_back(xs[2 * layer, b, :], rs[2 * layer, b, :], dn))
         dx = new
     return readout, dx
 
 
 def inner_forward_kernel(
-    base, kwb, gains, w_qkv, w_out, w_up, w_down, last, xs, qkv, ups, probs, slope, att
+    base, kwb, gains, w_qkv, w_out, w_up, w_down, last, xs, rs, qkv, ups, probs, slope, att
 ):
     blocks = block_list(INNER, 1)
     x = forward(
-        [base[0:INNER, :]], blocks, 0, kwb, gains, w_qkv, w_out, w_up, w_down, xs, qkv, ups, probs, slope, att
+        [base[0:INNER, :]], blocks, 0, kwb, gains, w_qkv, w_out, w_up, w_down, xs, rs, qkv, ups, probs, slope, att
     )
     last[...] = x[0]
 
 
 def inner_backward_kernel(
-    last, xs, qkv, ups, probs, slope, kwb, gains, w_energy, w_qkv, w_out, w_up, w_down, terms, dx, acc, att, dqkv
+    last, xs, rs, qkv, ups, probs, slope, kwb, gains, w_energy, w_qkv, w_out, w_up, w_down, terms, dx, acc, att, dqkv
 ):
     blocks = block_list(INNER, 1)
     readout, out = backward(
@@ -356,6 +357,7 @@
         w_up,
         w_down,
         xs,
+        rs,
         qkv,
         ups,
         probs,
@@ -396,6 +398,7 @@
     mid,
     high,
     xs,
+    rs,
     qkv,
     ups,
     probs,
@@ -404,13 +407,13 @@
     dqkv,
     acc,
 ):
-    blocks = block_list(OUTER, 2)
+    blocks = block_list(OUTER, 3)
     arrived = jnp.concatenate([arr_r[...], arr_m[...], arr_l[...]], axis=0)
     x = []
     for b in blocks:
         here = shifted(b, INNER)
         x.append(base[here, :] + dot_nn(far[here, :], arrived))
-    stores = (xs, qkv, ups, probs, slope, att)
+    stores = (xs, rs, qkv, ups, probs, slope, att)
     weights = (w_qkv, w_out, w_up, w_down)
     x = forward(x, blocks, INNER, kwb, gains, *weights, *stores)
     tokens[0:INNER, :] = inner_last[...].astype(BF)
@@ -420,7 +423,6 @@
 
     w = wfeat[...]
     whi = w.astype(BF)
-    wlo = (w - whi.astype(F32)).astype(BF)
     ones8 = jnp.ones((8, 128), BF)
 
     def to_row(parts):
@@ -428,7 +430,8 @@
         return (dot_nt(ones8, hi) + dot_nt(ones8, lo))[0:1]
 
     hi, lo = split2(jnp.concatenate([inner_dx[...]] + dx, axis=0))
-    back = dot_nt(whi, hi) + dot_nt(whi, lo) + dot_nt(wlo, hi)
+    pair = dot_nt(jnp.concatenate([w.astype(BF).astype(F32), w - whi.astype(F32)], axis=0).astype(BF), hi)
+    back = pair[0:NFEAT] + pair[NFEAT : 2 * NFEAT] + dot_nt(whi, lo)
     readout = to_row([inner_terms[...]] + terms)
     reads[...] = readout
     acc_row = to_row([inner_acc[...], acc[...]])
@@ -551,6 +554,7 @@
 def inner_stores(n):
     return [
         shape((4, n, D)),
+        shape((4, n, 128)),
         shape((2, n, 3 * D)),
         shape((2, n, FF)),
         shape((2, n, D)),

time: 59.1 us -> 59.4 us (level)
  starting transfers between devices: 21 us -> 22.3 us
    ppermute x12, starting transfers between devices: 21 us -> 22.3 us  [exchange(): return (lax.ppermute(low, axis, outer), lax.ppermute(high, axis, inner))]
where the time goes in v6:
time: 59.4 us; the launch traced here: 59.3 us
  Pallas kernels  27.1 us (46%)
  starting transfers between devices  22.3 us (38%)
  waiting for transfers between devices  8.67 us (15%)
  between operations  0.97 us (2%)
    pallas_call x8, Pallas kernels, vmem_call(): pl.pallas_call(kernel, out_shape=outs, in_specs=[pl.BlockSpec(memory_spac...  27.1 us
    ppermute x12, starting transfers between devices, exchange(): return (lax.ppermute(low, axis, outer), lax.ppermute(high, axis, inner))  22.3 us
    ppermute x12, waiting for transfers between devices, exchange(): return (lax.ppermute(low, axis, outer), lax.ppermute(high, axis, inner))  8.67 us
  transfers between devices with their start and end apart: 12, of which 6 were waited for; matrix products, arithmetic and copies ran while one was open for 0% of the time, Pallas kernels for 14%

profile of v6, /device:TPU:0, one launch (start us, length us, event | category | flops | bytes accessed | tf_op | source)
XLA Modules:
  0.0 59.3 jit_solution(7901272833583176852)
XLA Ops:
  0.6 0.0 copy-start.7
  0.6 0.0 copy-start.8
  0.7 0.0 copy-start.5
  0.7 0.0 copy-start.6
  0.7 0.0 copy-start.9
  0.7 0.0 copy-start.10
  0.7 0.0 copy-start.3
  0.7 0.0 copy-start.4
  0.7 2.4 %shard_map.184 = (bf16[768,256]{1,0:T(8,128)(2,1)S(1)}, bf16[144,256]{1,0:T(8,128)(2,1)S(1)}, bf16[144,256]{1,0:T(8,128)(2,1)S(1)}, bf16[144,256]{1,0:T(8,128)(2,1)S(1)}, f32[432,8]{1,0:T(8,128)S(1)}) custom-call(bf16[32,256]{1,0:T(8,128)(2,1)} %state_far.1, bf16[256,256]{1,0:T(8,128)(2,1)} %w_far.1, bf16[768,256]{1,0:T(8,128)(2,1)} %prev_far.1, s32[416]{0:T(512)} %send_far.1), custom_call_target="tpu_custom_call" | custom-call | tf_op jit(solution)/shard_map/pallas_call | solution.py:493
  3.1 1.5 %collective-permute-start = (bf16[144,256]{1,0:T(8,128)(2,1)S(1)}, bf16[144,256]{1,0:T(8,128)(2,1)S(1)}, u32[]{:S(2)}, u32[]{:S(2)}) collective-permute-start(bf16[144,256]{1,0:T(8,128)(2,1)S(1)} %get-tuple-element.49), channel_id=1, source_target_pairs={{0,96},{32,64},{64,32},{96,0},{1,97},{33,65},{65,33},{97,1},{2,98}... | collective-permute-start | bytes 221192 | tf_op jit(solution)/shard_map/ppermute | solution.py:615
  4.6 0.7 %collective-permute-start.1 = (bf16[144,256]{1,0:T(8,128)(2,1)S(1)}, bf16[144,256]{1,0:T(8,128)(2,1)S(1)}, u32[]{:S(2)}, u32[]{:S(2)}) collective-permute-start(bf16[144,256]{1,0:T(8,128)(2,1)S(1)} %get-tuple-element.51), channel_id=1, source_target_pairs={{0,32},{32,0},{64,96},{96,64},{1,33},{33,1},{65,97},{97,65},{2,34}... | collective-permute-start | bytes 221192 | tf_op jit(solution)/shard_map/ppermute | solution.py:615
  5.3 0.0 copy-start.2
  5.3 0.0 copy-done.7
  5.3 0.0 copy-done.8
  5.3 0.0 copy-start.12
  5.3 1.0 %shard_map.187 = (bf16[768,432]{1,0:T(8,128)(2,1)S(1)}, bf16[432,768]{1,0:T(8,128)(2,1)S(1)}, f32[32,432]{1,0:T(8,128)S(1)}) custom-call(s32[768]{0:T(1024)S(1)} %copy-done.7, s32[768]{0:T(1024)S(1)} %copy-done.8, f32[432,8]{1,0:T(8,128)S(1)} %get-tuple-element.67.where), custom_call_target="tpu_custom_call" | custom-call | tf_op jit(solution)/shard_map/pallas_call | solution.py:493
  6.3 0.0 copy-start
  6.3 1.0 %collective-permute-done = bf16[144,256]{1,0:T(8,128)(2,1)S(1)} collective-permute-done((bf16[144,256]{1,0:T(8,128)(2,1)S(1)}, bf16[144,256]{1,0:T(8,128)(2,1)S(1)}, u32[]{:S(2)}, u32[]{:S(2)}) %collective-permute-start) | collective-permute-done | bytes 73760 | tf_op jit(solution)/shard_map/ppermute | solution.py:615
  7.3 0.0 collective-permute-done.1
  7.3 0.0 copy-start.1
  7.3 1.8 %collective-permute-start.3 = (bf16[3,3,16,256]{3,2,1,0:T(8,128)(2,1)S(1)}, bf16[3,3,16,256]{3,2,1,0:T(8,128)(2,1)S(1)}, u32[]{:S(2)}, u32[]{:S(2)}) collective-permute-start(bf16[3,3,16,256]{3,2,1,0:T(8,128)(2,1)S(1)} %get-tuple-element.56), channel_id=1, source_target_pairs={{0,8},{8,0},{16,24},{24,16},{1,9},{9,1},{17,25},{25,17},{2,10},{10... | collective-permute-start | bytes 221192 | tf_op jit(solution)/shard_map/ppermute | solution.py:615
  9.1 2.2 %collective-permute-start.2 = (bf16[3,3,16,256]{3,2,1,0:T(8,128)(2,1)S(1)}, bf16[3,3,16,256]{3,2,1,0:T(8,128)(2,1)S(1)}, u32[]{:S(2)}, u32[]{:S(2)}) collective-permute-start(bf16[3,3,16,256]{3,2,1,0:T(8,128)(2,1)S(1)} %get-tuple-element.55), channel_id=1, source_target_pairs={{0,24},{8,16},{16,8},{24,0},{1,25},{9,17},{17,9},{25,1},{2,26},{10... | collective-permute-start | bytes 221192 | tf_op jit(solution)/shard_map/ppermute | solution.py:615
  11.4 0.0 copy-done.5
  11.4 0.0 copy-done.6
  11.4 0.0 copy-done.9
  11.4 0.0 copy-done.10
  11.4 0.0 copy-done.12
  11.4 1.0 %shard_map.185 = (f32[768,256]{1,0:T(8,128)S(1)}, f32[768,128]{1,0:T(8,128)S(1)}, f32[72,768]{1,0:T(8,128)S(1)}, f32[8,768]{1,0:T(8,128)S(1)}, f32[72,256]{1,0:T(8,128)S(1)}) custom-call(f32[3,768]{1,0:T(4,128)S(1)} %copy-done.9, s32[768]{0:T(1024)S(1)} %copy-done.8, s32[768]{0:T(1024)S(1)} %copy-done.7, s32[32]{0:T(128)S(1)} %copy-done.12, ...), custom_call_target="tpu_custom_call" | custom-call | tf_op jit(solution)/shard_map/pallas_call | solution.py:493
  12.5 0.0 copy-done.3
  12.5 0.0 copy-done.4
  12.5 0.0 copy-done.2
  12.5 0.0 copy-done
  12.5 0.0 copy-done.1
  12.5 2.4 %shard_map.186 = (f32[96,256]{1,0:T(8,128)S(1)}, f32[4,96,256]{2,1,0:T(8,128)S(1)}, f32[4,96,128]{2,1,0:T(8,128)S(1)}, f32[2,96,768]{2,1,0:T(8,128)S(1)}, f32[2,...) custom-call(f32[768,256]{1,0:T(8,128)S(1)} %get-tuple-element.54.base, ...), custom_call_target="tpu_custom_call" | custom-call | tf_op jit(solution)/shard_map/pallas_call | solution.py:493
  14.9 0.0 collective-permute-done.3
  14.9 0.0 collective-permute-done.2
  15.0 0.0 copy-start.11
  15.0 1.6 %collective-permute-start.5 = (bf16[3,3,16,256]{3,2,1,0:T(8,128)(2,1)S(1)}, bf16[3,3,16,256]{3,2,1,0:T(8,128)(2,1)S(1)}, u32[]{:S(2)}, u32[]{:S(2)}) collective-permute-start(bf16[3,3,16,256]{3,2,1,0:T(8,128)(2,1)S(1)} %pad_maximum_fusion.4), channel_id=1, source_target_pairs={{0,1},{1,0},{2,3},{3,2},{4,5},{5,4},{6,7},{7,6},{8,9},{9,8},{10,11... | collective-permute-start | bytes 221192 | tf_op jit(solution)/shard_map/ppermute | solution.py:615
  16.5 5.6 %collective-permute-start.4 = (bf16[3,3,16,256]{3,2,1,0:T(8,128)(2,1)S(1)}, bf16[3,3,16,256]{3,2,1,0:T(8,128)(2,1)S(1)}, u32[]{:S(2)}, u32[]{:S(2)}) collective-permute-start(bf16[3,3,16,256]{3,2,1,0:T(8,128)(2,1)S(1)} %pad_maximum_fusion.3), channel_id=1, source_target_pairs={{0,7},{1,2},{2,1},{3,4},{4,3},{5,6},{6,5},{7,0},{8,15},{9,10},{10,... | collective-permute-start | bytes 221192 | tf_op jit(solution)/shard_map/ppermute | solution.py:615
  22.1 0.0 copy-done.11
  22.2 2.9 %shard_map.188 = (f32[96,128]{1,0:T(8,128)S(1)}, f32[96,256]{1,0:T(8,128)S(1)}, f32[96,128]{1,0:T(8,128)S(1)}) custom-call(f32[96,256]{1,0:T(8,128)S(1)} %get-tuple-element.73.last.inner_last, f32[4,96,256]{2,1,0:T(8,128)S(1)} %get-tuple-element.74.xs, f32[4,96,128]{2,1,0:T(8,128)S(1)} %get-tuple-element.75.rs, f32[2,96,768]{2,1,0:T(8,128)S(1)} %get-tuple-element.76.qkv, ...), custom_call_target="tpu_custom_call" | custom-call | tf_op jit(solution)/shard_map/pallas_call | solution.py:493
  25.1 0.0 collective-permute-done.5
  25.1 0.0 collective-permute-done.4
  25.1 15.4 %shard_map.189 = (bf16[768,256]{1,0:T(8,128)(2,1)}, f32[1,768]{1,0:T(1,128)S(1)}, f32[8,768]{1,0:T(8,128)S(1)}, f32[8,144]{1,0:T(8,128)S(1)}, f32[8,144]{1,0:T(8,128)S(1)}, /*index=5*/f32[8,144]{1,0:T(8,128)S(1)}) custom-call(f32[768,256]{1,0:T(8,128)S(1)} %get-tuple-element.54.base, bf16[144,256]{1,0:T(8,128)(2,1)S(1)} %bitcast.23, ...), custom_call_target="tpu_custom_call" | custom-call | tf_op jit(solution)/shard_map/pallas_call | solution.py:493
  40.5 0.0 collective-permute-start.6
  40.5 1.8 %collective-permute-start.7 = (f32[8,144]{1,0:T(8,128)S(1)}, f32[8,144]{1,0:T(8,128)S(1)}, u32[]{:S(2)}, u32[]{:S(2)}) collective-permute-start(f32[8,144]{1,0:T(8,128)S(1)} %get-tuple-element.86), channel_id=1, source_target_pairs={{0,32},{32,0},{64,96},{96,64},{1,33},{33,1},{65,97},{97,65},{2,34}... | collective-permute-start | bytes 13832 | tf_op jit(solution)/shard_map/ppermute | solution.py:615
  42.3 1.3 %collective-permute-done.6 = f32[8,144]{1,0:T(8,128)S(1)} collective-permute-done((f32[8,144]{1,0:T(8,128)S(1)}, f32[8,144]{1,0:T(8,128)S(1)}, u32[]{:S(2)}, u32[]{:S(2)}) %collective-permute-start.6) | collective-permute-done | bytes 4640 | tf_op jit(solution)/shard_map/ppermute | solution.py:615
  43.6 0.0 collective-permute-done.7
  43.6 0.1 fusion.7
  43.7 2.0 %collective-permute-start.8 = (f32[3,8,48]{2,1,0:T(8,128)S(1)}, f32[3,8,48]{2,1,0:T(8,128)S(1)}, u32[]{:S(2)}, u32[]{:S(2)}) collective-permute-start(f32[3,8,48]{2,1,0:T(8,128)S(1)} %get-tuple-element.116), channel_id=1, source_target_pairs={{0,24},{8,16},{16,8},{24,0},{1,25},{9,17},{17,9},{25,1},{2,26},{10... | collective-permute-start | bytes 13832 | tf_op jit(solution)/shard_map/ppermute | solution.py:615
  45.7 0.0 collective-permute-start.9
  45.7 2.9 %collective-permute-done.8 = f32[3,8,48]{2,1,0:T(8,128)S(1)} collective-permute-done((f32[3,8,48]{2,1,0:T(8,128)S(1)}, f32[3,8,48]{2,1,0:T(8,128)S(1)}, u32[]{:S(2)}, u32[]{:S(2)}) %collective-permute-start.8) | collective-permute-done | bytes 4640 | tf_op jit(solution)/shard_map/ppermute | solution.py:615
  48.6 0.8 %collective-permute-done.9 = f32[3,8,48]{2,1,0:T(8,128)S(1)} collective-permute-done((f32[3,8,48]{2,1,0:T(8,128)S(1)}, f32[3,8,48]{2,1,0:T(8,128)S(1)}, u32[]{:S(2)}, u32[]{:S(2)}) %collective-permute-start.9) | collective-permute-done | bytes 4640 | tf_op jit(solution)/shard_map/ppermute | solution.py:615
  49.4 0.1 fusion.6
  49.5 5.0 %collective-permute-start.10 = (f32[3,3,8,16]{3,2,1,0:T(8,128)S(1)}, f32[3,3,8,16]{3,2,1,0:T(8,128)S(1)}, u32[]{:S(2)}, u32[]{:S(2)}) collective-permute-start(f32[3,3,8,16]{3,2,1,0:T(8,128)S(1)} %get-tuple-element.93), channel_id=1, source_target_pairs={{0,7},{1,2},{2,1},{3,4},{4,3},{5,6},{6,5},{7,0},{8,15},{9,10},{10,... | collective-permute-start | bytes 13832 | tf_op jit(solution)/shard_map/ppermute | solution.py:615
  54.5 0.0 collective-permute-start.11
  54.5 1.2 %shard_map.190 = (f32[8,32]{1,0:T(8,128)S(1)}, f32[1,32]{1,0:T(1,128)}) custom-call(f32[8,768]{1,0:T(8,128)S(1)} %get-tuple-element.88.grad, s32[768]{0:T(1024)S(1)} %copy-done.7, f32[8,768]{1,0:T(8,128)S(1)} %get-tuple-element.70.rows, f32[1,768]{1,0:T(1,128)S(1)} %get-tuple-element.89.reads), custom_call_target="tpu_custom_call" | custom-call | tf_op jit(solution)/shard_map/pallas_call | solution.py:493
  55.8 1.4 %collective-permute-done.10.r = f32[3,3,8,16]{3,2,1,0:T(8,128)S(1)} collective-permute-done((f32[3,3,8,16]{3,2,1,0:T(8,128)S(1)}, f32[3,3,8,16]{3,2,1,0:T(8,128)S(1)}, u32[]{:S(2)}, u32[]{:S(2)}) %collective-permute-start.10) | collective-permute-done | bytes 4640 | tf_op jit(solution)/shard_map/ppermute | solution.py:615
  57.1 1.3 %collective-permute-done.11.l = f32[3,3,8,16]{3,2,1,0:T(8,128)S(1)} collective-permute-done((f32[3,3,8,16]{3,2,1,0:T(8,128)S(1)}, f32[3,3,8,16]{3,2,1,0:T(8,128)S(1)}, u32[]{:S(2)}, u32[]{:S(2)}) %collective-permute-start.11) | collective-permute-done | bytes 4640 | tf_op jit(solution)/shard_map/ppermute | solution.py:615
  58.5 0.8 %shard_map.191 = f32[3,32]{1,0:T(4,128)} custom-call(f32[8,32]{1,0:T(8,128)S(1)} %get-tuple-element.91.partial, f32[32,432]{1,0:T(8,128)S(1)} %get-tuple-element.92.mt, f32[3,3,8,16]{3,2,1,0:T(8,128)S(1)} %collective-permute-done.10.r, f32[3,3,8,16]{3,2,1,0:T(8,128)S(1)} %get-tuple-element.113.m, f32[3,3,8,16]{3,2,1,0:T(8,128)S(1)} %collective-permute-done.11.l), custom_call_target="tpu_custom_call" | custom-call | tf_op jit(solution)/shard_map/pallas_call | solution.py:493
  (13 shorter events, 0.1 us)
Async XLA Ops:
  0.6 4.7 %copy-start.7 = (s32[768]{0:T(1024)S(1)}, s32[768]{0:T(1024)}, u32[]{:S(2)}) copy-start(s32[768]{0:T(1024)} %slot.5) | copy-start | bytes 9220
  0.6 4.7 %copy-start.8 = (s32[768]{0:T(1024)S(1)}, s32[768]{0:T(1024)}, u32[]{:S(2)}) copy-start(s32[768]{0:T(1024)} %mask.3) | copy-start | bytes 9220
  0.7 10.7 %copy-start.5 = (f32[64,256]{1,0:T(8,128)S(1)}, f32[64,256]{1,0:T(8,128)}, u32[]{:S(2)}) copy-start(f32[64,256]{1,0:T(8,128)} %w_rbf.1) | copy-start | bytes 196612
  0.7 10.7 %copy-start.6 = (bf16[85,256]{1,0:T(8,128)(2,1)S(1)}, bf16[85,256]{1,0:T(8,128)(2,1)}, u32[]{:S(2)}) copy-start(bf16[85,256]{1,0:T(8,128)(2,1)} %table.1) | copy-start | bytes 130564
  0.7 10.7 %copy-start.9 = (f32[3,768]{1,0:T(4,128)S(1)}, f32[3,768]{1,0:T(4,128)}, u32[]{:S(2)}) copy-start(f32[3,768]{1,0:T(4,128)} %disp) | copy-start | bytes 27652
  0.7 10.7 %copy-start.10 = (f32[3,256]{1,0:T(4,128)S(1)}, f32[3,256]{1,0:T(4,128)}, u32[]{:S(2)}) copy-start(f32[3,256]{1,0:T(4,128)} %w_vec.1) | copy-start | bytes 9220
  0.7 11.8 %copy-start.3 = (bf16[2,256,256]{2,1,0:T(8,128)(2,1)S(1)}, bf16[2,256,256]{2,1,0:T(8,128)(2,1)}, u32[]{:S(2)}) copy-start(bf16[2,256,256]{2,1,0:T(8,128)(2,1)} %w_out.5) | copy-start | bytes 786436
  0.7 11.8 %copy-start.4 = (f32[5,256]{1,0:T(8,128)S(1)}, f32[5,256]{1,0:T(8,128)}, u32[]{:S(2)}) copy-start(f32[5,256]{1,0:T(8,128)} %gains.5) | copy-start | bytes 15364
  3.1 4.2 %collective-permute-start = (bf16[144,256]{1,0:T(8,128)(2,1)S(1)}, bf16[144,256]{1,0:T(8,128)(2,1)S(1)}, u32[]{:S(2)}, u32[]{:S(2)}) collective-permute-start(bf16[144,256]{1,0:T(8,128)(2,1)S(1)} %get-tuple-element.49), channel_id=1, source_target_pairs={{0,96},{32,64},{64,32},{96,0},{1,97},{33,65},{65,33},{97,1},{2,98}... | collective-permute-start | bytes 221192 | tf_op jit(solution)/shard_map/ppermute | solution.py:615
  4.6 2.7 %collective-permute-start.1 = (bf16[144,256]{1,0:T(8,128)(2,1)S(1)}, bf16[144,256]{1,0:T(8,128)(2,1)S(1)}, u32[]{:S(2)}, u32[]{:S(2)}) collective-permute-start(bf16[144,256]{1,0:T(8,128)(2,1)S(1)} %get-tuple-element.51), channel_id=1, source_target_pairs={{0,32},{32,0},{64,96},{96,64},{1,33},{33,1},{65,97},{97,65},{2,34}... | collective-permute-start | bytes 221192 | tf_op jit(solution)/shard_map/ppermute | solution.py:615
  5.3 7.2 %copy-start.2 = (bf16[2,512,256]{2,1,0:T(8,128)(2,1)S(1)}, bf16[2,512,256]{2,1,0:T(8,128)(2,1)}, u32[]{:S(2)}) copy-start(bf16[2,512,256]{2,1,0:T(8,128)(2,1)} %w_down.5) | copy-start | bytes 1572868
  5.3 6.1 %copy-start.12 = (s32[32]{0:T(128)S(1)}, s32[32]{0:T(128)}, u32[]{:S(2)}) copy-start(s32[32]{0:T(128)} %species.1) | copy-start | bytes 388
  6.3 6.2 %copy-start = (bf16[2,256,768]{2,1,0:T(8,128)(2,1)S(1)}, bf16[2,256,768]{2,1,0:T(8,128)(2,1)}, u32[]{:S(2)}) copy-start(bf16[2,256,768]{2,1,0:T(8,128)(2,1)} %w_qkv.5) | copy-start | bytes 2359300
  7.3 5.2 %copy-start.1 = (bf16[2,256,512]{2,1,0:T(8,128)(2,1)S(1)}, bf16[2,256,512]{2,1,0:T(8,128)(2,1)}, u32[]{:S(2)}) copy-start(bf16[2,256,512]{2,1,0:T(8,128)(2,1)} %w_up.5) | copy-start | bytes 1572868
  7.3 7.6 %collective-permute-start.3 = (bf16[3,3,16,256]{3,2,1,0:T(8,128)(2,1)S(1)}, bf16[3,3,16,256]{3,2,1,0:T(8,128)(2,1)S(1)}, u32[]{:S(2)}, u32[]{:S(2)}) collective-permute-start(bf16[3,3,16,256]{3,2,1,0:T(8,128)(2,1)S(1)} %get-tuple-element.56), channel_id=1, source_target_pairs={{0,8},{8,0},{16,24},{24,16},{1,9},{9,1},{17,25},{25,17},{2,10},{10... | collective-permute-start | bytes 221192 | tf_op jit(solution)/shard_map/ppermute | solution.py:615
  9.1 5.8 %collective-permute-start.2 = (bf16[3,3,16,256]{3,2,1,0:T(8,128)(2,1)S(1)}, bf16[3,3,16,256]{3,2,1,0:T(8,128)(2,1)S(1)}, u32[]{:S(2)}, u32[]{:S(2)}) collective-permute-start(bf16[3,3,16,256]{3,2,1,0:T(8,128)(2,1)S(1)} %get-tuple-element.55), channel_id=1, source_target_pairs={{0,24},{8,16},{16,8},{24,0},{1,25},{9,17},{17,9},{25,1},{2,26},{10... | collective-permute-start | bytes 221192 | tf_op jit(solution)/shard_map/ppermute | solution.py:615
  15.0 7.2 %copy-start.11 = (f32[256]{0:T(256)S(1)}, f32[256]{0:T(256)}, u32[]{:S(2)}) copy-start(f32[256]{0:T(256)} %param.33) | copy-start | bytes 3076
  15.0 10.1 %collective-permute-start.5 = (bf16[3,3,16,256]{3,2,1,0:T(8,128)(2,1)S(1)}, bf16[3,3,16,256]{3,2,1,0:T(8,128)(2,1)S(1)}, u32[]{:S(2)}, u32[]{:S(2)}) collective-permute-start(bf16[3,3,16,256]{3,2,1,0:T(8,128)(2,1)S(1)} %pad_maximum_fusion.4), channel_id=1, source_target_pairs={{0,1},{1,0},{2,3},{3,2},{4,5},{5,4},{6,7},{7,6},{8,9},{9,8},{10,11... | collective-permute-start | bytes 221192 | tf_op jit(solution)/shard_map/ppermute | solution.py:615
  16.5 8.6 %collective-permute-start.4 = (bf16[3,3,16,256]{3,2,1,0:T(8,128)(2,1)S(1)}, bf16[3,3,16,256]{3,2,1,0:T(8,128)(2,1)S(1)}, u32[]{:S(2)}, u32[]{:S(2)}) collective-permute-start(bf16[3,3,16,256]{3,2,1,0:T(8,128)(2,1)S(1)} %pad_maximum_fusion.3), channel_id=1, source_target_pairs={{0,7},{1,2},{2,1},{3,4},{4,3},{5,6},{6,5},{7,0},{8,15},{9,10},{10,... | collective-permute-start | bytes 221192 | tf_op jit(solution)/shard_map/ppermute | solution.py:615
  40.5 3.1 %collective-permute-start.6 = (f32[8,144]{1,0:T(8,128)S(1)}, f32[8,144]{1,0:T(8,128)S(1)}, u32[]{:S(2)}, u32[]{:S(2)}) collective-permute-start(f32[8,144]{1,0:T(8,128)S(1)} %get-tuple-element.84), channel_id=1, source_target_pairs={{0,96},{32,64},{64,32},{96,0},{1,97},{33,65},{65,33},{97,1},{2,98}... | collective-permute-start | bytes 13832 | tf_op jit(solution)/shard_map/ppermute | solution.py:615
  40.5 3.1 %collective-permute-start.7 = (f32[8,144]{1,0:T(8,128)S(1)}, f32[8,144]{1,0:T(8,128)S(1)}, u32[]{:S(2)}, u32[]{:S(2)}) collective-permute-start(f32[8,144]{1,0:T(8,128)S(1)} %get-tuple-element.86), channel_id=1, source_target_pairs={{0,32},{32,0},{64,96},{96,64},{1,33},{33,1},{65,97},{97,65},{2,34}... | collective-permute-start | bytes 13832 | tf_op jit(solution)/shard_map/ppermute | solution.py:615
  43.7 4.9 %collective-permute-start.8 = (f32[3,8,48]{2,1,0:T(8,128)S(1)}, f32[3,8,48]{2,1,0:T(8,128)S(1)}, u32[]{:S(2)}, u32[]{:S(2)}) collective-permute-start(f32[3,8,48]{2,1,0:T(8,128)S(1)} %get-tuple-element.116), channel_id=1, source_target_pairs={{0,24},{8,16},{16,8},{24,0},{1,25},{9,17},{17,9},{25,1},{2,26},{10... | collective-permute-start | bytes 13832 | tf_op jit(solution)/shard_map/ppermute | solution.py:615
  45.7 3.7 %collective-permute-start.9 = (f32[3,8,48]{2,1,0:T(8,128)S(1)}, f32[3,8,48]{2,1,0:T(8,128)S(1)}, u32[]{:S(2)}, u32[]{:S(2)}) collective-permute-start(f32[3,8,48]{2,1,0:T(8,128)S(1)} %get-tuple-element.117), channel_id=1, source_target_pairs={{0,8},{8,0},{16,24},{24,16},{1,9},{9,1},{17,25},{25,17},{2,10},{10... | collective-permute-start | bytes 13832 | tf_op jit(solution)/shard_map/ppermute | solution.py:615
  49.5 7.7 %collective-permute-start.10 = (f32[3,3,8,16]{3,2,1,0:T(8,128)S(1)}, f32[3,3,8,16]{3,2,1,0:T(8,128)S(1)}, u32[]{:S(2)}, u32[]{:S(2)}) collective-permute-start(f32[3,3,8,16]{3,2,1,0:T(8,128)S(1)} %get-tuple-element.93), channel_id=1, source_target_pairs={{0,7},{1,2},{2,1},{3,4},{4,3},{5,6},{6,5},{7,0},{8,15},{9,10},{10,... | collective-permute-start | bytes 13832 | tf_op jit(solution)/shard_map/ppermute | solution.py:615
  54.5 4.0 %collective-permute-start.11 = (f32[3,3,8,16]{3,2,1,0:T(8,128)S(1)}, f32[3,3,8,16]{3,2,1,0:T(8,128)S(1)}, u32[]{:S(2)}, u32[]{:S(2)}) collective-permute-start(f32[3,3,8,16]{3,2,1,0:T(8,128)S(1)} %get-tuple-element.94), channel_id=1, source_target_pairs={{0,1},{1,0},{2,3},{3,2},{4,5},{5,4},{6,7},{7,6},{8,9},{9,8},{10,11... | collective-permute-start | bytes 13832 | tf_op jit(solution)/shard_map/ppermute | solution.py:615

commit v7 on v6

--- a/solution.py
+++ b/solution.py
@@ -408,7 +408,7 @@
     acc,
 ):
     blocks = block_list(OUTER, 3)
-    arrived = jnp.concatenate([arr_r[...], arr_m[...], arr_l[...]], axis=0)
+    arrived = jnp.concatenate([arr_l[...], arr_m[...], arr_r[...]], axis=0)
     x = []
     for b in blocks:
         here = shifted(b, INNER)
@@ -652,7 +652,7 @@
     low, high, *saved = lax.optimization_barrier((low, high, *saved))
     low, high = exchange(low, high, "gz")
     terms, dx, acc = inner_backward(saved, kwb, gains, w_energy, weights)
-    arr = [v.reshape(SIDE, D) for v in (low, mid, high)]
+    arr = [v.reshape(SIDE, D) for v in (high, mid, low)]
     tokens, reads, grad, low, mid, high = layers(
         base,
         arr,

time: 59.4 us -> 58.6 us (0.987)
  starting transfers between devices: 22.3 us -> 19.6 us
  waiting for transfers between devices: 8.67 us -> 10.6 us
    ppermute x12, starting transfers between devices: 22.3 us -> 19.6 us  [exchange(): return (lax.ppermute(low, axis, outer), lax.ppermute(high, axis, inner))]
    ppermute x12, waiting for transfers between devices: 8.67 us -> 10.6 us  [exchange(): return (lax.ppermute(low, axis, outer), lax.ppermute(high, axis, inner))]
  transfers between devices with their start and end apart: 12 -> 12, of which waited for: 6 -> 6; matrix products, arithmetic and copies ran while one was open for 0% -> 0% of each run, Pallas kernels for 14% -> 15%
where the time goes in v7:
time: 58.6 us; the launch traced here: 58.5 us
  Pallas kernels  27.1 us (46%)
  starting transfers between devices  19.6 us (33%)
  waiting for transfers between devices  10.6 us (18%)
  between operations  0.96 us (2%)
    pallas_call x8, Pallas kernels, vmem_call(): pl.pallas_call(kernel, out_shape=outs, in_specs=[pl.BlockSpec(memory_spac...  27.1 us
    ppermute x12, starting transfers between devices, exchange(): return (lax.ppermute(low, axis, outer), lax.ppermute(high, axis, inner))  19.6 us
    ppermute x12, waiting for transfers between devices, exchange(): return (lax.ppermute(low, axis, outer), lax.ppermute(high, axis, inner))  10.6 us
  transfers between devices with their start and end apart: 12, of which 6 were waited for; matrix products, arithmetic and copies ran while one was open for 0% of the time, Pallas kernels for 15%

profile of v7, /device:TPU:0, one launch (start us, length us, event | category | flops | bytes accessed | tf_op | source)
XLA Modules:
  0.0 58.5 jit_solution(5906598736293791822)
XLA Ops:
  0.6 0.0 copy-start.7
  0.6 0.0 copy-start.8
  0.7 0.0 copy-start.5
  0.7 0.0 copy-start.6
  0.7 0.0 copy-start.9
  0.7 0.0 copy-start.10
  0.7 0.0 copy-start.3
  0.7 0.0 copy-start.4
  0.7 2.4 %shard_map.184 = (bf16[768,256]{1,0:T(8,128)(2,1)S(1)}, bf16[144,256]{1,0:T(8,128)(2,1)S(1)}, bf16[144,256]{1,0:T(8,128)(2,1)S(1)}, bf16[144,256]{1,0:T(8,128)(2,1)S(1)}, f32[432,8]{1,0:T(8,128)S(1)}) custom-call(bf16[32,256]{1,0:T(8,128)(2,1)} %state_far.1, bf16[256,256]{1,0:T(8,128)(2,1)} %w_far.1, bf16[768,256]{1,0:T(8,128)(2,1)} %prev_far.1, s32[416]{0:T(512)} %send_far.1), custom_call_target="tpu_custom_call" | custom-call | tf_op jit(solution)/shard_map/pallas_call | solution.py:493
  3.1 1.5 %collective-permute-start = (bf16[144,256]{1,0:T(8,128)(2,1)S(1)}, bf16[144,256]{1,0:T(8,128)(2,1)S(1)}, u32[]{:S(2)}, u32[]{:S(2)}) collective-permute-start(bf16[144,256]{1,0:T(8,128)(2,1)S(1)} %get-tuple-element.49), channel_id=1, source_target_pairs={{0,96},{32,64},{64,32},{96,0},{1,97},{33,65},{65,33},{97,1},{2,98}... | collective-permute-start | bytes 221192 | tf_op jit(solution)/shard_map/ppermute | solution.py:615
  4.6 0.7 %collective-permute-start.1 = (bf16[144,256]{1,0:T(8,128)(2,1)S(1)}, bf16[144,256]{1,0:T(8,128)(2,1)S(1)}, u32[]{:S(2)}, u32[]{:S(2)}) collective-permute-start(bf16[144,256]{1,0:T(8,128)(2,1)S(1)} %get-tuple-element.51), channel_id=1, source_target_pairs={{0,32},{32,0},{64,96},{96,64},{1,33},{33,1},{65,97},{97,65},{2,34}... | collective-permute-start | bytes 221192 | tf_op jit(solution)/shard_map/ppermute | solution.py:615
  5.3 0.0 copy-start.2
  5.3 0.0 copy-done.7
  5.3 0.0 copy-done.8
  5.3 0.0 copy-start.12
  5.3 1.0 %shard_map.187 = (bf16[768,432]{1,0:T(8,128)(2,1)S(1)}, bf16[432,768]{1,0:T(8,128)(2,1)S(1)}, f32[32,432]{1,0:T(8,128)S(1)}) custom-call(s32[768]{0:T(1024)S(1)} %copy-done.7, s32[768]{0:T(1024)S(1)} %copy-done.8, f32[432,8]{1,0:T(8,128)S(1)} %get-tuple-element.67.where), custom_call_target="tpu_custom_call" | custom-call | tf_op jit(solution)/shard_map/pallas_call | solution.py:493
  6.3 0.0 copy-start
  6.3 1.0 %collective-permute-done = bf16[144,256]{1,0:T(8,128)(2,1)S(1)} collective-permute-done((bf16[144,256]{1,0:T(8,128)(2,1)S(1)}, bf16[144,256]{1,0:T(8,128)(2,1)S(1)}, u32[]{:S(2)}, u32[]{:S(2)}) %collective-permute-start) | collective-permute-done | bytes 73760 | tf_op jit(solution)/shard_map/ppermute | solution.py:615
  7.3 0.0 collective-permute-done.1
  7.3 0.0 copy-start.1
  7.3 1.8 %collective-permute-start.3 = (bf16[3,3,16,256]{3,2,1,0:T(8,128)(2,1)S(1)}, bf16[3,3,16,256]{3,2,1,0:T(8,128)(2,1)S(1)}, u32[]{:S(2)}, u32[]{:S(2)}) collective-permute-start(bf16[3,3,16,256]{3,2,1,0:T(8,128)(2,1)S(1)} %get-tuple-element.56), channel_id=1, source_target_pairs={{0,8},{8,0},{16,24},{24,16},{1,9},{9,1},{17,25},{25,17},{2,10},{10... | collective-permute-start | bytes 221192 | tf_op jit(solution)/shard_map/ppermute | solution.py:615
  9.1 2.2 %collective-permute-start.2 = (bf16[3,3,16,256]{3,2,1,0:T(8,128)(2,1)S(1)}, bf16[3,3,16,256]{3,2,1,0:T(8,128)(2,1)S(1)}, u32[]{:S(2)}, u32[]{:S(2)}) collective-permute-start(bf16[3,3,16,256]{3,2,1,0:T(8,128)(2,1)S(1)} %get-tuple-element.55), channel_id=1, source_target_pairs={{0,24},{8,16},{16,8},{24,0},{1,25},{9,17},{17,9},{25,1},{2,26},{10... | collective-permute-start | bytes 221192 | tf_op jit(solution)/shard_map/ppermute | solution.py:615
  11.4 0.0 copy-done.5
  11.4 0.0 copy-done.6
  11.4 0.0 copy-done.9
  11.4 0.0 copy-done.10
  11.4 0.0 copy-done.12
  11.4 1.0 %shard_map.185 = (f32[768,256]{1,0:T(8,128)S(1)}, f32[768,128]{1,0:T(8,128)S(1)}, f32[72,768]{1,0:T(8,128)S(1)}, f32[8,768]{1,0:T(8,128)S(1)}, f32[72,256]{1,0:T(8,128)S(1)}) custom-call(f32[3,768]{1,0:T(4,128)S(1)} %copy-done.9, s32[768]{0:T(1024)S(1)} %copy-done.8, s32[768]{0:T(1024)S(1)} %copy-done.7, s32[32]{0:T(128)S(1)} %copy-done.12, ...), custom_call_target="tpu_custom_call" | custom-call | tf_op jit(solution)/shard_map/pallas_call | solution.py:493
  12.5 0.0 copy-done.3
  12.5 0.0 copy-done.4
  12.5 0.0 copy-done.2
  12.5 0.0 copy-done
  12.5 0.0 copy-done.1
  12.5 2.4 %shard_map.186 = (f32[96,256]{1,0:T(8,128)S(1)}, f32[4,96,256]{2,1,0:T(8,128)S(1)}, f32[4,96,128]{2,1,0:T(8,128)S(1)}, f32[2,96,768]{2,1,0:T(8,128)S(1)}, f32[2,...) custom-call(f32[768,256]{1,0:T(8,128)S(1)} %get-tuple-element.54.base, ...), custom_call_target="tpu_custom_call" | custom-call | tf_op jit(solution)/shard_map/pallas_call | solution.py:493
  14.9 0.0 collective-permute-done.3
  14.9 0.0 collective-permute-done.2
  15.0 0.0 copy-start.11
  15.0 6.3 %collective-permute-start.5 = (bf16[3,3,16,256]{3,2,1,0:T(8,128)(2,1)S(1)}, bf16[3,3,16,256]{3,2,1,0:T(8,128)(2,1)S(1)}, u32[]{:S(2)}, u32[]{:S(2)}) collective-permute-start(bf16[3,3,16,256]{3,2,1,0:T(8,128)(2,1)S(1)} %pad_maximum_fusion.3), channel_id=1, source_target_pairs={{0,7},{1,2},{2,1},{3,4},{4,3},{5,6},{6,5},{7,0},{8,15},{9,10},{10,... | collective-permute-start | bytes 221192 | tf_op jit(solution)/shard_map/ppermute | solution.py:615
  21.3 0.0 collective-permute-start.4
  21.3 0.0 copy-done.11
  21.3 2.9 %shard_map.188 = (f32[96,128]{1,0:T(8,128)S(1)}, f32[96,256]{1,0:T(8,128)S(1)}, f32[96,128]{1,0:T(8,128)S(1)}) custom-call(f32[96,256]{1,0:T(8,128)S(1)} %get-tuple-element.73.last.inner_last, f32[4,96,256]{2,1,0:T(8,128)S(1)} %get-tuple-element.74.xs, f32[4,96,128]{2,1,0:T(8,128)S(1)} %get-tuple-element.75.rs, f32[2,96,768]{2,1,0:T(8,128)S(1)} %get-tuple-element.76.qkv, ...), custom_call_target="tpu_custom_call" | custom-call | tf_op jit(solution)/shard_map/pallas_call | solution.py:493
  24.3 0.0 collective-permute-done.5
  24.3 1.4 %collective-permute-done.4 = bf16[3,3,16,256]{3,2,1,0:T(8,128)(2,1)S(1)} collective-permute-done((bf16[3,3,16,256]{3,2,1,0:T(8,128)(2,1)S(1)}, bf16[3,3,16,256]{3,2,1,0:T(8,128)(2,1)S(1)}, u32[]{:S(2)}, u32[]{:S(2)}) %collective-permute-start.4) | collective-permute-done | bytes 73760 | tf_op jit(solution)/shard_map/ppermute | solution.py:615
  25.7 15.4 %shard_map.189 = (bf16[768,256]{1,0:T(8,128)(2,1)}, f32[1,768]{1,0:T(1,128)S(1)}, f32[8,768]{1,0:T(8,128)S(1)}, f32[8,144]{1,0:T(8,128)S(1)}, f32[8,144]{1,0:T(8,128)S(1)}, /*index=5*/f32[8,144]{1,0:T(8,128)S(1)}) custom-call(f32[768,256]{1,0:T(8,128)S(1)} %get-tuple-element.54.base, bf16[144,256]{1,0:T(8,128)(2,1)S(1)} %bitcast.23, ...), custom_call_target="tpu_custom_call" | custom-call | tf_op jit(solution)/shard_map/pallas_call | solution.py:493
  41.1 0.0 collective-permute-start.6
  41.1 1.3 %collective-permute-start.7 = (f32[8,144]{1,0:T(8,128)S(1)}, f32[8,144]{1,0:T(8,128)S(1)}, u32[]{:S(2)}, u32[]{:S(2)}) collective-permute-start(f32[8,144]{1,0:T(8,128)S(1)} %get-tuple-element.86), channel_id=1, source_target_pairs={{0,32},{32,0},{64,96},{96,64},{1,33},{33,1},{65,97},{97,65},{2,34}... | collective-permute-start | bytes 13832 | tf_op jit(solution)/shard_map/ppermute | solution.py:615
  42.4 1.8 %collective-permute-done.6 = f32[8,144]{1,0:T(8,128)S(1)} collective-permute-done((f32[8,144]{1,0:T(8,128)S(1)}, f32[8,144]{1,0:T(8,128)S(1)}, u32[]{:S(2)}, u32[]{:S(2)}) %collective-permute-start.6) | collective-permute-done | bytes 4640 | tf_op jit(solution)/shard_map/ppermute | solution.py:615
  44.2 0.0 collective-permute-done.7
  44.2 0.1 fusion.7
  44.3 2.0 %collective-permute-start.8 = (f32[3,8,48]{2,1,0:T(8,128)S(1)}, f32[3,8,48]{2,1,0:T(8,128)S(1)}, u32[]{:S(2)}, u32[]{:S(2)}) collective-permute-start(f32[3,8,48]{2,1,0:T(8,128)S(1)} %get-tuple-element.116), channel_id=1, source_target_pairs={{0,24},{8,16},{16,8},{24,0},{1,25},{9,17},{17,9},{25,1},{2,26},{10... | collective-permute-start | bytes 13832 | tf_op jit(solution)/shard_map/ppermute | solution.py:615
  46.2 0.0 collective-permute-start.9
  46.2 2.9 %collective-permute-done.8 = f32[3,8,48]{2,1,0:T(8,128)S(1)} collective-permute-done((f32[3,8,48]{2,1,0:T(8,128)S(1)}, f32[3,8,48]{2,1,0:T(8,128)S(1)}, u32[]{:S(2)}, u32[]{:S(2)}) %collective-permute-start.8) | collective-permute-done | bytes 4640 | tf_op jit(solution)/shard_map/ppermute | solution.py:615
  49.2 0.7 %collective-permute-done.9 = f32[3,8,48]{2,1,0:T(8,128)S(1)} collective-permute-done((f32[3,8,48]{2,1,0:T(8,128)S(1)}, f32[3,8,48]{2,1,0:T(8,128)S(1)}, u32[]{:S(2)}, u32[]{:S(2)}) %collective-permute-start.9) | collective-permute-done | bytes 4640 | tf_op jit(solution)/shard_map/ppermute | solution.py:615
  49.9 0.1 fusion.6
  50.0 3.7 %collective-permute-start.10 = (f32[3,3,8,16]{3,2,1,0:T(8,128)S(1)}, f32[3,3,8,16]{3,2,1,0:T(8,128)S(1)}, u32[]{:S(2)}, u32[]{:S(2)}) collective-permute-start(f32[3,3,8,16]{3,2,1,0:T(8,128)S(1)} %get-tuple-element.93), channel_id=1, source_target_pairs={{0,7},{1,2},{2,1},{3,4},{4,3},{5,6},{6,5},{7,0},{8,15},{9,10},{10,... | collective-permute-start | bytes 13832 | tf_op jit(solution)/shard_map/ppermute | solution.py:615
  53.7 0.0 collective-permute-start.11
  53.7 1.2 %shard_map.190 = (f32[8,32]{1,0:T(8,128)S(1)}, f32[1,32]{1,0:T(1,128)}) custom-call(f32[8,768]{1,0:T(8,128)S(1)} %get-tuple-element.88.grad, s32[768]{0:T(1024)S(1)} %copy-done.7, f32[8,768]{1,0:T(8,128)S(1)} %get-tuple-element.70.rows, f32[1,768]{1,0:T(1,128)S(1)} %get-tuple-element.89.reads), custom_call_target="tpu_custom_call" | custom-call | tf_op jit(solution)/shard_map/pallas_call | solution.py:493
  55.0 2.7 %collective-permute-done.10.r = f32[3,3,8,16]{3,2,1,0:T(8,128)S(1)} collective-permute-done((f32[3,3,8,16]{3,2,1,0:T(8,128)S(1)}, f32[3,3,8,16]{3,2,1,0:T(8,128)S(1)}, u32[]{:S(2)}, u32[]{:S(2)}) %collective-permute-start.10) | collective-permute-done | bytes 4640 | tf_op jit(solution)/shard_map/ppermute | solution.py:615
  57.7 0.0 collective-permute-done.11.l
  57.7 0.8 %shard_map.191 = f32[3,32]{1,0:T(4,128)} custom-call(f32[8,32]{1,0:T(8,128)S(1)} %get-tuple-element.91.partial, f32[32,432]{1,0:T(8,128)S(1)} %get-tuple-element.92.mt, f32[3,3,8,16]{3,2,1,0:T(8,128)S(1)} %collective-permute-done.10.r, f32[3,3,8,16]{3,2,1,0:T(8,128)S(1)} %get-tuple-element.113.m, f32[3,3,8,16]{3,2,1,0:T(8,128)S(1)} %collective-permute-done.11.l), custom_call_target="tpu_custom_call" | custom-call | tf_op jit(solution)/shard_map/pallas_call | solution.py:493
  (13 shorter events, 0.1 us)
Async XLA Ops:
  0.6 4.7 %copy-start.7 = (s32[768]{0:T(1024)S(1)}, s32[768]{0:T(1024)}, u32[]{:S(2)}) copy-start(s32[768]{0:T(1024)} %slot.5) | copy-start | bytes 9220
  0.6 4.7 %copy-start.8 = (s32[768]{0:T(1024)S(1)}, s32[768]{0:T(1024)}, u32[]{:S(2)}) copy-start(s32[768]{0:T(1024)} %mask.3) | copy-start | bytes 9220
  0.7 10.7 %copy-start.5 = (f32[64,256]{1,0:T(8,128)S(1)}, f32[64,256]{1,0:T(8,128)}, u32[]{:S(2)}) copy-start(f32[64,256]{1,0:T(8,128)} %w_rbf.1) | copy-start | bytes 196612
  0.7 10.7 %copy-start.6 = (bf16[85,256]{1,0:T(8,128)(2,1)S(1)}, bf16[85,256]{1,0:T(8,128)(2,1)}, u32[]{:S(2)}) copy-start(bf16[85,256]{1,0:T(8,128)(2,1)} %table.1) | copy-start | bytes 130564
  0.7 10.7 %copy-start.9 = (f32[3,768]{1,0:T(4,128)S(1)}, f32[3,768]{1,0:T(4,128)}, u32[]{:S(2)}) copy-start(f32[3,768]{1,0:T(4,128)} %disp) | copy-start | bytes 27652
  0.7 10.7 %copy-start.10 = (f32[3,256]{1,0:T(4,128)S(1)}, f32[3,256]{1,0:T(4,128)}, u32[]{:S(2)}) copy-start(f32[3,256]{1,0:T(4,128)} %w_vec.1) | copy-start | bytes 9220
  0.7 11.8 %copy-start.3 = (bf16[2,256,256]{2,1,0:T(8,128)(2,1)S(1)}, bf16[2,256,256]{2,1,0:T(8,128)(2,1)}, u32[]{:S(2)}) copy-start(bf16[2,256,256]{2,1,0:T(8,128)(2,1)} %w_out.5) | copy-start | bytes 786436
  0.7 11.8 %copy-start.4 = (f32[5,256]{1,0:T(8,128)S(1)}, f32[5,256]{1,0:T(8,128)}, u32[]{:S(2)}) copy-start(f32[5,256]{1,0:T(8,128)} %gains.5) | copy-start | bytes 15364
  3.1 4.2 %collective-permute-start = (bf16[144,256]{1,0:T(8,128)(2,1)S(1)}, bf16[144,256]{1,0:T(8,128)(2,1)S(1)}, u32[]{:S(2)}, u32[]{:S(2)}) collective-permute-start(bf16[144,256]{1,0:T(8,128)(2,1)S(1)} %get-tuple-element.49), channel_id=1, source_target_pairs={{0,96},{32,64},{64,32},{96,0},{1,97},{33,65},{65,33},{97,1},{2,98}... | collective-permute-start | bytes 221192 | tf_op jit(solution)/shard_map/ppermute | solution.py:615
  4.6 2.7 %collective-permute-start.1 = (bf16[144,256]{1,0:T(8,128)(2,1)S(1)}, bf16[144,256]{1,0:T(8,128)(2,1)S(1)}, u32[]{:S(2)}, u32[]{:S(2)}) collective-permute-start(bf16[144,256]{1,0:T(8,128)(2,1)S(1)} %get-tuple-element.51), channel_id=1, source_target_pairs={{0,32},{32,0},{64,96},{96,64},{1,33},{33,1},{65,97},{97,65},{2,34}... | collective-permute-start | bytes 221192 | tf_op jit(solution)/shard_map/ppermute | solution.py:615
  5.3 7.2 %copy-start.2 = (bf16[2,512,256]{2,1,0:T(8,128)(2,1)S(1)}, bf16[2,512,256]{2,1,0:T(8,128)(2,1)}, u32[]{:S(2)}) copy-start(bf16[2,512,256]{2,1,0:T(8,128)(2,1)} %w_down.5) | copy-start | bytes 1572868
  5.3 6.1 %copy-start.12 = (s32[32]{0:T(128)S(1)}, s32[32]{0:T(128)}, u32[]{:S(2)}) copy-start(s32[32]{0:T(128)} %species.1) | copy-start | bytes 388
  6.3 6.2 %copy-start = (bf16[2,256,768]{2,1,0:T(8,128)(2,1)S(1)}, bf16[2,256,768]{2,1,0:T(8,128)(2,1)}, u32[]{:S(2)}) copy-start(bf16[2,256,768]{2,1,0:T(8,128)(2,1)} %w_qkv.5) | copy-start | bytes 2359300
  7.3 5.2 %copy-start.1 = (bf16[2,256,512]{2,1,0:T(8,128)(2,1)S(1)}, bf16[2,256,512]{2,1,0:T(8,128)(2,1)}, u32[]{:S(2)}) copy-start(bf16[2,256,512]{2,1,0:T(8,128)(2,1)} %w_up.5) | copy-start | bytes 1572868
  7.3 7.6 %collective-permute-start.3 = (bf16[3,3,16,256]{3,2,1,0:T(8,128)(2,1)S(1)}, bf16[3,3,16,256]{3,2,1,0:T(8,128)(2,1)S(1)}, u32[]{:S(2)}, u32[]{:S(2)}) collective-permute-start(bf16[3,3,16,256]{3,2,1,0:T(8,128)(2,1)S(1)} %get-tuple-element.56), channel_id=1, source_target_pairs={{0,8},{8,0},{16,24},{24,16},{1,9},{9,1},{17,25},{25,17},{2,10},{10... | collective-permute-start | bytes 221192 | tf_op jit(solution)/shard_map/ppermute | solution.py:615
  9.1 5.8 %collective-permute-start.2 = (bf16[3,3,16,256]{3,2,1,0:T(8,128)(2,1)S(1)}, bf16[3,3,16,256]{3,2,1,0:T(8,128)(2,1)S(1)}, u32[]{:S(2)}, u32[]{:S(2)}) collective-permute-start(bf16[3,3,16,256]{3,2,1,0:T(8,128)(2,1)S(1)} %get-tuple-element.55), channel_id=1, source_target_pairs={{0,24},{8,16},{16,8},{24,0},{1,25},{9,17},{17,9},{25,1},{2,26},{10... | collective-permute-start | bytes 221192 | tf_op jit(solution)/shard_map/ppermute | solution.py:615
  15.0 6.4 %copy-start.11 = (f32[256]{0:T(256)S(1)}, f32[256]{0:T(256)}, u32[]{:S(2)}) copy-start(f32[256]{0:T(256)} %param.33) | copy-start | bytes 3076
  15.0 9.3 %collective-permute-start.5 = (bf16[3,3,16,256]{3,2,1,0:T(8,128)(2,1)S(1)}, bf16[3,3,16,256]{3,2,1,0:T(8,128)(2,1)S(1)}, u32[]{:S(2)}, u32[]{:S(2)}) collective-permute-start(bf16[3,3,16,256]{3,2,1,0:T(8,128)(2,1)S(1)} %pad_maximum_fusion.3), channel_id=1, source_target_pairs={{0,7},{1,2},{2,1},{3,4},{4,3},{5,6},{6,5},{7,0},{8,15},{9,10},{10,... | collective-permute-start | bytes 221192 | tf_op jit(solution)/shard_map/ppermute | solution.py:615
  21.3 4.4 %collective-permute-start.4 = (bf16[3,3,16,256]{3,2,1,0:T(8,128)(2,1)S(1)}, bf16[3,3,16,256]{3,2,1,0:T(8,128)(2,1)S(1)}, u32[]{:S(2)}, u32[]{:S(2)}) collective-permute-start(bf16[3,3,16,256]{3,2,1,0:T(8,128)(2,1)S(1)} %pad_maximum_fusion.4), channel_id=1, source_target_pairs={{0,1},{1,0},{2,3},{3,2},{4,5},{5,4},{6,7},{7,6},{8,9},{9,8},{10,11... | collective-permute-start | bytes 221192 | tf_op jit(solution)/shard_map/ppermute | solution.py:615
  41.1 3.1 %collective-permute-start.6 = (f32[8,144]{1,0:T(8,128)S(1)}, f32[8,144]{1,0:T(8,128)S(1)}, u32[]{:S(2)}, u32[]{:S(2)}) collective-permute-start(f32[8,144]{1,0:T(8,128)S(1)} %get-tuple-element.84), channel_id=1, source_target_pairs={{0,96},{32,64},{64,32},{96,0},{1,97},{33,65},{65,33},{97,1},{2,98}... | collective-permute-start | bytes 13832 | tf_op jit(solution)/shard_map/ppermute | solution.py:615
  41.1 3.1 %collective-permute-start.7 = (f32[8,144]{1,0:T(8,128)S(1)}, f32[8,144]{1,0:T(8,128)S(1)}, u32[]{:S(2)}, u32[]{:S(2)}) collective-permute-start(f32[8,144]{1,0:T(8,128)S(1)} %get-tuple-element.86), channel_id=1, source_target_pairs={{0,32},{32,0},{64,96},{96,64},{1,33},{33,1},{65,97},{97,65},{2,34}... | collective-permute-start | bytes 13832 | tf_op jit(solution)/shard_map/ppermute | solution.py:615
  44.3 4.9 %collective-permute-start.8 = (f32[3,8,48]{2,1,0:T(8,128)S(1)}, f32[3,8,48]{2,1,0:T(8,128)S(1)}, u32[]{:S(2)}, u32[]{:S(2)}) collective-permute-start(f32[3,8,48]{2,1,0:T(8,128)S(1)} %get-tuple-element.116), channel_id=1, source_target_pairs={{0,24},{8,16},{16,8},{24,0},{1,25},{9,17},{17,9},{25,1},{2,26},{10... | collective-permute-start | bytes 13832 | tf_op jit(solution)/shard_map/ppermute | solution.py:615
  46.2 3.7 %collective-permute-start.9 = (f32[3,8,48]{2,1,0:T(8,128)S(1)}, f32[3,8,48]{2,1,0:T(8,128)S(1)}, u32[]{:S(2)}, u32[]{:S(2)}) collective-permute-start(f32[3,8,48]{2,1,0:T(8,128)S(1)} %get-tuple-element.117), channel_id=1, source_target_pairs={{0,8},{8,0},{16,24},{24,16},{1,9},{9,1},{17,25},{25,17},{2,10},{10... | collective-permute-start | bytes 13832 | tf_op jit(solution)/shard_map/ppermute | solution.py:615
  50.0 7.7 %collective-permute-start.10 = (f32[3,3,8,16]{3,2,1,0:T(8,128)S(1)}, f32[3,3,8,16]{3,2,1,0:T(8,128)S(1)}, u32[]{:S(2)}, u32[]{:S(2)}) collective-permute-start(f32[3,3,8,16]{3,2,1,0:T(8,128)S(1)} %get-tuple-element.93), channel_id=1, source_target_pairs={{0,7},{1,2},{2,1},{3,4},{4,3},{5,6},{6,5},{7,0},{8,15},{9,10},{10,... | collective-permute-start | bytes 13832 | tf_op jit(solution)/shard_map/ppermute | solution.py:615
  53.7 4.0 %collective-permute-start.11 = (f32[3,3,8,16]{3,2,1,0:T(8,128)S(1)}, f32[3,3,8,16]{3,2,1,0:T(8,128)S(1)}, u32[]{:S(2)}, u32[]{:S(2)}) collective-permute-start(f32[3,3,8,16]{3,2,1,0:T(8,128)S(1)} %get-tuple-element.94), channel_id=1, source_target_pairs={{0,1},{1,0},{2,3},{3,2},{4,5},{5,4},{6,7},{7,6},{8,9},{9,8},{10,11... | collective-permute-start | bytes 13832 | tf_op jit(solution)/shard_map/ppermute | solution.py:615
